TPU v7x, 128 devices: a whole 4x4x4 slice. The times are simulated.
128 devices in a mesh: lat: 16 (over y, x_lo, core), ens: 8 (over z, x_hi).
Axes of the slice: x: 4 (x_hi: 2, x_lo: 2; x = x_hi * 2 + x_lo), y: 4, z: 4, core: 2. Of those that a mesh axis runs over, the one named last changes fastest.
Arguments:
- passed_on: float32 [8, 192, 16, 384], P('ens', None, None, 'lat'), may hold values from -6 to 6
- passed_grad: float32 [8, 192, 16, 384], P('ens', None, None, 'lat'), may hold values from -6 to 6
- latent: float32 [8, 192, 16, 384], P('ens', None, 'lat'), may hold values from -6 to 6
- mix_factors: float32 [2, 96, 96], replicated, may hold values from -0.25 to 0.25
- in_kernel: bfloat16 [2, 9, 48, 512], replicated, may hold values from -0.3125 to 0.3125
- in_bias: float32 [2, 512], replicated, may hold values from -3 to 3
- out_kernel: bfloat16 [2, 9, 96, 512], replicated, may hold values from -0.09375 to 0.09375
- out_bias: float32 [2, 96], replicated, may hold values from -3 to 3
Outputs:
- rebuilt: float32 [8, 96, 32, 768], P('ens', None, 'lat')
- input_grad: float32 [8, 96, 32, 768], P('ens', None, 'lat')
- mix_grad: float32 [2, 96, 96], replicated
- in_kernel_grad: float32 [2, 9, 48, 512], replicated
- in_bias_grad: float32 [2, 512], replicated
- out_kernel_grad: float32 [2, 9, 96, 512], replicated
- out_bias_grad: float32 [2, 96], replicated
All inputs are finite; a program needn't handle non-finite values.
Results may differ from a plain program's by a relative error of at most 0.0028.
Values may be sent and summed in bfloat16 or wider, within the bound.
No kernel may reach another device: no remote copies, remote signals or barrier semaphores. Data moves between devices by JAX's collectives and lax.ppermute only.
A program may use at most 192 MiB of HBM per device.

v0:
```python
import functools

import jax
import jax.numpy as jnp
from jax import lax
from jax.experimental import pallas as pl
from jax.experimental.pallas import tpu as pltpu
from jax.sharding import Mesh, PartitionSpec as P

BF = jnp.bfloat16
F32 = jnp.float32
HIGH = lax.Precision.HIGHEST
LAT = ("y", "xl", "c")
ENS = ("z", "xh")
CHIPS = ("y", "xl", "z", "xh")
HALF = 48
CH = 96
HID = 512
COLS = 384
ROW = 768
CELLS = 1536
IN_ROWS = 448
IN_HALF = 224
TAP_HALF = 144
MIB = 1024 * 1024


def mm(a, b):
    return lax.dot_general(a, b, (((1,), (0,)), ((), ())), preferred_element_type=F32)


def mm_nt(a, b):
    return lax.dot_general(a, b, (((1,), (1,)), ((), ())), preferred_element_type=F32)


def mm_high(a, b):
    return lax.dot_general(
        a, b, (((1,), (0,)), ((), ())), preferred_element_type=F32, precision=HIGH
    )


def split3(x):
    hi = x.astype(BF)
    rest = x - hi.astype(F32)
    mid = rest.astype(BF)
    low = (rest - mid.astype(F32)).astype(BF)
    return hi, mid, low


def from_left(x):
    lane = lax.broadcasted_iota(jnp.int32, x.shape, 1)
    return jnp.where(lane == 0, 0.0, pltpu.roll(x, 1, 1))


def from_right(x):
    width = x.shape[1]
    lane = lax.broadcasted_iota(jnp.int32, x.shape, 1)
    return jnp.where(lane == width - 1, 0.0, pltpu.roll(x, width - 1, 1))


def sds(shape, dtype):
    return jax.ShapeDtypeStruct(shape, dtype)


def call(body, outs, ins, scratch=(), smem=(), hbm=(), flops=0, name=None, limit=16):
    moved = sum(x.size * x.dtype.itemsize for x in list(ins) + list(outs))
    return pl.pallas_call(
        body,
        out_shape=outs,
        in_specs=[
            pl.BlockSpec(
                memory_space=pltpu.SMEM if i in smem else pltpu.HBM if i in hbm else pltpu.VMEM
            )
            for i in range(len(ins))
        ],
        out_specs=[pl.BlockSpec(memory_space=pltpu.VMEM) for _ in outs],
        scratch_shapes=list(scratch),
        compiler_params=pltpu.CompilerParams(vmem_limit_bytes=limit * MIB),
        cost_estimate=pl.CostEstimate(flops=flops, bytes_accessed=moved, transcendentals=0),
        name=name,
    )(*ins)


def payload_kernel(on_ref, grad_ref, out_ref):
    bands, width = on_ref.shape[2], 2 * CH
    blank = jnp.zeros(on_ref.shape[1:], BF)
    for s in range(on_ref.shape[0]):
        on = on_ref[s]
        hi = on.astype(BF)
        grad = grad_ref[s]
        ghi = grad.astype(BF)
        out_ref[s, :, :width] = hi
        out_ref[s, :, width : 2 * width] = (on - hi.astype(F32)).astype(BF)
        if s + 1 < on_ref.shape[0]:
            out_ref[s + 1, :, 2 * width : 3 * width] = hi
        if s > 0:
            out_ref[s - 1, :, 3 * width : 4 * width] = hi
        out_ref[s, :, 4 * width : 5 * width] = ghi
        out_ref[s, :, 5 * width : 6 * width] = (grad - ghi.astype(F32)).astype(BF)
    out_ref[0, :, 2 * width : 3 * width] = blank
    out_ref[on_ref.shape[0] - 1, :, 3 * width : 4 * width] = blank


def payload(on, grad):
    bands, width, channels = on.shape
    return call(
        payload_kernel, [sds((bands, width, 6 * channels), BF)], [on, grad], name="payload", limit=56
    )[0]


def prep_kernel(
    mix_ref, w1_ref, w2_ref, b1_ref, b2_ref, *refs
):
    stage1, stage2 = refs[-2:]
    flows = mix_ref.shape[0]
    row = lax.broadcasted_iota(jnp.int32, (CH, CH), 0)
    col = lax.broadcasted_iota(jnp.int32, (CH, CH), 1)
    eye = (row == col).astype(F32)
    near = (row // 16) == (col // 16)
    units = []
    for k in range(flows):
        mix = mix_ref[k]
        units.append(jnp.where(row > col, mix, 0.0))
        units.append(jnp.where(row < col, mix, 0.0))
    inner = [jnp.where(near, u, 0.0) for u in units]
    outer = [u - i for u, i in zip(units, inner)]
    power = inner
    blocks = [eye - n for n in inner]
    for _ in range(3):
        power = [mm_high(p, p) for p in power]
        blocks = [mm_high(b, eye + p) for b, p in zip(blocks, power)]
    power = [mm_high(b, o) for b, o in zip(blocks, outer)]
    whole = [eye - p for p in power]
    for _ in range(2):
        power = [mm_high(p, p) for p in power]
        whole = [mm_high(w, eye + p) for w, p in zip(whole, power)]
    inverses = [mm_high(w, b) for w, b in zip(whole, blocks)]
    for k in range(flows):
        inv_ref, lut_ref, w1t_ref, w2t_ref, w2k_ref, w1k_ref, b2c_ref = refs[7 * k : 7 * k + 7]
        inv_ref[...] = mm_high(inverses[2 * k + 1], inverses[2 * k])
        lut_ref[...] = mm_high(units[2 * k] + eye, units[2 * k + 1] + eye).T
        for tap in range(9):
            stage1[tap * HALF : (tap + 1) * HALF, :] = 0.5 * w1_ref[k, tap].astype(F32)
            stage2[tap * CH : (tap + 1) * CH, :] = 0.5 * w2_ref[k, 8 - tap].astype(F32)
        hi, mid, low = split3(0.5 * b1_ref[k : k + 1, :])
        stage1[9 * HALF :, :] = jnp.zeros((IN_ROWS - 9 * HALF, HID), F32)
        for i, part in enumerate((hi, mid, low)):
            stage1[9 * HALF + i : 9 * HALF + i + 1, :] = part.astype(F32)
        w1t_ref[...] = stage1[...].T.astype(BF)
        w2t_ref[...] = stage2[...].T.astype(BF)
        for a in range(3):
            for b in range(3):
                w2k_ref[b * CH : (b + 1) * CH, a * HID : (a + 1) * HID] = w2_ref[k, 3 * a + b]
                w1k_ref[b * HALF : (b + 1) * HALF, a * HID : (a + 1) * HID] = w1_ref[
                    k, 3 * (2 - a) + b
                ]
        b2c_ref[...] = jnp.broadcast_to(b2_ref[k : k + 1, :], (8, CH)).T


def prep(mix_factors, in_kernel, out_kernel, in_bias, out_bias):
    flows = mix_factors.shape[0]
    outs = call(
        prep_kernel,
        [
            sds((CH, CH), F32),
            sds((CH, CH), F32),
            sds((HID, IN_ROWS), BF),
            sds((HID, 9 * CH), BF),
            sds((3 * CH, 3 * HID), BF),
            sds((3 * HALF, 3 * HID), BF),
            sds((CH, 8), F32),
        ]
        * flows,
        [mix_factors, in_kernel, out_kernel, in_bias, out_bias],
        scratch=[pltpu.VMEM((IN_ROWS, HID), F32), pltpu.VMEM((9 * CH, HID), F32)],
        name="prep",
        limit=56,
    )
    return [outs[i::7] for i in range(7)]


def turn_kernel(recv_ref, above_ref, mid_ref, below_ref, ya_ref, ga_ref, stage):
    width = 2 * CH
    row = lax.broadcasted_iota(jnp.int32, (width, width), 0)
    col = lax.broadcasted_iota(jnp.int32, (width, width), 1)
    pick = (col == 4 * (row % HALF) + row // HALF).astype(BF)
    none = jnp.zeros((width, width), BF)
    first = jnp.concatenate([pick, none], axis=1)
    second = jnp.concatenate([none, pick], axis=1)
    both = jnp.concatenate([pick, pick], axis=1)
    sources, count = recv_ref.shape[0], recv_ref.shape[1]
    for s in range(sources):
        stage[s * count : (s + 1) * count, :] = recv_ref[s].astype(F32)
    pair = stage[:, : 2 * width].astype(BF)
    kept = mm_nt(both, pair)
    mid_ref[...] = mm_nt(first, pair).astype(BF)
    pair = stage[:, 2 * width : 4 * width].astype(BF)
    above_ref[...] = mm_nt(first, pair).astype(BF)
    below_ref[...] = mm_nt(second, pair).astype(BF)
    grad = mm_nt(both, stage[:, 4 * width :].astype(BF))
    for k in range(4):
        ya_ref[:, k * COLS : (k + 1) * COLS] = kept[k * HALF : (k + 1) * HALF]
        ga_ref[:, k * COLS : (k + 1) * COLS] = grad[k * HALF : (k + 1) * HALF]


def turn(recv):
    return call(
        turn_kernel,
        [sds((2 * CH, COLS), BF)] * 3 + [sds((HALF, CELLS), F32)] * 2,
        [recv],
        scratch=[pltpu.VMEM((COLS, recv.shape[2]), F32)],
        flops=4 * 10**9,
        name="turn",
    )


def stack_planes(even, odd, factor=None):
    if factor is not None:
        even = (even.astype(F32) * factor).astype(BF)
        odd = (odd.astype(F32) * factor).astype(BF)
    left = from_left(odd.astype(F32)).astype(BF)
    right = from_right(even.astype(F32)).astype(BF)
    return jnp.concatenate([left, even, odd, right], axis=0)


def fill_input_columns(flags_ref, above_ref, mid_ref, below_ref, columns, first, count):
    refs = {-2: (above_ref, 0), -1: (above_ref, CH), 0: (mid_ref, 0)}
    refs.update({1: (mid_ref, CH), 2: (below_ref, 0), 3: (below_ref, CH)})
    for source in range(first - 1, first + count + 1):
        ref, at = refs[source]
        factor = flags_ref[0] if source < 0 else flags_ref[1] if source > 1 else None
        stacked = stack_planes(ref[at : at + HALF], ref[at + HALF : at + CH], factor)
        for a in range(3):
            target = source - a + 1 - first
            if 0 <= target < count:
                for p in range(2):
                    lane = (2 * target + p) * COLS
                    columns[a * 144 : (a + 1) * 144, lane : lane + COLS] = stacked[
                        p * HALF : p * HALF + 144
                    ]
    extra = IN_ROWS - 9 * HALF
    row = lax.broadcasted_iota(jnp.int32, (extra, count * ROW), 0)
    columns[9 * HALF :, :] = jnp.where(row < 3, 1.0, 0.0).astype(BF)


def fill_grad_columns(flags_ref, above_ref, mid_ref, below_ref, columns):
    for source in range(-2, 4):
        ref = above_ref if source < 0 else below_ref if source > 1 else mid_ref
        factor = flags_ref[0] if source < 0 else flags_ref[1] if source > 1 else None
        at = (source % 2) * 2 * CH
        stacked = stack_planes(ref[at : at + CH], ref[at + CH : at + 2 * CH], factor)
        for a in range(3):
            target = source - a + 2
            if 0 <= target < 4:
                for p in range(2):
                    lane = (2 * target + p) * COLS
                    columns[a * 288 : (a + 1) * 288, lane : lane + COLS] = stacked[
                        p * CH : p * CH + 288
                    ]


def put_out_grad(raw, moved, out_ref):
    for r in range(2):
        for p in range(2):
            lane = (2 * r + p) * COLS
            at = (2 * r + p) * CH
            out_ref[at : at + HALF] = raw[:, lane : lane + COLS].astype(BF)
            out_ref[at + HALF : at + CH] = moved[:, lane : lane + COLS].astype(BF)


def forward_kernel(with_grad, flags_ref, *refs):
    above_ref, mid_ref, below_ref, *weights, ya_ref, yb_ref = refs[:9]
    columns, pre, outs, *held, sems = refs[-8:]
    w1t_ref, w2k_ref, b2_ref, inv_ref = held
    copies = [
        pltpu.make_async_copy(source, target, sems.at[i])
        for i, (source, target) in enumerate(zip(weights, held))
    ]
    for copy in copies:
        copy.start()
    if with_grad:
        x_ref, rows, slope_ref, next_ref, grad_ref, moved_ref = refs[9:-8]
    else:
        x_ref, rows, slope_ref, scale_ref = refs[9:-8]
    fill_input_columns(flags_ref, above_ref, mid_ref, below_ref, columns, -1, 4)
    for copy in copies:
        copy.wait()
    for h in range(4):
        pre[h % 2] = mm(w1t_ref[...], columns[:, h * ROW : (h + 1) * ROW])
        inside = flags_ref[0] if h == 0 else flags_ref[1] if h == 3 else None

        def activate(step, carry):
            at = pl.multiple_of(step * 16, 16)
            half = pre[h % 2, pl.ds(at, 16), :]
            bent = jnp.tanh(half)
            more = 1.0 + bent
            hidden = half * more
            slope = more * (1.0 + half * (1.0 - bent))
            if inside is not None:
                hidden = hidden * inside
                slope = slope * inside
            rows[pl.ds(h * HID + at, 16), :] = hidden.astype(BF)
            slope_ref[pl.ds(h * HID + at, 16), :] = slope
            return carry

        lax.fori_loop(0, HID // 16, activate, 0, unroll=True)
    for r in range(2):
        taps = mm(w2k_ref[...], rows[r * HID : (r + 3) * HID, :])
        even, odd = taps[:, :COLS], taps[:, COLS:]
        lane = 2 * r * COLS
        outs[:, lane : lane + COLS] = from_left(odd[:CH]) + even[CH : 2 * CH] + odd[2 * CH :]
        outs[:, lane + COLS : lane + ROW] = even[:CH] + odd[CH : 2 * CH] + from_right(even[2 * CH :])
    raw = outs[:HALF] + b2_ref[:HALF, :1]
    shift = outs[HALF:] + b2_ref[HALF:, :1]
    inverse = 1.0 + jnp.exp(-(raw + 2.0))
    scale = 1.0 / inverse
    moved_in = yb_ref[...] * inverse - shift
    x = mm_high(inv_ref[...], jnp.concatenate([ya_ref[...], moved_in], axis=0))
    x_ref[...] = x
    if with_grad:
        moved_grad = yb_ref[...]
        moved = moved_grad * scale
        moved_ref[...] = moved
        put_out_grad((moved_grad * yb_ref[...] - 1.0) * (1.0 - scale), moved, grad_ref)
        for k in range(4):
            next_ref[k * HALF : (k + 1) * HALF] = x[:HALF, k * COLS : (k + 1) * COLS].astype(BF)
    else:
        scale_ref[...] = scale


def forward(flags, above, mid, below, w1t, w2k, b2c, inv, ya, yb, with_grad):
    outs = [sds((CH, CELLS), F32), sds((4 * HID, ROW), BF), sds((4 * HID, ROW), F32)]
    if with_grad:
        outs += [
            sds((2 * CH, COLS), BF),
            sds((4 * CH, COLS), BF),
            sds((HALF, CELLS), F32),
        ]
    else:
        outs += [sds((HALF, CELLS), F32)]
    return call(
        functools.partial(forward_kernel, with_grad),
        outs,
        [flags, above, mid, below, w1t, w2k, b2c, inv, ya, yb],
        scratch=[
            pltpu.VMEM((IN_ROWS, 4 * ROW), BF),
            pltpu.VMEM((2, HID, ROW), F32),
            pltpu.VMEM((CH, CELLS), F32),
            pltpu.VMEM((HID, IN_ROWS), BF),
            pltpu.VMEM((3 * CH, 3 * HID), BF),
            pltpu.VMEM((CH, 8), F32),
            pltpu.VMEM((CH, CH), F32),
            pltpu.SemaphoreType.DMA((4,)),
        ],
        smem=(0,),
        hbm=(4, 5, 6, 7),
        limit=24,
        flops=4 * 10**9,
        name="forward",
    )


def backward_kernel(
    flags_ref, above_ref, mid_ref, below_ref, w2t_ref, slope_ref, w1k_ref, gpre_ref, in_ref,
    columns, hid_grad,
):
    fill_grad_columns(flags_ref, above_ref, mid_ref, below_ref, columns)
    for h in range(4):
        hid_grad[h % 2] = mm(w2t_ref[...], columns[:, h * ROW : (h + 1) * ROW])

        def slope(step, carry):
            at = pl.multiple_of(step * 16, 16)
            gpre_ref[pl.ds(h * HID + at, 16), :] = (
                hid_grad[h % 2, pl.ds(at, 16), :] * slope_ref[pl.ds(h * HID + at, 16), :]
            ).astype(BF)
            return carry

        lax.fori_loop(0, HID // 16, slope, 0, unroll=True)
    b0, b1, b2 = slice(0, HALF), slice(HALF, CH), slice(CH, 3 * HALF)
    for r in range(2):
        taps = mm(w1k_ref[...], gpre_ref[r * HID : (r + 3) * HID, :])
        even, odd = taps[:, :COLS], taps[:, COLS:]
        in_ref[r * CH : r * CH + HALF] = odd[b0] + even[b1] + from_left(odd[b2])
        in_ref[r * CH + HALF : (r + 1) * CH] = from_right(even[b0]) + odd[b1] + even[b2]


def backward(flags, above, mid, below, w2t, slope, w1k):
    return call(
        backward_kernel,
        [sds((4 * HID, ROW), BF), sds((2 * CH, COLS), F32)],
        [flags, above, mid, below, w2t, slope, w1k],
        scratch=[pltpu.VMEM((9 * CH, 4 * ROW), BF), pltpu.VMEM((2, HID, ROW), F32)],
        smem=(0,),
        flops=6 * 10**9,
        limit=20,
        name="backward",
    )


def out_weight_kernel(core_ref, grad_ref, rows_ref, keep_ref, give_ref, bias_ref, left, right, whole):
    for r in range(2):
        at = 2 * r * CH
        stacked = stack_planes(grad_ref[at : at + CH], grad_ref[at + CH : at + 2 * CH])
        left[r] = stacked[: 3 * CH]
        right[r] = stacked[CH:]
    part = [jnp.concatenate([left[r], right[r]], axis=1) for r in range(2)]
    for a in range(3):
        whole[...] = mm_nt(part[0], rows_ref[a * HID : (a + 1) * HID]) + mm_nt(
            part[1], rows_ref[(a + 1) * HID : (a + 2) * HID]
        )
        for ref, core in ((keep_ref, core_ref[0]), (give_ref, 1 - core_ref[0])):
            ref[a] = whole[pl.ds(pl.multiple_of(core * TAP_HALF, 8), TAP_HALF), :]
    ones = jnp.ones((8, COLS), BF)
    total = mm_nt(ones, grad_ref[:CH]) + mm_nt(ones, grad_ref[CH : 2 * CH])
    bias_ref[...] = total + (
        mm_nt(ones, grad_ref[2 * CH : 3 * CH]) + mm_nt(ones, grad_ref[3 * CH :])
    )


def out_weight(core, grad, rows):
    return call(
        out_weight_kernel,
        [sds((3, TAP_HALF, HID), F32), sds((3, TAP_HALF, HID), F32), sds((8, CH), F32)],
        [core, grad, rows],
        scratch=[
            pltpu.VMEM((2, 3 * CH, COLS), BF),
            pltpu.VMEM((2, 3 * CH, COLS), BF),
            pltpu.VMEM((3 * CH, HID), F32),
        ],
        smem=(0,),
        flops=2 * 10**9,
        name="out_weight",
    )


def in_weight_kernel(
    core_ref, flags_ref, above_ref, mid_ref, below_ref, gpre_ref, keep_ref, give_ref, columns,
    whole,
):
    fill_input_columns(flags_ref, above_ref, mid_ref, below_ref, columns, 0, 2)
    whole[...] = mm_nt(columns[:, :ROW], gpre_ref[HID : 2 * HID]) + mm_nt(
        columns[:, ROW:], gpre_ref[2 * HID : 3 * HID]
    )
    for ref, core in ((keep_ref, core_ref[0]), (give_ref, 1 - core_ref[0])):
        ref[...] = whole[pl.ds(pl.multiple_of(core * IN_HALF, 8), IN_HALF), :]


def in_weight(core, flags, above, mid, below, gpre):
    return call(
        in_weight_kernel,
        [sds((IN_HALF, HID), F32), sds((IN_HALF, HID), F32)],
        [core, flags, above, mid, below, gpre],
        scratch=[pltpu.VMEM((IN_ROWS, CELLS), BF), pltpu.VMEM((IN_ROWS, HID), F32)],
        smem=(0, 1),
        flops=10**9,
        name="in_weight",
    )


def close_kernel(next_step, flow, core_ref, *refs):
    in_ref, ga_ref, moved_ref, lut_ref, x_ref, mix_ref, bias_ref = refs[:7]
    whole, small = refs[-2:]
    if next_step:
        scale_ref, gx_ref, keep_ref, give_ref, grad_ref, nmoved_ref = refs[7:-2]
    else:
        gx_ref, keep_ref, give_ref = refs[7:-2]
    for k in range(4):
        lane = k * COLS
        whole[:HALF, lane : lane + COLS] = (
            ga_ref[:HALF, lane : lane + COLS] + in_ref[k * HALF : (k + 1) * HALF]
        )
    whole[HALF:] = moved_ref[...]
    gx = mm_high(lut_ref[...], whole[...])
    gx_ref[...] = gx
    if next_step:
        scale = scale_ref[...]
        moved_grad = gx[HALF:]
        moved = moved_grad * scale
        nmoved_ref[...] = moved
        put_out_grad((moved_grad * x_ref[HALF:] - 1.0) * (1.0 - scale), moved, grad_ref)
    ghi, gmid, _ = split3(whole[...])
    xhi, xmid, _ = split3(x_ref[...])
    outer = mm_nt(ghi, xhi) + (mm_nt(ghi, xmid) + mm_nt(gmid, xhi))
    row = lax.broadcasted_iota(jnp.int32, (CH, CH), 0)
    col = lax.broadcasted_iota(jnp.int32, (CH, CH), 1)
    eye = (row == col).astype(F32)
    mix = mix_ref[flow]
    lower = jnp.where(row > col, mix, 0.0) + eye
    upper = jnp.where(row < col, mix, 0.0) + eye
    by_upper = mm_high(outer, upper.T)
    by_lower = mm_high(lower.T, outer)
    small[:, :CH] = jnp.where(row > col, by_upper, jnp.where(row < col, by_lower, 0.0))
    small[:, CH:] = jnp.zeros((CH, 2 * 128 - CH), F32)
    small[:8, 128 : 128 + CH] = bias_ref[...]
    for ref, core in ((keep_ref, core_ref[0]), (give_ref, 1 - core_ref[0])):
        ref[...] = small[pl.ds(pl.multiple_of(core * HALF, 8), HALF), :]


def close(core, gin, ga, moved, lut, x, mix, flow, bias, scale=None):
    outs = [sds((CH, CELLS), F32), sds((HALF, 256), F32), sds((HALF, 256), F32)]
    ins = [core, gin, ga, moved, lut, x, mix, bias]
    if scale is not None:
        outs += [sds((4 * CH, COLS), BF), sds((HALF, CELLS), F32)]
        ins += [scale]
    return call(
        functools.partial(close_kernel, scale is not None, flow),
        outs,
        ins,
        scratch=[pltpu.VMEM((CH, CELLS), F32), pltpu.VMEM((CH, 256), F32)],
        smem=(0,),
        flops=10**9,
        name="close",
    )


def weave_kernel(x_ref, out_ref):
    size = 256
    row = lax.broadcasted_iota(jnp.int32, (size, size), 0)
    col = lax.broadcasted_iota(jnp.int32, (size, size), 1)
    place = (col == 2 * (row % 128) + row // 128).astype(BF)
    for r in range(2):
        for t in range(3):
            lane = r * ROW + t * 128
            pair = jnp.concatenate(
                [x_ref[:, lane : lane + 128], x_ref[:, lane + COLS : lane + COLS + 128]], axis=1
            )
            hi, mid, low = split3(pair)
            woven = mm(hi, place) + (mm(mid, place) + mm(low, place))
            out_ref[0, :, r, t * size : (t + 1) * size] = woven


def weave(x):
    return call(weave_kernel, [sds((1, CH, 2, ROW), F32)], [x], name="weave")[0]


PARTS = ((0, IN_HALF), (224, TAP_HALF), (368, TAP_HALF), (512, TAP_HALF), (656, HALF))
FLOW_ROWS = 704
GROUP = 88


def merge_kernel(*refs):
    out_ref, total = refs[-2:]
    for k in range(2):
        own_in, own_out, own_small, got_in, got_out, got_small = refs[6 * k : 6 * k + 6]
        at = k * FLOW_ROWS
        total[at : at + IN_HALF] = own_in[...] + got_in[...]
        for a in range(3):
            start = at + IN_HALF + a * TAP_HALF
            total[start : start + TAP_HALF] = own_out[a] + got_out[a]
        small = own_small[...] + got_small[...]
        start = at + FLOW_ROWS - HALF
        total[start : start + HALF, :256] = small
        total[start : start + HALF, 256:] = small - small.astype(BF).astype(F32)
    for g in range(2 * FLOW_ROWS // GROUP):
        for lane in range(4):
            out_ref[4 * g + lane] = total[
                g * GROUP : (g + 1) * GROUP, lane * 128 : (lane + 1) * 128
            ].astype(BF)


def merge(own0, got0, own1, got1):
    shares = 2 * FLOW_ROWS // GROUP * 4
    return call(
        merge_kernel,
        [sds((shares, GROUP, 128), BF)],
        [*own0, *got0, *own1, *got1],
        scratch=[pltpu.VMEM((2 * FLOW_ROWS, HID), F32)],
        name="merge",
    )[0]


def total_kernel(cells, shares_ref, out_ref):
    total = shares_ref[0].astype(F32)
    for s in range(1, shares_ref.shape[0]):
        total += shares_ref[s].astype(F32)
    mean = (total * (1.0 / cells)).astype(BF)
    for s in range(shares_ref.shape[0]):
        out_ref[s] = mean


def totals(shares, cells):
    return call(
        functools.partial(total_kernel, cells), [sds(shares.shape, BF)], [shares], name="totals"
    )[0]


def unpack_kernel(core_ref, mine_ref, other_ref, win_ref, wout_ref, mix_ref, bin_ref, bout_ref, rows):
    mine_first = core_ref[0] == 0
    for half in range(2):
        for g in range(2 * FLOW_ROWS // GROUP):
            for lane in range(4):
                mine = mine_ref[4 * g + lane].astype(F32)
                other = other_ref[4 * g + lane].astype(F32)
                first, second = (mine, other) if half == 0 else (other, mine)
                rows[half, g * GROUP : (g + 1) * GROUP, lane * 128 : (lane + 1) * 128] = jnp.where(
                    mine_first, first, second
                )
    for k in range(2):
        at = k * FLOW_ROWS
        win_ref[k, :IN_HALF] = rows[0, at : at + IN_HALF]
        win_ref[k, IN_HALF:] = rows[1, at : at + 9 * HALF - IN_HALF]
        bin_ref[k : k + 1, :] = rows[1, at + 9 * HALF - IN_HALF : at + 9 * HALF - IN_HALF + 1]
        for a in range(3):
            start = at + IN_HALF + a * TAP_HALF
            wout_ref[k, 3 * a + 2] = rows[0, start : start + CH]
            wout_ref[k, 3 * a + 1, :HALF] = rows[0, start + CH : start + TAP_HALF]
            wout_ref[k, 3 * a + 1, HALF:] = rows[1, start : start + HALF]
            wout_ref[k, 3 * a] = rows[1, start + HALF : start + TAP_HALF]
        start = at + FLOW_ROWS - HALF
        for half in range(2):
            block = rows[half, start : start + HALF]
            mix_ref[k, half * HALF : (half + 1) * HALF] = block[:, :CH] + block[:, 256 : 256 + CH]
        block = rows[0, start : start + 8]
        bout_ref[k] = block[:, 128 : 128 + CH] + block[:, 384 : 384 + CH]


def unpack(core, mine, other):
    return call(
        unpack_kernel,
        [
            sds((2, 9 * HALF, HID), F32),
            sds((2, 9, CH, HID), F32),
            sds((2, CH, CH), F32),
            sds((2, HID), F32),
            sds((2, 8, CH), F32),
        ],
        [core, mine, other],
        scratch=[pltpu.VMEM((2, 2 * FLOW_ROWS, HID), F32)],
        smem=(0,),
        name="unpack",
    )


def after(x, *others):
    return lax.optimization_barrier((x, *others))[0]


def local(passed_on, passed_grad, latent, mix_factors, in_kernel, in_bias, out_kernel, out_bias):
    lat_index = lax.axis_index(LAT)
    lat_count = lax.axis_size(LAT)
    forth = [(i, (i + 1) % lat_count) for i in range(lat_count)]
    back = [(t, s) for s, t in forth]
    swap = [(0, 1), (1, 0)]
    flags = jnp.stack([lat_index > 0, lat_index < lat_count - 1]).astype(F32)
    core = lax.axis_index("c").astype(jnp.int32).reshape(1)

    block = payload(
        jnp.transpose(passed_on[0], (1, 2, 0)), jnp.transpose(passed_grad[0], (1, 2, 0))
    )
    recv = lax.all_to_all(block, LAT, 0, 0, tiled=True)
    inv, lut, w1t, w2t, w2k, w1k, b2c = prep(mix_factors, in_kernel, out_kernel, in_bias, out_bias)
    w1 = in_kernel.reshape(2, 9 * HALF, HID)
    yb = latent.reshape(HALF, CELLS)

    above, mid, below, ya, ga = turn(recv)
    x1, rows1, slope1, next_mid, grad1, moved1 = forward(
        flags, above, mid, below, w1t[1], w2k[1], b2c[1], inv[1], ya, yb, True
    )
    above0 = lax.ppermute(next_mid, LAT, forth)
    below0 = lax.ppermute(next_mid, LAT, back)
    top1 = lax.ppermute(grad1, LAT, forth)
    bottom1 = lax.ppermute(grad1, LAT, back)
    keep_out1, give_out1, bias1 = out_weight(core, grad1, rows1)
    x0, rows0, slope0, scale0 = forward(
        after(flags, keep_out1), above0, next_mid, below0, w1t[0], w2k[0], b2c[0], inv[0],
        x1[:HALF], x1[HALF:], False,
    )
    got_out1 = lax.ppermute(give_out1, "c", swap)
    gpre1, in1 = backward(after(flags, x0), top1, grad1, bottom1, w2t[1], slope1, w1k[1])
    gx1, keep_small1, give_small1, grad0, moved0 = close(
        core, in1, ga, moved1, lut[1], x1, mix_factors, 1, bias1, scale0
    )
    top0 = lax.ppermute(grad0, LAT, forth)
    bottom0 = lax.ppermute(grad0, LAT, back)
    got_small1 = lax.ppermute(give_small1, "c", swap)
    keep_in1, give_in1 = in_weight(after(core, grad0), flags, above, mid, below, gpre1)
    got_in1 = lax.ppermute(give_in1, "c", swap)
    keep_out0, give_out0, bias0 = out_weight(after(core, keep_in1), grad0, rows0)
    rebuilt = weave(after(x0, keep_out0))
    gpre0, in0 = backward(after(flags, rebuilt), top0, grad0, bottom0, w2t[0], slope0, w1k[0])
    got_out0 = lax.ppermute(give_out0, "c", swap)
    keep_in0, give_in0 = in_weight(after(core, in0), flags, above0, next_mid, below0, gpre0)
    got_in0 = lax.ppermute(give_in0, "c", swap)
    gx0, keep_small0, give_small0 = close(
        after(core, keep_in0), in0, gx1, moved0, lut[0], x0, mix_factors, 0, bias0
    )
    got_small0 = lax.ppermute(give_small0, "c", swap)

    packed = merge(
        (keep_in0, keep_out0, keep_small0),
        (got_in0, got_out0, got_small0),
        (keep_in1, keep_out1, keep_small1),
        (got_in1, got_out1, got_small1),
    )
    shares = lax.all_to_all(packed, CHIPS, 0, 0, tiled=True)
    input_grad = weave(after(gx0, packed))
    cells = float(CELLS * lat_count * lax.axis_size(ENS))
    spread = totals(after(shares, input_grad), cells)
    mine = lax.all_to_all(spread, CHIPS, 0, 0, tiled=True)
    other = lax.ppermute(mine, "c", swap)
    in_grad, out_grad, mix_grad, in_bias_grad, out_bias_grad = unpack(core, mine, other)
    return (
        rebuilt,
        input_grad,
        mix_grad,
        in_grad.reshape(2, 9, HALF, HID),
        in_bias_grad,
        out_grad,
        out_bias_grad[:, 0],
    )


def solution(mesh):
    split = Mesh(mesh.devices.reshape(4, 2, 2, 4, 2), ("y", "xl", "c", "z", "xh"))
    return jax.shard_map(
        local,
        mesh=split,
        in_specs=(
            P(ENS, None, None, LAT),
            P(ENS, None, None, LAT),
            P(ENS, None, LAT, None),
            P(),
            P(),
            P(),
            P(),
            P(),
        ),
        out_specs=(P(ENS, None, LAT, None), P(ENS, None, LAT, None), P(), P(), P(), P(), P()),
        check_vma=False,
    )
```

profile of v0, /device:TPU:1, one launch (start us, length us, event | category | flops | bytes accessed | tf_op | source)
XLA Modules:
  0.0 137.8 jit_solution(299000417374698939)
XLA Ops:
  0.6 2.3 %payload.1 = bf16[16,24,1152]{2,1,0:T(8,128)(2,1)} custom-call(f32[16,24,192]{2,1,0:T(8,128)} %bitcast.11, f32[16,24,192]{2,1,0:T(8,128)} %bitcast.12), custom_call_target="tpu_custom_call" | custom-call | bytes 1474560 | tf_op jit(solution)/shard_map/payload/pallas_call | solution.py:67
  3.0 6.9 %all-to-all-start = ((bf16[16,24,1152]{2,1,0:T(8,128)(2,1)}), bf16[16,24,1152]{2,1,0:T(8,128)(2,1)S(1)}, u32[]{:S(2)}, u32[]{:S(2)}) async-start(bf16[16,24,1152]{2,1,0:T(8,128)(2,1)} %payload.1), calls=%async_computation | async-start | bytes 1769472 | tf_op jit(solution)/shard_map/all_to_all | solution.py:650
  9.9 0.7 reduce
  10.6 7.0 %prep.1 = (f32[96,96]{1,0:T(8,128)}, f32[96,96]{1,0:T(8,128)}, bf16[512,448]{1,0:T(8,128)(2,1)}, bf16[512,864]{1,0:T(8,128)(2,1)}, bf16[288,1536]{1,0:T(8,128)(2...) custom-call(f32[2,96,96]{2,1,0:T(8,128)} %refs_5_.3, ...), custom_call_target="tpu_custom_call" | custom-call | bytes 8227584 | tf_op jit(solution)/shard_map/prep/pallas_call | solution.py:67
  17.7 6.2 %all-to-all-done.recv_ref = bf16[16,24,1152]{2,1,0:T(8,128)(2,1)S(1)} async-done(((bf16[16,24,1152]{2,1,0:T(8,128)(2,1)}), bf16[16,24,1152]{2,1,0:T(8,128)(2,1)S(1)}, u32[]{:S(2)}, u32[]{:S(2)}) %all-to-all-start) | async-done | bytes 884768 | tf_op jit(solution)/shard_map/all_to_all | solution.py:650
  23.9 0.7 turn.1
  24.7 5.8 %forward.2 = (f32[96,1536]{1,0:T(8,128)S(1)}, bf16[2048,768]{1,0:T(8,128)(2,1)S(1)}, f32[2048,768]{1,0:T(8,128)S(1)}, bf16[192,384]{1,0:T(8,128)(2,1)S(1)}, bf16...) custom-call(f32[2]{0:T(128)S(1)} %add_convert_fusion.flags_ref, ...), custom_call_target="tpu_custom_call" | custom-call | flops 4000000000 | bytes 13179912 | tf_op jit(solution)/shard_map/forward/pallas_call | solution.py:67
  30.5 0.9 collective-permute-start.1
  31.4 0.9 collective-permute-start
  32.3 1.7 %collective-permute-start.2 = (bf16[384,384]{1,0:T(8,128)(2,1)S(1)}, bf16[384,384]{1,0:T(8,128)(2,1)S(1)}, u32[]{:S(2)}, u32[]{:S(2)}) collective-permute-start(bf16[384,384]{1,0:T(8,128)(2,1)S(1)} %get-tuple-element.81.grad_ref.mid_ref), channel_id=1, source_target_pairs={{0,8},{8,16},{16,24},{24,32},{32,40},{40,48},{48,56},{56,64},{64,7... | collective-permute-start | bytes 884744 | tf_op jit(solution)/shard_map/ppermute | solution.py:661
  34.2 1.7 %out_weight.2 = (f32[3,144,512]{2,1,0:T(8,128)S(1)}, f32[3,144,512]{2,1,0:T(8,128)S(1)}, f32[8,96]{1,0:T(8,128)S(1)}) custom-call(s32[1]{0:T(128)} %bitcast.2.core_ref, bf16[384,384]{1,0:T(8,128)(2,1)S(1)} %get-tuple-element.81.grad_ref.mid_ref, bf16[2048,768]{1,0:T(8,128)(2,1)S(1)} %get-tuple-element.82.rows_ref), custom_call_target="tpu_custom_call" | custom-call | flops 2000000000 | bytes 5213188 | tf_op jit(solution)/shard_map/out_weight/pallas_call | solution.py:67
  36.0 5.7 %forward.3 = (f32[96,1536]{1,0:T(8,128)S(1)}, bf16[2048,768]{1,0:T(8,128)(2,1)S(1)}, f32[2048,768]{1,0:T(8,128)S(1)}, f32[48,1536]{1,0:T(8,128)S(1)}) custom-call(f32[2]{0:T(128)S(1)} %add_convert_fusion.flags_ref, bf16[192,384]{1,0:T(8,128)(2,1)S(1)} %collective-permute-done.refs_0_.above_ref, bf16[192,384]{1,0:T(8,128)(2,1)S(1)} %get-tuple-element.85.refs_1_.mid_ref, ...), custom_call_target="tpu_custom_call" | custom-call | flops 4000000000 | bytes 12737544 | tf_op jit(solution)/shard_map/forward/pallas_call | solution.py:67
  42.0 5.0 %backward.2 = (bf16[2048,768]{1,0:T(8,128)(2,1)S(1)}, f32[192,384]{1,0:T(8,128)S(1)}) custom-call(f32[2]{0:T(128)S(1)} %add_convert_fusion.flags_ref, bf16[384,384]{1,0:T(8,128)(2,1)S(1)} %collective-permute-done.2.above_ref, bf16[384,384]{1,0:T(8,128)(2,1)S(1)} %get-tuple-element.81.grad_ref.mid_ref, bf16[384,384]{1,0:T(8,128)(2,1)S(1)} %collective-permute-done.3.below_ref, ...), custom_call_target="tpu_custom_call" | custom-call | flops 6000000000 | bytes 11943944 | tf_op jit(solution)/shard_map/backward/pallas_call | solution.py:67
  47.0 1.3 close.2
  48.3 3.6 %collective-permute-start.5 = (bf16[384,384]{1,0:T(8,128)(2,1)S(1)}, bf16[384,384]{1,0:T(8,128)(2,1)S(1)}, u32[]{:S(2)}, u32[]{:S(2)}) collective-permute-start(bf16[384,384]{1,0:T(8,128)(2,1)S(1)} %get-tuple-element.102.grad_ref.mid_ref), channel_id=1, source_target_pairs={{8,0},{16,8},{24,16},{32,24},{40,32},{48,40},{56,48},{64,56},{72,6... | collective-permute-start | bytes 884744 | tf_op jit(solution)/shard_map/ppermute | solution.py:674
  51.9 1.4 %collective-permute-start.10 = (f32[3,144,512]{2,1,0:T(8,128)S(1)}, f32[3,144,512]{2,1,0:T(8,128)S(1)}, u32[]{:S(2)}, u32[]{:S(2)}) collective-permute-start(f32[3,144,512]{2,1,0:T(8,128)S(1)} %get-tuple-element.130), channel_id=1, source_target_pairs={{0,8},{8,0},{1,9},{9,1},{2,10},{10,2},{3,11},{11,3},{4,12},{12,4},... | collective-permute-start | bytes 2654216 | tf_op jit(solution)/shard_map/ppermute | solution.py:668
  53.3 1.5 %in_weight.2 = (f32[224,512]{1,0:T(8,128)S(1)}, f32[224,512]{1,0:T(8,128)S(1)}) custom-call(s32[1]{0:T(128)} %bitcast.2.core_ref, f32[2]{0:T(128)S(1)} %add_convert_fusion.flags_ref, bf16[192,384]{1,0:T(8,128)(2,1)S(1)} %get-tuple-element.73.refs_0_.above_ref, bf16[192,384]{1,0:T(8,128)(2,1)S(1)} %get-tuple-element.74.refs_1_.mid_ref, ...), custom_call_target="tpu_custom_call" | custom-call | flops 1000000000 | bytes 4505612 | tf_op jit(solution)/shard_map/in_weight/pallas_call | solution.py:67
  54.9 1.7 %out_weight.3 = (f32[3,144,512]{2,1,0:T(8,128)S(1)}, f32[3,144,512]{2,1,0:T(8,128)S(1)}, f32[8,96]{1,0:T(8,128)S(1)}) custom-call(s32[1]{0:T(128)} %bitcast.2.core_ref, bf16[384,384]{1,0:T(8,128)(2,1)S(1)} %get-tuple-element.102.grad_ref.mid_ref, bf16[2048,768]{1,0:T(8,128)(2,1)S(1)} %get-tuple-element.107.rows_ref), custom_call_target="tpu_custom_call" | custom-call | flops 2000000000 | bytes 5213188 | tf_op jit(solution)/shard_map/out_weight/pallas_call | solution.py:67
  56.7 1.4 %weave.2 = f32[1,96,2,768]{3,2,1,0:T(2,128)} custom-call(f32[96,1536]{1,0:T(8,128)S(1)} %get-tuple-element.109.x_ref.refs_4_), custom_call_target="tpu_custom_call" | custom-call | bytes 1179648 | tf_op jit(solution)/shard_map/weave/pallas_call | solution.py:67
  58.7 4.9 %backward.3 = (bf16[2048,768]{1,0:T(8,128)(2,1)S(1)}, f32[192,384]{1,0:T(8,128)S(1)}) custom-call(f32[2]{0:T(128)S(1)} %add_convert_fusion.flags_ref, bf16[384,384]{1,0:T(8,128)(2,1)S(1)} %collective-permute-done.4.above_ref, bf16[384,384]{1,0:T(8,128)(2,1)S(1)} %get-tuple-element.102.grad_ref.mid_ref, ...), custom_call_target="tpu_custom_call" | custom-call | flops 6000000000 | bytes 11943944 | tf_op jit(solution)/shard_map/backward/pallas_call | solution.py:67
  63.5 1.5 %in_weight.3 = (f32[224,512]{1,0:T(8,128)S(1)}, f32[224,512]{1,0:T(8,128)S(1)}) custom-call(s32[1]{0:T(128)} %bitcast.2.core_ref, f32[2]{0:T(128)S(1)} %add_convert_fusion.flags_ref, bf16[192,384]{1,0:T(8,128)(2,1)S(1)} %collective-permute-done.refs_0_.above_ref, bf16[192,384]{1,0:T(8,128)(2,1)S(1)} %get-tuple-element.85.refs_1_.mid_ref, ...), custom_call_target="tpu_custom_call" | custom-call | flops 1000000000 | bytes 4505612 | tf_op jit(solution)/shard_map/in_weight/pallas_call | solution.py:67
  65.1 3.0 %collective-permute-start.6 = (f32[224,512]{1,0:T(8,128)S(1)}, f32[224,512]{1,0:T(8,128)S(1)}, u32[]{:S(2)}, u32[]{:S(2)}) collective-permute-start(f32[224,512]{1,0:T(8,128)S(1)} %get-tuple-element.125), channel_id=1, source_target_pairs={{0,8},{8,0},{1,9},{9,1},{2,10},{10,2},{3,11},{11,3},{4,12},{12,4},... | collective-permute-start | bytes 1376264 | tf_op jit(solution)/shard_map/ppermute | solution.py:683
  68.2 1.3 close.3
  70.0 0.9 collective-permute-done.8.refs_5_
  70.9 1.4 merge.1
  72.2 8.5 %all-to-all-start.1 = ((bf16[64,88,128]{2,1,0:T(8,128)(2,1)}), bf16[64,88,128]{2,1,0:T(8,128)(2,1)S(1)}, u32[]{:S(2)}, u32[]{:S(2)}) async-start(bf16[64,88,128]{2,1,0:T(8,128)(2,1)} %merge.1), calls=%async_computation.1 | async-start | bytes 2883584 | tf_op jit(solution)/shard_map/all_to_all | solution.py:695
  80.8 1.4 %weave.3 = f32[1,96,2,768]{3,2,1,0:T(2,128)} custom-call(f32[96,1536]{1,0:T(8,128)S(1)} %get-tuple-element.132.x_ref), custom_call_target="tpu_custom_call" | custom-call | bytes 1179648 | tf_op jit(solution)/shard_map/weave/pallas_call | solution.py:67
  82.2 20.2 %all-to-all-done.1.shares_ref = bf16[64,88,128]{2,1,0:T(8,128)(2,1)S(1)} async-done(((bf16[64,88,128]{2,1,0:T(8,128)(2,1)}), bf16[64,88,128]{2,1,0:T(8,128)(2,1)S(1)}, u32[]{:S(2)}, u32[]{:S(2)}) %all-to-all-start.1) | async-done | bytes 1441824 | tf_op jit(solution)/shard_map/all_to_all | solution.py:695
  102.7 24.6 %all_to_all.15.mine_ref = bf16[64,88,128]{2,1,0:T(8,128)(2,1)S(1)} all-to-all(bf16[64,88,128]{2,1,0:T(8,128)(2,1)S(1)} %totals.1), channel_id=1, replica_groups=mesh['y'=4,'xl'=2,'c'=2,'z'=4,'xh'=2] {'y','xl','z','xh'}, dimensions={0} | all-to-all | bytes 2883584 | tf_op jit(solution)/shard_map/all_to_all | solution.py:699
  127.3 4.0 %collective-permute-start.12 = (bf16[64,88,128]{2,1,0:T(8,128)(2,1)S(1)}, bf16[64,88,128]{2,1,0:T(8,128)(2,1)S(1)}, u32[]{:S(2)}, u32[]{:S(2)}) collective-permute-start(bf16[64,88,128]{2,1,0:T(8,128)(2,1)S(1)} %all_to_all.15.mine_ref), channel_id=1, source_target_pairs={{0,8},{8,0},{1,9},{9,1},{2,10},{10,2},{3,11},{11,3},{4,12},{12,4},... | collective-permute-start | bytes 4325384 | tf_op jit(solution)/shard_map/ppermute | solution.py:700
  131.3 2.8 %collective-permute-done.12.other_ref = bf16[64,88,128]{2,1,0:T(8,128)(2,1)S(1)} collective-permute-done((bf16[64,88,128]{2,1,0:T(8,128)(2,1)S(1)}, bf16[64,88,128]{2,1,0:T(8,128)(2,1)S(1)}, u32[]{:S(2)}, u32[]{:S(2)}) %collective-permute-start.12) | collective-permute-done | bytes 1441824 | tf_op jit(solution)/shard_map/ppermute | solution.py:700
  134.2 3.0 %unpack.1 = (f32[2,432,512]{2,1,0:T(8,128)}, f32[2,9,96,512]{3,2,1,0:T(8,128)}, f32[2,96,96]{2,1,0:T(8,128)}, f32[2,512]{1,0:T(2,128)}, f32[2,8,96]{2,1,0:T(8,128)S(1)}) custom-call(s32[1]{0:T(128)} %bitcast.2.core_ref, bf16[64,88,128]{2,1,0:T(8,128)(2,1)S(1)} %all_to_all.15.mine_ref, bf16[64,88,128]{2,1,0:T(8,128)(2,1)S(1)} %collective-permute-done.12.other_ref), custom_call_target="tpu_custom_call" | custom-call | bytes 8275972 | tf_op jit(solution)/shard_map/unpack/pallas_call | solution.py:67
  (54 shorter events, 2.5 us)
Async XLA Ops:
  0.6 9.2 %copy-start.15 = (f32[1,192,1,384]{3,2,1,0:T(1,128)S(1)}, f32[1,192,1,384]{3,2,1,0:T(1,128)}, u32[]{:S(2)}) copy-start(f32[1,192,1,384]{3,2,1,0:T(1,128)} %param.10) | copy-start | bytes 884740
  3.0 21.0 %all-to-all-start = ((bf16[16,24,1152]{2,1,0:T(8,128)(2,1)}), bf16[16,24,1152]{2,1,0:T(8,128)(2,1)S(1)}, u32[]{:S(2)}, u32[]{:S(2)}) async-start(bf16[16,24,1152]{2,1,0:T(8,128)(2,1)} %payload.1), calls=%async_computation | async-start | bytes 1769472 | tf_op jit(solution)/shard_map/all_to_all | solution.py:650
  17.7 6.9 %copy-start.4 = (bf16[288,1536]{1,0:T(8,128)(2,1)S(1)}, bf16[288,1536]{1,0:T(8,128)(2,1)}, u32[]{:S(2)}) copy-start(bf16[288,1536]{1,0:T(8,128)(2,1)} %get-tuple-element.77.refs_4_) | copy-start | bytes 2654212
  17.7 6.9 %copy-start.6 = (bf16[512,448]{1,0:T(8,128)(2,1)S(1)}, bf16[512,448]{1,0:T(8,128)(2,1)}, u32[]{:S(2)}) copy-start(bf16[512,448]{1,0:T(8,128)(2,1)} %get-tuple-element.76.refs_3_) | copy-start | bytes 1376260
  17.7 7.0 %copy-start.13 = (f32[96,96]{1,0:T(8,128)S(1)}, f32[96,96]{1,0:T(8,128)}, u32[]{:S(2)}) copy-start(f32[96,96]{1,0:T(8,128)} %get-tuple-element.79.refs_6_) | copy-start | bytes 110596
  17.7 7.0 %copy-start.14 = (f32[96,8]{1,0:T(8,128)S(1)}, f32[96,8]{1,0:T(8,128)}, u32[]{:S(2)}) copy-start(f32[96,8]{1,0:T(8,128)} %get-tuple-element.78.refs_5_) | copy-start | bytes 9220
  30.5 5.4 %collective-permute-start.1 = (bf16[192,384]{1,0:T(8,128)(2,1)S(1)}, bf16[192,384]{1,0:T(8,128)(2,1)S(1)}, u32[]{:S(2)}, u32[]{:S(2)}) collective-permute-start(bf16[192,384]{1,0:T(8,128)(2,1)S(1)} %get-tuple-element.85.refs_1_.mid_ref), channel_id=1, source_target_pairs={{8,0},{16,8},{24,16},{32,24},{40,32},{48,40},{56,48},{64,56},{72,6... | collective-permute-start | bytes 442376 | tf_op jit(solution)/shard_map/ppermute | solution.py:660
  31.4 4.5 %collective-permute-start = (bf16[192,384]{1,0:T(8,128)(2,1)S(1)}, bf16[192,384]{1,0:T(8,128)(2,1)S(1)}, u32[]{:S(2)}, u32[]{:S(2)}) collective-permute-start(bf16[192,384]{1,0:T(8,128)(2,1)S(1)} %get-tuple-element.85.refs_1_.mid_ref), channel_id=1, source_target_pairs={{0,8},{8,16},{16,24},{24,32},{32,40},{40,48},{48,56},{56,64},{64,7... | collective-permute-start | bytes 442376 | tf_op jit(solution)/shard_map/ppermute | solution.py:659
  32.3 9.6 %collective-permute-start.3 = (bf16[384,384]{1,0:T(8,128)(2,1)S(1)}, bf16[384,384]{1,0:T(8,128)(2,1)S(1)}, u32[]{:S(2)}, u32[]{:S(2)}) collective-permute-start(bf16[384,384]{1,0:T(8,128)(2,1)S(1)} %get-tuple-element.81.grad_ref.mid_ref), channel_id=1, source_target_pairs={{8,0},{16,8},{24,16},{32,24},{40,32},{48,40},{56,48},{64,56},{72,6... | collective-permute-start | bytes 884744 | tf_op jit(solution)/shard_map/ppermute | solution.py:662
  32.3 9.6 %collective-permute-start.2 = (bf16[384,384]{1,0:T(8,128)(2,1)S(1)}, bf16[384,384]{1,0:T(8,128)(2,1)S(1)}, u32[]{:S(2)}, u32[]{:S(2)}) collective-permute-start(bf16[384,384]{1,0:T(8,128)(2,1)S(1)} %get-tuple-element.81.grad_ref.mid_ref), channel_id=1, source_target_pairs={{0,8},{8,16},{16,24},{24,32},{32,40},{40,48},{48,56},{56,64},{64,7... | collective-permute-start | bytes 884744 | tf_op jit(solution)/shard_map/ppermute | solution.py:661
  34.1 1.8 %copy-start.3 = (bf16[288,1536]{1,0:T(8,128)(2,1)S(1)}, bf16[288,1536]{1,0:T(8,128)(2,1)}, u32[]{:S(2)}) copy-start(bf16[288,1536]{1,0:T(8,128)(2,1)} %get-tuple-element.87.refs_4_) | copy-start | bytes 2654212
  34.1 1.8 %copy-start.5 = (bf16[512,448]{1,0:T(8,128)(2,1)S(1)}, bf16[512,448]{1,0:T(8,128)(2,1)}, u32[]{:S(2)}) copy-start(bf16[512,448]{1,0:T(8,128)(2,1)} %get-tuple-element.86.refs_3_) | copy-start | bytes 1376260
  34.1 1.8 %copy-start.11 = (f32[96,96]{1,0:T(8,128)S(1)}, f32[96,96]{1,0:T(8,128)}, u32[]{:S(2)}) copy-start(f32[96,96]{1,0:T(8,128)} %get-tuple-element.89.refs_6_) | copy-start | bytes 110596
  34.2 1.8 %copy-start.12 = (f32[96,8]{1,0:T(8,128)S(1)}, f32[96,8]{1,0:T(8,128)}, u32[]{:S(2)}) copy-start(f32[96,8]{1,0:T(8,128)} %get-tuple-element.88.refs_5_) | copy-start | bytes 9220
  36.0 6.0 %copy-start.2 = (bf16[512,864]{1,0:T(8,128)(2,1)S(1)}, bf16[512,864]{1,0:T(8,128)(2,1)}, u32[]{:S(2)}) copy-start(bf16[512,864]{1,0:T(8,128)(2,1)} %get-tuple-element.93.w2t_ref) | copy-start | bytes 2654212
  36.0 5.9 %copy-start.8 = (bf16[144,1536]{1,0:T(8,128)(2,1)S(1)}, bf16[144,1536]{1,0:T(8,128)(2,1)}, u32[]{:S(2)}) copy-start(bf16[144,1536]{1,0:T(8,128)(2,1)} %get-tuple-element.95.w1k_ref) | copy-start | bytes 1327108
  41.9 5.0 %copy-start = (f32[2,96,96]{2,1,0:T(8,128)S(1)}, f32[2,96,96]{2,1,0:T(8,128)}, u32[]{:S(2)}) copy-start(f32[2,96,96]{2,1,0:T(8,128)} %refs_5_.3) | copy-start | bytes 221188
  42.0 5.0 %copy-start.10 = (f32[96,96]{1,0:T(8,128)S(1)}, f32[96,96]{1,0:T(8,128)}, u32[]{:S(2)}) copy-start(f32[96,96]{1,0:T(8,128)} %get-tuple-element.99.refs_3_) | copy-start | bytes 110596
  48.3 10.4 %collective-permute-start.5 = (bf16[384,384]{1,0:T(8,128)(2,1)S(1)}, bf16[384,384]{1,0:T(8,128)(2,1)S(1)}, u32[]{:S(2)}, u32[]{:S(2)}) collective-permute-start(bf16[384,384]{1,0:T(8,128)(2,1)S(1)} %get-tuple-element.102.grad_ref.mid_ref), channel_id=1, source_target_pairs={{8,0},{16,8},{24,16},{32,24},{40,32},{48,40},{56,48},{64,56},{72,6... | collective-permute-start | bytes 884744 | tf_op jit(solution)/shard_map/ppermute | solution.py:674
  51.9 6.8 %collective-permute-start.4 = (bf16[384,384]{1,0:T(8,128)(2,1)S(1)}, bf16[384,384]{1,0:T(8,128)(2,1)S(1)}, u32[]{:S(2)}, u32[]{:S(2)}) collective-permute-start(bf16[384,384]{1,0:T(8,128)(2,1)S(1)} %get-tuple-element.102.grad_ref.mid_ref), channel_id=1, source_target_pairs={{0,8},{8,16},{16,24},{24,32},{32,40},{40,48},{48,56},{56,64},{64,7... | collective-permute-start | bytes 884744 | tf_op jit(solution)/shard_map/ppermute | solution.py:673
  51.9 19.0 %collective-permute-start.10 = (f32[3,144,512]{2,1,0:T(8,128)S(1)}, f32[3,144,512]{2,1,0:T(8,128)S(1)}, u32[]{:S(2)}, u32[]{:S(2)}) collective-permute-start(f32[3,144,512]{2,1,0:T(8,128)S(1)} %get-tuple-element.130), channel_id=1, source_target_pairs={{0,8},{8,0},{1,9},{9,1},{2,10},{10,2},{3,11},{11,3},{4,12},{12,4},... | collective-permute-start | bytes 2654216 | tf_op jit(solution)/shard_map/ppermute | solution.py:668
  54.9 3.8 %copy-start.1 = (bf16[512,864]{1,0:T(8,128)(2,1)S(1)}, bf16[512,864]{1,0:T(8,128)(2,1)}, u32[]{:S(2)}) copy-start(bf16[512,864]{1,0:T(8,128)(2,1)} %get-tuple-element.111.w2t_ref) | copy-start | bytes 2654212
  54.9 3.8 %copy-start.7 = (bf16[144,1536]{1,0:T(8,128)(2,1)S(1)}, bf16[144,1536]{1,0:T(8,128)(2,1)}, u32[]{:S(2)}) copy-start(bf16[144,1536]{1,0:T(8,128)(2,1)} %get-tuple-element.113.w1k_ref) | copy-start | bytes 1327108
  56.6 14.2 %collective-permute-start.9 = (f32[224,512]{1,0:T(8,128)S(1)}, f32[224,512]{1,0:T(8,128)S(1)}, u32[]{:S(2)}, u32[]{:S(2)}) collective-permute-start(f32[224,512]{1,0:T(8,128)S(1)} %get-tuple-element.129), channel_id=1, source_target_pairs={{0,8},{8,0},{1,9},{9,1},{2,10},{10,2},{3,11},{11,3},{4,12},{12,4},... | collective-permute-start | bytes 1376264 | tf_op jit(solution)/shard_map/ppermute | solution.py:677
  58.1 12.7 %collective-permute-start.7 = (f32[3,144,512]{2,1,0:T(8,128)S(1)}, f32[3,144,512]{2,1,0:T(8,128)S(1)}, u32[]{:S(2)}, u32[]{:S(2)}) collective-permute-start(f32[3,144,512]{2,1,0:T(8,128)S(1)} %get-tuple-element.126), channel_id=1, source_target_pairs={{0,8},{8,0},{1,9},{9,1},{2,10},{10,2},{3,11},{11,3},{4,12},{12,4},... | collective-permute-start | bytes 2654216 | tf_op jit(solution)/shard_map/ppermute | solution.py:681
  63.5 4.7 %copy-start.9 = (f32[96,96]{1,0:T(8,128)S(1)}, f32[96,96]{1,0:T(8,128)}, u32[]{:S(2)}) copy-start(f32[96,96]{1,0:T(8,128)} %get-tuple-element.121.refs_3_) | copy-start | bytes 110596
  65.1 5.8 %collective-permute-start.6 = (f32[224,512]{1,0:T(8,128)S(1)}, f32[224,512]{1,0:T(8,128)S(1)}, u32[]{:S(2)}, u32[]{:S(2)}) collective-permute-start(f32[224,512]{1,0:T(8,128)S(1)} %get-tuple-element.125), channel_id=1, source_target_pairs={{0,8},{8,0},{1,9},{9,1},{2,10},{10,2},{3,11},{11,3},{4,12},{12,4},... | collective-permute-start | bytes 1376264 | tf_op jit(solution)/shard_map/ppermute | solution.py:683
  68.1 1.5 %collective-permute-start.11 = (f32[48,256]{1,0:T(8,128)S(1)}, f32[48,256]{1,0:T(8,128)S(1)}, u32[]{:S(2)}, u32[]{:S(2)}) collective-permute-start(f32[48,256]{1,0:T(8,128)S(1)} %get-tuple-element.131), channel_id=1, source_target_pairs={{0,8},{8,0},{1,9},{9,1},{2,10},{10,2},{3,11},{11,3},{4,12},{12,4},... | collective-permute-start | bytes 147464 | tf_op jit(solution)/shard_map/ppermute | solution.py:675
  69.6 1.3 collective-permute-start.8
  72.2 30.2 %all-to-all-start.1 = ((bf16[64,88,128]{2,1,0:T(8,128)(2,1)}), bf16[64,88,128]{2,1,0:T(8,128)(2,1)S(1)}, u32[]{:S(2)}, u32[]{:S(2)}) async-start(bf16[64,88,128]{2,1,0:T(8,128)(2,1)} %merge.1), calls=%async_computation.1 | async-start | bytes 2883584 | tf_op jit(solution)/shard_map/all_to_all | solution.py:695
  127.3 6.9 %collective-permute-start.12 = (bf16[64,88,128]{2,1,0:T(8,128)(2,1)S(1)}, bf16[64,88,128]{2,1,0:T(8,128)(2,1)S(1)}, u32[]{:S(2)}, u32[]{:S(2)}) collective-permute-start(bf16[64,88,128]{2,1,0:T(8,128)(2,1)S(1)} %all_to_all.15.mine_ref), channel_id=1, source_target_pairs={{0,8},{8,0},{1,9},{9,1},{2,10},{10,2},{3,11},{11,3},{4,12},{12,4},... | collective-permute-start | bytes 4325384 | tf_op jit(solution)/shard_map/ppermute | solution.py:700
where the time goes:
time: 138 us
  Pallas kernels  48 us (35%)
  starting transfers between devices  32.2 us (23%)
  waiting for transfers between devices  30.5 us (22%)
  blocking collectives  24.6 us (18%)
    pallas_call x18, Pallas kernels, call(): pl.pallas_call(body, out_shape=outs, in_specs=[pl.BlockSpec(memory_space=...  48 us
    all_to_all x1, blocking collectives, local(): mine = lax.all_to_all(spread, CHIPS, 0, 0, tiled=True)  24.6 us
    all_to_all x1, waiting for transfers between devices, local(): shares = lax.all_to_all(packed, CHIPS, 0, 0, tiled=True)  20.2 us
    all_to_all x1, starting transfers between devices, local(): shares = lax.all_to_all(packed, CHIPS, 0, 0, tiled=True)  8.54 us
    all_to_all x1, starting transfers between devices, local(): recv = lax.all_to_all(block, LAT, 0, 0, tiled=True)  6.91 us
    all_to_all x1, waiting for transfers between devices, local(): recv = lax.all_to_all(block, LAT, 0, 0, tiled=True)  6.17 us
    ppermute x1, starting transfers between devices, local(): other = lax.ppermute(mine, 'c', swap)  4.02 us
    ppermute x1, starting transfers between devices, local(): bottom0 = lax.ppermute(grad0, LAT, back)  3.62 us
  transfers between devices with their start and end apart: 15, of which 6 were waited for; matrix products, arithmetic and copies ran while one was open for 1% of the time, Pallas kernels for 20%

commit v1 on v0

--- a/solution.py
+++ b/solution.py
@@ -62,15 +62,13 @@
     return jax.ShapeDtypeStruct(shape, dtype)
 
 
-def call(body, outs, ins, scratch=(), smem=(), hbm=(), flops=0, name=None, limit=16):
+def call(body, outs, ins, scratch=(), smem=(), flops=0, name=None, limit=16):
     moved = sum(x.size * x.dtype.itemsize for x in list(ins) + list(outs))
     return pl.pallas_call(
         body,
         out_shape=outs,
         in_specs=[
-            pl.BlockSpec(
-                memory_space=pltpu.SMEM if i in smem else pltpu.HBM if i in hbm else pltpu.VMEM
-            )
+            pl.BlockSpec(memory_space=pltpu.SMEM if i in smem else pltpu.VMEM)
             for i in range(len(ins))
         ],
         out_specs=[pl.BlockSpec(memory_space=pltpu.VMEM) for _ in outs],
@@ -82,21 +80,19 @@
 
 
 def payload_kernel(on_ref, grad_ref, out_ref):
-    bands, width = on_ref.shape[2], 2 * CH
+    width = on_ref.shape[2]
     blank = jnp.zeros(on_ref.shape[1:], BF)
     for s in range(on_ref.shape[0]):
         on = on_ref[s]
         hi = on.astype(BF)
         grad = grad_ref[s]
-        ghi = grad.astype(BF)
         out_ref[s, :, :width] = hi
         out_ref[s, :, width : 2 * width] = (on - hi.astype(F32)).astype(BF)
         if s + 1 < on_ref.shape[0]:
             out_ref[s + 1, :, 2 * width : 3 * width] = hi
         if s > 0:
             out_ref[s - 1, :, 3 * width : 4 * width] = hi
-        out_ref[s, :, 4 * width : 5 * width] = ghi
-        out_ref[s, :, 5 * width : 6 * width] = (grad - ghi.astype(F32)).astype(BF)
+        out_ref[s, :, 4 * width :] = grad.astype(BF)
     out_ref[0, :, 2 * width : 3 * width] = blank
     out_ref[on_ref.shape[0] - 1, :, 3 * width : 4 * width] = blank
 
@@ -104,7 +100,7 @@
 def payload(on, grad):
     bands, width, channels = on.shape
     return call(
-        payload_kernel, [sds((bands, width, 6 * channels), BF)], [on, grad], name="payload", limit=56
+        payload_kernel, [sds((bands, width, 5 * channels), BF)], [on, grad], name="payload", limit=56
     )[0]
 
 
@@ -197,7 +193,7 @@
     pair = stage[:, 2 * width : 4 * width].astype(BF)
     above_ref[...] = mm_nt(first, pair).astype(BF)
     below_ref[...] = mm_nt(second, pair).astype(BF)
-    grad = mm_nt(both, stage[:, 4 * width :].astype(BF))
+    grad = mm_nt(pick, stage[:, 4 * width :].astype(BF))
     for k in range(4):
         ya_ref[:, k * COLS : (k + 1) * COLS] = kept[k * HALF : (k + 1) * HALF]
         ga_ref[:, k * COLS : (k + 1) * COLS] = grad[k * HALF : (k + 1) * HALF]
@@ -269,22 +265,13 @@
 
 
 def forward_kernel(with_grad, flags_ref, *refs):
-    above_ref, mid_ref, below_ref, *weights, ya_ref, yb_ref = refs[:9]
-    columns, pre, outs, *held, sems = refs[-8:]
-    w1t_ref, w2k_ref, b2_ref, inv_ref = held
-    copies = [
-        pltpu.make_async_copy(source, target, sems.at[i])
-        for i, (source, target) in enumerate(zip(weights, held))
-    ]
-    for copy in copies:
-        copy.start()
+    above_ref, mid_ref, below_ref, w1t_ref, w2k_ref, b2_ref, inv_ref, ya_ref, yb_ref = refs[:9]
+    columns, pre, outs = refs[-3:]
     if with_grad:
-        x_ref, rows, slope_ref, next_ref, grad_ref, moved_ref = refs[9:-8]
+        x_ref, rows, slope_ref, next_ref, grad_ref, moved_ref = refs[9:-3]
     else:
-        x_ref, rows, slope_ref, scale_ref = refs[9:-8]
+        x_ref, rows, slope_ref, scale_ref = refs[9:-3]
     fill_input_columns(flags_ref, above_ref, mid_ref, below_ref, columns, -1, 4)
-    for copy in copies:
-        copy.wait()
     for h in range(4):
         pre[h % 2] = mm(w1t_ref[...], columns[:, h * ROW : (h + 1) * ROW])
         inside = flags_ref[0] if h == 0 else flags_ref[1] if h == 3 else None
@@ -346,14 +333,8 @@
             pltpu.VMEM((IN_ROWS, 4 * ROW), BF),
             pltpu.VMEM((2, HID, ROW), F32),
             pltpu.VMEM((CH, CELLS), F32),
-            pltpu.VMEM((HID, IN_ROWS), BF),
-            pltpu.VMEM((3 * CH, 3 * HID), BF),
-            pltpu.VMEM((CH, 8), F32),
-            pltpu.VMEM((CH, CH), F32),
-            pltpu.SemaphoreType.DMA((4,)),
         ],
         smem=(0,),
-        hbm=(4, 5, 6, 7),
         limit=24,
         flops=4 * 10**9,
         name="forward",
@@ -457,13 +438,13 @@
     )
 
 
-def close_kernel(next_step, flow, core_ref, *refs):
+def close_kernel(next_step, flow, *refs):
     in_ref, ga_ref, moved_ref, lut_ref, x_ref, mix_ref, bias_ref = refs[:7]
-    whole, small = refs[-2:]
+    whole = refs[-1]
     if next_step:
-        scale_ref, gx_ref, keep_ref, give_ref, grad_ref, nmoved_ref = refs[7:-2]
+        scale_ref, gx_ref, small, grad_ref, nmoved_ref = refs[7:-1]
     else:
-        gx_ref, keep_ref, give_ref = refs[7:-2]
+        gx_ref, small = refs[7:-1]
     for k in range(4):
         lane = k * COLS
         whole[:HALF, lane : lane + COLS] = (
@@ -492,13 +473,11 @@
     small[:, :CH] = jnp.where(row > col, by_upper, jnp.where(row < col, by_lower, 0.0))
     small[:, CH:] = jnp.zeros((CH, 2 * 128 - CH), F32)
     small[:8, 128 : 128 + CH] = bias_ref[...]
-    for ref, core in ((keep_ref, core_ref[0]), (give_ref, 1 - core_ref[0])):
-        ref[...] = small[pl.ds(pl.multiple_of(core * HALF, 8), HALF), :]
-
-
-def close(core, gin, ga, moved, lut, x, mix, flow, bias, scale=None):
-    outs = [sds((CH, CELLS), F32), sds((HALF, 256), F32), sds((HALF, 256), F32)]
-    ins = [core, gin, ga, moved, lut, x, mix, bias]
+
+
+def close(gin, ga, moved, lut, x, mix, flow, bias, scale=None):
+    outs = [sds((CH, CELLS), F32), sds((CH, 256), F32)]
+    ins = [gin, ga, moved, lut, x, mix, bias]
     if scale is not None:
         outs += [sds((4 * CH, COLS), BF), sds((HALF, CELLS), F32)]
         ins += [scale]
@@ -506,8 +485,7 @@
         functools.partial(close_kernel, scale is not None, flow),
         outs,
         ins,
-        scratch=[pltpu.VMEM((CH, CELLS), F32), pltpu.VMEM((CH, 256), F32)],
-        smem=(0,),
+        scratch=[pltpu.VMEM((CH, CELLS), F32)],
         flops=10**9,
         name="close",
     )
@@ -533,7 +511,6 @@
     return call(weave_kernel, [sds((1, CH, 2, ROW), F32)], [x], name="weave")[0]
 
 
-PARTS = ((0, IN_HALF), (224, TAP_HALF), (368, TAP_HALF), (512, TAP_HALF), (656, HALF))
 FLOW_ROWS = 704
 GROUP = 88
 
@@ -541,16 +518,15 @@
 def merge_kernel(*refs):
     out_ref, total = refs[-2:]
     for k in range(2):
-        own_in, own_out, own_small, got_in, got_out, got_small = refs[6 * k : 6 * k + 6]
+        own_in, own_out, got_in, got_out, small = refs[5 * k : 5 * k + 5]
         at = k * FLOW_ROWS
         total[at : at + IN_HALF] = own_in[...] + got_in[...]
         for a in range(3):
             start = at + IN_HALF + a * TAP_HALF
             total[start : start + TAP_HALF] = own_out[a] + got_out[a]
-        small = own_small[...] + got_small[...]
         start = at + FLOW_ROWS - HALF
-        total[start : start + HALF, :256] = small
-        total[start : start + HALF, 256:] = small - small.astype(BF).astype(F32)
+        total[start : start + HALF, :256] = small[:HALF]
+        total[start : start + HALF, 256:] = small[HALF:]
     for g in range(2 * FLOW_ROWS // GROUP):
         for lane in range(4):
             out_ref[4 * g + lane] = total[
@@ -558,12 +534,12 @@
             ].astype(BF)
 
 
-def merge(own0, got0, own1, got1):
+def merge(first, second):
     shares = 2 * FLOW_ROWS // GROUP * 4
     return call(
         merge_kernel,
         [sds((shares, GROUP, 128), BF)],
-        [*own0, *got0, *own1, *got1],
+        [*first, *second],
         scratch=[pltpu.VMEM((2 * FLOW_ROWS, HID), F32)],
         name="merge",
     )[0]
@@ -607,11 +583,10 @@
             wout_ref[k, 3 * a + 1, HALF:] = rows[1, start : start + HALF]
             wout_ref[k, 3 * a] = rows[1, start + HALF : start + TAP_HALF]
         start = at + FLOW_ROWS - HALF
-        for half in range(2):
-            block = rows[half, start : start + HALF]
-            mix_ref[k, half * HALF : (half + 1) * HALF] = block[:, :CH] + block[:, 256 : 256 + CH]
-        block = rows[0, start : start + 8]
-        bout_ref[k] = block[:, 128 : 128 + CH] + block[:, 384 : 384 + CH]
+        block = rows[0, start : start + HALF] + rows[1, start : start + HALF]
+        mix_ref[k, :HALF] = block[:, :CH]
+        mix_ref[k, HALF:] = block[:, 256 : 256 + CH]
+        bout_ref[k : k + 1, :] = block[:1, 128 : 128 + CH]
 
 
 def unpack(core, mine, other):
@@ -622,7 +597,7 @@
             sds((2, 9, CH, HID), F32),
             sds((2, CH, CH), F32),
             sds((2, HID), F32),
-            sds((2, 8, CH), F32),
+            sds((2, CH), F32),
         ],
         [core, mine, other],
         scratch=[pltpu.VMEM((2, 2 * FLOW_ROWS, HID), F32)],
@@ -667,12 +642,11 @@
     )
     got_out1 = lax.ppermute(give_out1, "c", swap)
     gpre1, in1 = backward(after(flags, x0), top1, grad1, bottom1, w2t[1], slope1, w1k[1])
-    gx1, keep_small1, give_small1, grad0, moved0 = close(
-        core, in1, ga, moved1, lut[1], x1, mix_factors, 1, bias1, scale0
+    gx1, small1, grad0, moved0 = close(
+        in1, ga, moved1, lut[1], x1, mix_factors, 1, bias1, scale0
     )
     top0 = lax.ppermute(grad0, LAT, forth)
     bottom0 = lax.ppermute(grad0, LAT, back)
-    got_small1 = lax.ppermute(give_small1, "c", swap)
     keep_in1, give_in1 = in_weight(after(core, grad0), flags, above, mid, below, gpre1)
     got_in1 = lax.ppermute(give_in1, "c", swap)
     keep_out0, give_out0, bias0 = out_weight(after(core, keep_in1), grad0, rows0)
@@ -681,16 +655,13 @@
     got_out0 = lax.ppermute(give_out0, "c", swap)
     keep_in0, give_in0 = in_weight(after(core, in0), flags, above0, next_mid, below0, gpre0)
     got_in0 = lax.ppermute(give_in0, "c", swap)
-    gx0, keep_small0, give_small0 = close(
-        after(core, keep_in0), in0, gx1, moved0, lut[0], x0, mix_factors, 0, bias0
-    )
-    got_small0 = lax.ppermute(give_small0, "c", swap)
+    gx0, small0 = close(
+        after(in0, keep_in0), gx1, moved0, lut[0], x0, mix_factors, 0, bias0
+    )
 
     packed = merge(
-        (keep_in0, keep_out0, keep_small0),
-        (got_in0, got_out0, got_small0),
-        (keep_in1, keep_out1, keep_small1),
-        (got_in1, got_out1, got_small1),
+        (keep_in0, keep_out0, got_in0, got_out0, small0),
+        (keep_in1, keep_out1, got_in1, got_out1, small1),
     )
     shares = lax.all_to_all(packed, CHIPS, 0, 0, tiled=True)
     input_grad = weave(after(gx0, packed))
@@ -706,7 +677,7 @@
         in_grad.reshape(2, 9, HALF, HID),
         in_bias_grad,
         out_grad,
-        out_bias_grad[:, 0],
+        out_bias_grad,
     )
 
 

time: 138 us -> 134 us (0.971)
  Pallas kernels: 48 us -> 46.6 us
  transfers between devices with their start and end apart: 15 -> 13, of which waited for: 6 -> 5; matrix products, arithmetic and copies ran while one was open for 1% -> 1% of each run, Pallas kernels for 20% -> 21%
where the time goes in v1:
time: 134 us
  Pallas kernels  46.6 us (35%)
  starting transfers between devices  31.2 us (23%)
  waiting for transfers between devices  29.2 us (22%)
  blocking collectives  24.6 us (18%)
    pallas_call x18, Pallas kernels, call(): pl.pallas_call(body, out_shape=outs, in_specs=[pl.BlockSpec(memory_space=...  46.6 us
    all_to_all x1, blocking collectives, local(): mine = lax.all_to_all(spread, CHIPS, 0, 0, tiled=True)  24.6 us
    all_to_all x1, waiting for transfers between devices, local(): shares = lax.all_to_all(packed, CHIPS, 0, 0, tiled=True)  20.2 us
    all_to_all x1, starting transfers between devices, local(): shares = lax.all_to_all(packed, CHIPS, 0, 0, tiled=True)  8.58 us
    all_to_all x1, starting transfers between devices, local(): recv = lax.all_to_all(block, LAT, 0, 0, tiled=True)  6.91 us
    all_to_all x1, waiting for transfers between devices, local(): recv = lax.all_to_all(block, LAT, 0, 0, tiled=True)  5.1 us
    ppermute x1, starting transfers between devices, local(): other = lax.ppermute(mine, 'c', swap)  4.04 us
    ppermute x1, starting transfers between devices, local(): bottom0 = lax.ppermute(grad0, LAT, back)  3.1 us
  transfers between devices with their start and end apart: 13, of which 5 were waited for; matrix products, arithmetic and copies ran while one was open for 1% of the time, Pallas kernels for 21%

profile of v1, /device:TPU:1, one launch (start us, length us, event | category | flops | bytes accessed | tf_op | source)
XLA Modules:
  0.0 133.6 jit_solution(2645886189026515283)
XLA Ops:
  0.6 2.2 %payload.1 = bf16[16,24,960]{2,1,0:T(8,128)(2,1)} custom-call(f32[16,24,192]{2,1,0:T(8,128)} %bitcast.10, f32[16,24,192]{2,1,0:T(8,128)} %bitcast.11), custom_call_target="tpu_custom_call" | custom-call | bytes 1327104 | tf_op jit(solution)/shard_map/payload/pallas_call | solution.py:67
  2.9 6.9 %all-to-all-start = ((bf16[16,24,960]{2,1,0:T(8,128)(2,1)}), bf16[16,24,960]{2,1,0:T(8,128)(2,1)S(1)}, u32[]{:S(2)}, u32[]{:S(2)}) async-start(bf16[16,24,960]{2,1,0:T(8,128)(2,1)} %payload.1), calls=%async_computation | async-start | bytes 1572864 | tf_op jit(solution)/shard_map/all_to_all | solution.py:625
  9.8 0.7 reduce
  10.6 7.0 %prep.1 = (f32[96,96]{1,0:T(8,128)}, f32[96,96]{1,0:T(8,128)}, bf16[512,448]{1,0:T(8,128)(2,1)}, bf16[512,864]{1,0:T(8,128)(2,1)}, bf16[288,1536]{1,0:T(8,128)(2...) custom-call(f32[2,96,96]{2,1,0:T(8,128)} %refs_5_.3, ...), custom_call_target="tpu_custom_call" | custom-call | bytes 8227584 | tf_op jit(solution)/shard_map/prep/pallas_call | solution.py:67
  17.7 5.1 %all-to-all-done.recv_ref = bf16[16,24,960]{2,1,0:T(8,128)(2,1)S(1)} async-done(((bf16[16,24,960]{2,1,0:T(8,128)(2,1)}), bf16[16,24,960]{2,1,0:T(8,128)(2,1)S(1)}, u32[]{:S(2)}, u32[]{:S(2)}) %all-to-all-start) | async-done | bytes 737312 | tf_op jit(solution)/shard_map/all_to_all | solution.py:625
  22.8 0.7 turn.1
  23.5 5.2 %forward.2 = (f32[96,1536]{1,0:T(8,128)S(1)}, bf16[2048,768]{1,0:T(8,128)(2,1)S(1)}, f32[2048,768]{1,0:T(8,128)S(1)}, bf16[192,384]{1,0:T(8,128)(2,1)S(1)}, bf16...) custom-call(f32[2]{0:T(128)S(1)} %add_convert_fusion.flags_ref, ...), custom_call_target="tpu_custom_call" | custom-call | flops 4000000000 | bytes 13179912 | tf_op jit(solution)/shard_map/forward/pallas_call | solution.py:67
  28.7 0.9 collective-permute-start.1
  29.7 0.9 collective-permute-start
  30.5 1.7 %collective-permute-start.2 = (bf16[384,384]{1,0:T(8,128)(2,1)S(1)}, bf16[384,384]{1,0:T(8,128)(2,1)S(1)}, u32[]{:S(2)}, u32[]{:S(2)}) collective-permute-start(bf16[384,384]{1,0:T(8,128)(2,1)S(1)} %get-tuple-element.79.grad_ref.mid_ref), channel_id=1, source_target_pairs={{0,8},{8,16},{16,24},{24,32},{32,40},{40,48},{48,56},{56,64},{64,7... | collective-permute-start | bytes 884744 | tf_op jit(solution)/shard_map/ppermute | solution.py:636
  32.4 1.7 %out_weight.2 = (f32[3,144,512]{2,1,0:T(8,128)S(1)}, f32[3,144,512]{2,1,0:T(8,128)S(1)}, f32[8,96]{1,0:T(8,128)S(1)}) custom-call(s32[1]{0:T(128)} %bitcast.2.core_ref, bf16[384,384]{1,0:T(8,128)(2,1)S(1)} %get-tuple-element.79.grad_ref.mid_ref, bf16[2048,768]{1,0:T(8,128)(2,1)S(1)} %get-tuple-element.80.rows_ref), custom_call_target="tpu_custom_call" | custom-call | flops 2000000000 | bytes 5213188 | tf_op jit(solution)/shard_map/out_weight/pallas_call | solution.py:67
  34.2 5.1 %forward.3 = (f32[96,1536]{1,0:T(8,128)S(1)}, bf16[2048,768]{1,0:T(8,128)(2,1)S(1)}, f32[2048,768]{1,0:T(8,128)S(1)}, f32[48,1536]{1,0:T(8,128)S(1)}) custom-call(f32[2]{0:T(128)S(1)} %add_convert_fusion.flags_ref, bf16[192,384]{1,0:T(8,128)(2,1)S(1)} %collective-permute-done.refs_0_.above_ref, bf16[192,384]{1,0:T(8,128)(2,1)S(1)} %get-tuple-element.83.refs_1_.mid_ref, ...), custom_call_target="tpu_custom_call" | custom-call | flops 4000000000 | bytes 12737544 | tf_op jit(solution)/shard_map/forward/pallas_call | solution.py:67
  39.3 0.8 collective-permute-done.3.below_ref
  40.2 5.0 %backward.2 = (bf16[2048,768]{1,0:T(8,128)(2,1)S(1)}, f32[192,384]{1,0:T(8,128)S(1)}) custom-call(f32[2]{0:T(128)S(1)} %add_convert_fusion.flags_ref, bf16[384,384]{1,0:T(8,128)(2,1)S(1)} %collective-permute-done.2.above_ref, bf16[384,384]{1,0:T(8,128)(2,1)S(1)} %get-tuple-element.79.grad_ref.mid_ref, bf16[384,384]{1,0:T(8,128)(2,1)S(1)} %collective-permute-done.3.below_ref, ...), custom_call_target="tpu_custom_call" | custom-call | flops 6000000000 | bytes 11943944 | tf_op jit(solution)/shard_map/backward/pallas_call | solution.py:67
  45.2 1.3 close.2
  46.5 3.1 %collective-permute-start.5 = (bf16[384,384]{1,0:T(8,128)(2,1)S(1)}, bf16[384,384]{1,0:T(8,128)(2,1)S(1)}, u32[]{:S(2)}, u32[]{:S(2)}) collective-permute-start(bf16[384,384]{1,0:T(8,128)(2,1)S(1)} %get-tuple-element.100.grad_ref.mid_ref), channel_id=1, source_target_pairs={{8,0},{16,8},{24,16},{32,24},{40,32},{48,40},{56,48},{64,56},{72,6... | collective-permute-start | bytes 884744 | tf_op jit(solution)/shard_map/ppermute | solution.py:649
  49.6 1.4 %collective-permute-start.9 = (f32[3,144,512]{2,1,0:T(8,128)S(1)}, f32[3,144,512]{2,1,0:T(8,128)S(1)}, u32[]{:S(2)}, u32[]{:S(2)}) collective-permute-start(f32[3,144,512]{2,1,0:T(8,128)S(1)} %get-tuple-element.126), channel_id=1, source_target_pairs={{0,8},{8,0},{1,9},{9,1},{2,10},{10,2},{3,11},{11,3},{4,12},{12,4},... | collective-permute-start | bytes 2654216 | tf_op jit(solution)/shard_map/ppermute | solution.py:643
  51.0 1.5 %in_weight.2 = (f32[224,512]{1,0:T(8,128)S(1)}, f32[224,512]{1,0:T(8,128)S(1)}) custom-call(s32[1]{0:T(128)} %bitcast.2.core_ref, f32[2]{0:T(128)S(1)} %add_convert_fusion.flags_ref, bf16[192,384]{1,0:T(8,128)(2,1)S(1)} %get-tuple-element.71.refs_0_.above_ref, bf16[192,384]{1,0:T(8,128)(2,1)S(1)} %get-tuple-element.72.refs_1_.mid_ref, ...), custom_call_target="tpu_custom_call" | custom-call | flops 1000000000 | bytes 4505612 | tf_op jit(solution)/shard_map/in_weight/pallas_call | solution.py:67
  52.5 1.7 %out_weight.3 = (f32[3,144,512]{2,1,0:T(8,128)S(1)}, f32[3,144,512]{2,1,0:T(8,128)S(1)}, f32[8,96]{1,0:T(8,128)S(1)}) custom-call(s32[1]{0:T(128)} %bitcast.2.core_ref, bf16[384,384]{1,0:T(8,128)(2,1)S(1)} %get-tuple-element.100.grad_ref.mid_ref, bf16[2048,768]{1,0:T(8,128)(2,1)S(1)} %get-tuple-element.105.rows_ref), custom_call_target="tpu_custom_call" | custom-call | flops 2000000000 | bytes 5213188 | tf_op jit(solution)/shard_map/out_weight/pallas_call | solution.py:67
  54.4 1.4 %weave.2 = f32[1,96,2,768]{3,2,1,0:T(2,128)} custom-call(f32[96,1536]{1,0:T(8,128)S(1)} %get-tuple-element.107.x_ref.refs_4_), custom_call_target="tpu_custom_call" | custom-call | bytes 1179648 | tf_op jit(solution)/shard_map/weave/pallas_call | solution.py:67
  56.3 4.9 %backward.3 = (bf16[2048,768]{1,0:T(8,128)(2,1)S(1)}, f32[192,384]{1,0:T(8,128)S(1)}) custom-call(f32[2]{0:T(128)S(1)} %add_convert_fusion.flags_ref, bf16[384,384]{1,0:T(8,128)(2,1)S(1)} %collective-permute-done.4.above_ref, bf16[384,384]{1,0:T(8,128)(2,1)S(1)} %get-tuple-element.100.grad_ref.mid_ref, ...), custom_call_target="tpu_custom_call" | custom-call | flops 6000000000 | bytes 11943944 | tf_op jit(solution)/shard_map/backward/pallas_call | solution.py:67
  61.2 1.5 %in_weight.3 = (f32[224,512]{1,0:T(8,128)S(1)}, f32[224,512]{1,0:T(8,128)S(1)}) custom-call(s32[1]{0:T(128)} %bitcast.2.core_ref, f32[2]{0:T(128)S(1)} %add_convert_fusion.flags_ref, bf16[192,384]{1,0:T(8,128)(2,1)S(1)} %collective-permute-done.refs_0_.above_ref, bf16[192,384]{1,0:T(8,128)(2,1)S(1)} %get-tuple-element.83.refs_1_.mid_ref, ...), custom_call_target="tpu_custom_call" | custom-call | flops 1000000000 | bytes 4505612 | tf_op jit(solution)/shard_map/in_weight/pallas_call | solution.py:67
  62.7 3.0 %collective-permute-start.6 = (f32[224,512]{1,0:T(8,128)S(1)}, f32[224,512]{1,0:T(8,128)S(1)}, u32[]{:S(2)}, u32[]{:S(2)}) collective-permute-start(f32[224,512]{1,0:T(8,128)S(1)} %get-tuple-element.122), channel_id=1, source_target_pairs={{0,8},{8,0},{1,9},{9,1},{2,10},{10,2},{3,11},{11,3},{4,12},{12,4},... | collective-permute-start | bytes 1376264 | tf_op jit(solution)/shard_map/ppermute | solution.py:657
  65.7 1.2 close.3
  67.2 1.4 %merge.1 = bf16[64,88,128]{2,1,0:T(8,128)(2,1)} custom-call(f32[224,512]{1,0:T(8,128)S(1)} %get-tuple-element.115.refs_0_, f32[3,144,512]{2,1,0:T(8,128)S(1)} %get-tuple-element.106.refs_1_, f32[224,512]{1,0:T(8,128)S(1)} %collective-permute-done.6.refs_2_, f32[3,144,512]{2,1,0:T(8,128)S(1)} %collective-permute-done.7.refs_3_, ...), custom_call_target="tpu_custom_call" | custom-call | bytes 7012352 | tf_op jit(solution)/shard_map/merge/pallas_call | solution.py:67
  68.5 8.6 %all-to-all-start.1 = ((bf16[64,88,128]{2,1,0:T(8,128)(2,1)}), bf16[64,88,128]{2,1,0:T(8,128)(2,1)S(1)}, u32[]{:S(2)}, u32[]{:S(2)}) async-start(bf16[64,88,128]{2,1,0:T(8,128)(2,1)} %merge.1), calls=%async_computation.1 | async-start | bytes 2883584 | tf_op jit(solution)/shard_map/all_to_all | solution.py:666
  77.1 1.4 %weave.3 = f32[1,96,2,768]{3,2,1,0:T(2,128)} custom-call(f32[96,1536]{1,0:T(8,128)S(1)} %get-tuple-element.128.x_ref), custom_call_target="tpu_custom_call" | custom-call | bytes 1179648 | tf_op jit(solution)/shard_map/weave/pallas_call | solution.py:67
  78.5 20.2 %all-to-all-done.1.shares_ref = bf16[64,88,128]{2,1,0:T(8,128)(2,1)S(1)} async-done(((bf16[64,88,128]{2,1,0:T(8,128)(2,1)}), bf16[64,88,128]{2,1,0:T(8,128)(2,1)S(1)}, u32[]{:S(2)}, u32[]{:S(2)}) %all-to-all-start.1) | async-done | bytes 1441824 | tf_op jit(solution)/shard_map/all_to_all | solution.py:666
  99.0 24.6 %all_to_all.15.mine_ref = bf16[64,88,128]{2,1,0:T(8,128)(2,1)S(1)} all-to-all(bf16[64,88,128]{2,1,0:T(8,128)(2,1)S(1)} %totals.1), channel_id=1, replica_groups=mesh['y'=4,'xl'=2,'c'=2,'z'=4,'xh'=2] {'y','xl','z','xh'}, dimensions={0} | all-to-all | bytes 2883584 | tf_op jit(solution)/shard_map/all_to_all | solution.py:670
  123.6 4.0 %collective-permute-start.10 = (bf16[64,88,128]{2,1,0:T(8,128)(2,1)S(1)}, bf16[64,88,128]{2,1,0:T(8,128)(2,1)S(1)}, u32[]{:S(2)}, u32[]{:S(2)}) collective-permute-start(bf16[64,88,128]{2,1,0:T(8,128)(2,1)S(1)} %all_to_all.15.mine_ref), channel_id=1, source_target_pairs={{0,8},{8,0},{1,9},{9,1},{2,10},{10,2},{3,11},{11,3},{4,12},{12,4},... | collective-permute-start | bytes 4325384 | tf_op jit(solution)/shard_map/ppermute | solution.py:671
  127.7 2.8 %collective-permute-done.10.other_ref = bf16[64,88,128]{2,1,0:T(8,128)(2,1)S(1)} collective-permute-done((bf16[64,88,128]{2,1,0:T(8,128)(2,1)S(1)}, bf16[64,88,128]{2,1,0:T(8,128)(2,1)S(1)}, u32[]{:S(2)}, u32[]{:S(2)}) %collective-permute-start.10) | collective-permute-done | bytes 1441824 | tf_op jit(solution)/shard_map/ppermute | solution.py:671
  130.5 3.0 %unpack.1 = (f32[2,432,512]{2,1,0:T(8,128)}, f32[2,9,96,512]{3,2,1,0:T(8,128)}, f32[2,96,96]{2,1,0:T(8,128)}, f32[2,512]{1,0:T(2,128)}, f32[2,96]{1,0:T(2,128)}) custom-call(s32[1]{0:T(128)} %bitcast.2.core_ref, bf16[64,88,128]{2,1,0:T(8,128)(2,1)S(1)} %all_to_all.15.mine_ref, bf16[64,88,128]{2,1,0:T(8,128)(2,1)S(1)} %collective-permute-done.10.other_ref), custom_call_target="tpu_custom_call" | custom-call | bytes 8270596 | tf_op jit(solution)/shard_map/unpack/pallas_call | solution.py:67
  (49 shorter events, 1.3 us)
Async XLA Ops:
  0.6 9.1 %copy-start.15 = (f32[1,192,1,384]{3,2,1,0:T(1,128)S(1)}, f32[1,192,1,384]{3,2,1,0:T(1,128)}, u32[]{:S(2)}) copy-start(f32[1,192,1,384]{3,2,1,0:T(1,128)} %param.10) | copy-start | bytes 884740
  2.9 19.9 %all-to-all-start = ((bf16[16,24,960]{2,1,0:T(8,128)(2,1)}), bf16[16,24,960]{2,1,0:T(8,128)(2,1)S(1)}, u32[]{:S(2)}, u32[]{:S(2)}) async-start(bf16[16,24,960]{2,1,0:T(8,128)(2,1)} %payload.1), calls=%async_computation | async-start | bytes 1572864 | tf_op jit(solution)/shard_map/all_to_all | solution.py:625
  17.7 5.8 %copy-start.4 = (bf16[288,1536]{1,0:T(8,128)(2,1)S(1)}, bf16[288,1536]{1,0:T(8,128)(2,1)}, u32[]{:S(2)}) copy-start(bf16[288,1536]{1,0:T(8,128)(2,1)} %get-tuple-element.75.refs_4_) | copy-start | bytes 2654212
  17.7 5.8 %copy-start.6 = (bf16[512,448]{1,0:T(8,128)(2,1)S(1)}, bf16[512,448]{1,0:T(8,128)(2,1)}, u32[]{:S(2)}) copy-start(bf16[512,448]{1,0:T(8,128)(2,1)} %get-tuple-element.74.refs_3_) | copy-start | bytes 1376260
  17.7 5.9 %copy-start.13 = (f32[96,96]{1,0:T(8,128)S(1)}, f32[96,96]{1,0:T(8,128)}, u32[]{:S(2)}) copy-start(f32[96,96]{1,0:T(8,128)} %get-tuple-element.77.refs_6_) | copy-start | bytes 110596
  17.7 5.9 %copy-start.14 = (f32[96,8]{1,0:T(8,128)S(1)}, f32[96,8]{1,0:T(8,128)}, u32[]{:S(2)}) copy-start(f32[96,8]{1,0:T(8,128)} %get-tuple-element.76.refs_5_) | copy-start | bytes 9220
  28.7 5.4 %collective-permute-start.1 = (bf16[192,384]{1,0:T(8,128)(2,1)S(1)}, bf16[192,384]{1,0:T(8,128)(2,1)S(1)}, u32[]{:S(2)}, u32[]{:S(2)}) collective-permute-start(bf16[192,384]{1,0:T(8,128)(2,1)S(1)} %get-tuple-element.83.refs_1_.mid_ref), channel_id=1, source_target_pairs={{8,0},{16,8},{24,16},{32,24},{40,32},{48,40},{56,48},{64,56},{72,6... | collective-permute-start | bytes 442376 | tf_op jit(solution)/shard_map/ppermute | solution.py:635
  29.7 4.5 %collective-permute-start = (bf16[192,384]{1,0:T(8,128)(2,1)S(1)}, bf16[192,384]{1,0:T(8,128)(2,1)S(1)}, u32[]{:S(2)}, u32[]{:S(2)}) collective-permute-start(bf16[192,384]{1,0:T(8,128)(2,1)S(1)} %get-tuple-element.83.refs_1_.mid_ref), channel_id=1, source_target_pairs={{0,8},{8,16},{16,24},{24,32},{32,40},{40,48},{48,56},{56,64},{64,7... | collective-permute-start | bytes 442376 | tf_op jit(solution)/shard_map/ppermute | solution.py:634
  30.5 9.6 %collective-permute-start.3 = (bf16[384,384]{1,0:T(8,128)(2,1)S(1)}, bf16[384,384]{1,0:T(8,128)(2,1)S(1)}, u32[]{:S(2)}, u32[]{:S(2)}) collective-permute-start(bf16[384,384]{1,0:T(8,128)(2,1)S(1)} %get-tuple-element.79.grad_ref.mid_ref), channel_id=1, source_target_pairs={{8,0},{16,8},{24,16},{32,24},{40,32},{48,40},{56,48},{64,56},{72,6... | collective-permute-start | bytes 884744 | tf_op jit(solution)/shard_map/ppermute | solution.py:637
  30.5 9.6 %collective-permute-start.2 = (bf16[384,384]{1,0:T(8,128)(2,1)S(1)}, bf16[384,384]{1,0:T(8,128)(2,1)S(1)}, u32[]{:S(2)}, u32[]{:S(2)}) collective-permute-start(bf16[384,384]{1,0:T(8,128)(2,1)S(1)} %get-tuple-element.79.grad_ref.mid_ref), channel_id=1, source_target_pairs={{0,8},{8,16},{16,24},{24,32},{32,40},{40,48},{48,56},{56,64},{64,7... | collective-permute-start | bytes 884744 | tf_op jit(solution)/shard_map/ppermute | solution.py:636
  32.3 1.8 %copy-start.3 = (bf16[288,1536]{1,0:T(8,128)(2,1)S(1)}, bf16[288,1536]{1,0:T(8,128)(2,1)}, u32[]{:S(2)}) copy-start(bf16[288,1536]{1,0:T(8,128)(2,1)} %get-tuple-element.85.refs_4_) | copy-start | bytes 2654212
  32.3 1.8 %copy-start.5 = (bf16[512,448]{1,0:T(8,128)(2,1)S(1)}, bf16[512,448]{1,0:T(8,128)(2,1)}, u32[]{:S(2)}) copy-start(bf16[512,448]{1,0:T(8,128)(2,1)} %get-tuple-element.84.refs_3_) | copy-start | bytes 1376260
  32.3 1.8 %copy-start.11 = (f32[96,96]{1,0:T(8,128)S(1)}, f32[96,96]{1,0:T(8,128)}, u32[]{:S(2)}) copy-start(f32[96,96]{1,0:T(8,128)} %get-tuple-element.87.refs_6_) | copy-start | bytes 110596
  32.4 1.8 %copy-start.12 = (f32[96,8]{1,0:T(8,128)S(1)}, f32[96,8]{1,0:T(8,128)}, u32[]{:S(2)}) copy-start(f32[96,8]{1,0:T(8,128)} %get-tuple-element.86.refs_5_) | copy-start | bytes 9220
  34.2 6.0 %copy-start.2 = (bf16[512,864]{1,0:T(8,128)(2,1)S(1)}, bf16[512,864]{1,0:T(8,128)(2,1)}, u32[]{:S(2)}) copy-start(bf16[512,864]{1,0:T(8,128)(2,1)} %get-tuple-element.91.w2t_ref) | copy-start | bytes 2654212
  34.2 5.9 %copy-start.8 = (bf16[144,1536]{1,0:T(8,128)(2,1)S(1)}, bf16[144,1536]{1,0:T(8,128)(2,1)}, u32[]{:S(2)}) copy-start(bf16[144,1536]{1,0:T(8,128)(2,1)} %get-tuple-element.93.w1k_ref) | copy-start | bytes 1327108
  40.1 5.0 %copy-start = (f32[2,96,96]{2,1,0:T(8,128)S(1)}, f32[2,96,96]{2,1,0:T(8,128)}, u32[]{:S(2)}) copy-start(f32[2,96,96]{2,1,0:T(8,128)} %refs_5_.3) | copy-start | bytes 221188
  40.2 5.0 %copy-start.10 = (f32[96,96]{1,0:T(8,128)S(1)}, f32[96,96]{1,0:T(8,128)}, u32[]{:S(2)}) copy-start(f32[96,96]{1,0:T(8,128)} %get-tuple-element.97.refs_3_) | copy-start | bytes 110596
  46.5 9.8 %collective-permute-start.5 = (bf16[384,384]{1,0:T(8,128)(2,1)S(1)}, bf16[384,384]{1,0:T(8,128)(2,1)S(1)}, u32[]{:S(2)}, u32[]{:S(2)}) collective-permute-start(bf16[384,384]{1,0:T(8,128)(2,1)S(1)} %get-tuple-element.100.grad_ref.mid_ref), channel_id=1, source_target_pairs={{8,0},{16,8},{24,16},{32,24},{40,32},{48,40},{56,48},{64,56},{72,6... | collective-permute-start | bytes 884744 | tf_op jit(solution)/shard_map/ppermute | solution.py:649
  49.6 6.7 %collective-permute-start.4 = (bf16[384,384]{1,0:T(8,128)(2,1)S(1)}, bf16[384,384]{1,0:T(8,128)(2,1)S(1)}, u32[]{:S(2)}, u32[]{:S(2)}) collective-permute-start(bf16[384,384]{1,0:T(8,128)(2,1)S(1)} %get-tuple-element.100.grad_ref.mid_ref), channel_id=1, source_target_pairs={{0,8},{8,16},{16,24},{24,32},{32,40},{40,48},{48,56},{56,64},{64,7... | collective-permute-start | bytes 884744 | tf_op jit(solution)/shard_map/ppermute | solution.py:648
  49.6 17.4 %collective-permute-start.9 = (f32[3,144,512]{2,1,0:T(8,128)S(1)}, f32[3,144,512]{2,1,0:T(8,128)S(1)}, u32[]{:S(2)}, u32[]{:S(2)}) collective-permute-start(f32[3,144,512]{2,1,0:T(8,128)S(1)} %get-tuple-element.126), channel_id=1, source_target_pairs={{0,8},{8,0},{1,9},{9,1},{2,10},{10,2},{3,11},{11,3},{4,12},{12,4},... | collective-permute-start | bytes 2654216 | tf_op jit(solution)/shard_map/ppermute | solution.py:643
  52.5 3.8 %copy-start.1 = (bf16[512,864]{1,0:T(8,128)(2,1)S(1)}, bf16[512,864]{1,0:T(8,128)(2,1)}, u32[]{:S(2)}) copy-start(bf16[512,864]{1,0:T(8,128)(2,1)} %get-tuple-element.109.w2t_ref) | copy-start | bytes 2654212
  52.5 3.8 %copy-start.7 = (bf16[144,1536]{1,0:T(8,128)(2,1)S(1)}, bf16[144,1536]{1,0:T(8,128)(2,1)}, u32[]{:S(2)}) copy-start(bf16[144,1536]{1,0:T(8,128)(2,1)} %get-tuple-element.111.w1k_ref) | copy-start | bytes 1327108
  54.3 12.7 %collective-permute-start.8 = (f32[224,512]{1,0:T(8,128)S(1)}, f32[224,512]{1,0:T(8,128)S(1)}, u32[]{:S(2)}, u32[]{:S(2)}) collective-permute-start(f32[224,512]{1,0:T(8,128)S(1)} %get-tuple-element.125), channel_id=1, source_target_pairs={{0,8},{8,0},{1,9},{9,1},{2,10},{10,2},{3,11},{11,3},{4,12},{12,4},... | collective-permute-start | bytes 1376264 | tf_op jit(solution)/shard_map/ppermute | solution.py:651
  55.8 11.4 %collective-permute-start.7 = (f32[3,144,512]{2,1,0:T(8,128)S(1)}, f32[3,144,512]{2,1,0:T(8,128)S(1)}, u32[]{:S(2)}, u32[]{:S(2)}) collective-permute-start(f32[3,144,512]{2,1,0:T(8,128)S(1)} %get-tuple-element.123), channel_id=1, source_target_pairs={{0,8},{8,0},{1,9},{9,1},{2,10},{10,2},{3,11},{11,3},{4,12},{12,4},... | collective-permute-start | bytes 2654216 | tf_op jit(solution)/shard_map/ppermute | solution.py:655
  61.2 4.6 %copy-start.9 = (f32[96,96]{1,0:T(8,128)S(1)}, f32[96,96]{1,0:T(8,128)}, u32[]{:S(2)}) copy-start(f32[96,96]{1,0:T(8,128)} %get-tuple-element.119.refs_3_) | copy-start | bytes 110596
  62.7 4.4 %collective-permute-start.6 = (f32[224,512]{1,0:T(8,128)S(1)}, f32[224,512]{1,0:T(8,128)S(1)}, u32[]{:S(2)}, u32[]{:S(2)}) collective-permute-start(f32[224,512]{1,0:T(8,128)S(1)} %get-tuple-element.122), channel_id=1, source_target_pairs={{0,8},{8,0},{1,9},{9,1},{2,10},{10,2},{3,11},{11,3},{4,12},{12,4},... | collective-permute-start | bytes 1376264 | tf_op jit(solution)/shard_map/ppermute | solution.py:657
  68.5 30.2 %all-to-all-start.1 = ((bf16[64,88,128]{2,1,0:T(8,128)(2,1)}), bf16[64,88,128]{2,1,0:T(8,128)(2,1)S(1)}, u32[]{:S(2)}, u32[]{:S(2)}) async-start(bf16[64,88,128]{2,1,0:T(8,128)(2,1)} %merge.1), calls=%async_computation.1 | async-start | bytes 2883584 | tf_op jit(solution)/shard_map/all_to_all | solution.py:666
  123.6 6.9 %collective-permute-start.10 = (bf16[64,88,128]{2,1,0:T(8,128)(2,1)S(1)}, bf16[64,88,128]{2,1,0:T(8,128)(2,1)S(1)}, u32[]{:S(2)}, u32[]{:S(2)}) collective-permute-start(bf16[64,88,128]{2,1,0:T(8,128)(2,1)S(1)} %all_to_all.15.mine_ref), channel_id=1, source_target_pairs={{0,8},{8,0},{1,9},{9,1},{2,10},{10,2},{3,11},{11,3},{4,12},{12,4},... | collective-permute-start | bytes 4325384 | tf_op jit(solution)/shard_map/ppermute | solution.py:671

commit v2 on v1

--- a/solution.py
+++ b/solution.py
@@ -62,17 +62,25 @@
     return jax.ShapeDtypeStruct(shape, dtype)
 
 
-def call(body, outs, ins, scratch=(), smem=(), flops=0, name=None, limit=16):
+def call(
+    body, outs, ins, scratch=(), smem=(), hbm=(), hbm_outs=(), alias=None, flops=0, name=None, limit=16
+):
     moved = sum(x.size * x.dtype.itemsize for x in list(ins) + list(outs))
     return pl.pallas_call(
         body,
         out_shape=outs,
         in_specs=[
-            pl.BlockSpec(memory_space=pltpu.SMEM if i in smem else pltpu.VMEM)
+            pl.BlockSpec(
+                memory_space=pltpu.SMEM if i in smem else pltpu.HBM if i in hbm else pltpu.VMEM
+            )
             for i in range(len(ins))
         ],
-        out_specs=[pl.BlockSpec(memory_space=pltpu.VMEM) for _ in outs],
+        out_specs=[
+            pl.BlockSpec(memory_space=pltpu.HBM if i in hbm_outs else pltpu.VMEM)
+            for i in range(len(outs))
+        ],
         scratch_shapes=list(scratch),
+        input_output_aliases=alias or {},
         compiler_params=pltpu.CompilerParams(vmem_limit_bytes=limit * MIB),
         cost_estimate=pl.CostEstimate(flops=flops, bytes_accessed=moved, transcendentals=0),
         name=name,
@@ -560,49 +568,109 @@
     )[0]
 
 
-def unpack_kernel(core_ref, mine_ref, other_ref, win_ref, wout_ref, mix_ref, bin_ref, bout_ref, rows):
-    mine_first = core_ref[0] == 0
+def half_copies(half, k, rows, win_ref, wout_ref, sems):
+    at = k * FLOW_ROWS
+    count = IN_HALF if half == 0 else 9 * HALF - IN_HALF
+    pairs = [(at, count, win_ref.at[k, pl.ds(half * IN_HALF, count), :])]
+    for a in range(3):
+        start = at + IN_HALF + a * TAP_HALF
+        if half == 0:
+            pairs.append((start, CH, wout_ref.at[k, 3 * a + 2]))
+            pairs.append((start + CH, HALF, wout_ref.at[k, 3 * a + 1, pl.ds(0, HALF), :]))
+        else:
+            pairs.append((start, HALF, wout_ref.at[k, 3 * a + 1, pl.ds(HALF, HALF), :]))
+            pairs.append((start + HALF, CH, wout_ref.at[k, 3 * a]))
+    return [
+        pltpu.make_async_copy(rows.at[pl.ds(first, size), :], target, sems.at[7 * k + i])
+        for i, (first, size, target) in enumerate(pairs)
+    ]
+
+
+def put_half(half_now, shares_ref, rows, win_ref, wout_ref, sems):
+    groups = FLOW_ROWS // GROUP
+    for k in range(2):
+        for g in range(k * groups, (k + 1) * groups):
+            for lane in range(4):
+                rows[g * GROUP : (g + 1) * GROUP, lane * 128 : (lane + 1) * 128] = shares_ref[
+                    4 * g + lane
+                ].astype(F32)
+        for half in range(2):
+
+            @pl.when(half_now == half)
+            def _():
+                for copy in half_copies(half, k, rows, win_ref, wout_ref, sems):
+                    copy.start()
+
+
+def wait_half(half_now, rows, win_ref, wout_ref, sems):
     for half in range(2):
-        for g in range(2 * FLOW_ROWS // GROUP):
-            for lane in range(4):
-                mine = mine_ref[4 * g + lane].astype(F32)
-                other = other_ref[4 * g + lane].astype(F32)
-                first, second = (mine, other) if half == 0 else (other, mine)
-                rows[half, g * GROUP : (g + 1) * GROUP, lane * 128 : (lane + 1) * 128] = jnp.where(
-                    mine_first, first, second
-                )
+
+        @pl.when(half_now == half)
+        def _():
+            for k in range(2):
+                for copy in half_copies(half, k, rows, win_ref, wout_ref, sems):
+                    copy.wait()
+
+
+def unpack_own_kernel(core_ref, mine_ref, win_ref, wout_ref, rows, sems):
+    put_half(core_ref[0], mine_ref, rows, win_ref, wout_ref, sems)
+    wait_half(core_ref[0], rows, win_ref, wout_ref, sems)
+
+
+def unpack_other_kernel(
+    core_ref, mine_ref, other_ref, _win, _wout, win_ref, wout_ref, mix_ref, bin_ref, bout_ref,
+    rows, sems,
+):
+    put_half(1 - core_ref[0], other_ref, rows, win_ref, wout_ref, sems)
+    groups = FLOW_ROWS // GROUP
     for k in range(2):
-        at = k * FLOW_ROWS
-        win_ref[k, :IN_HALF] = rows[0, at : at + IN_HALF]
-        win_ref[k, IN_HALF:] = rows[1, at : at + 9 * HALF - IN_HALF]
-        bin_ref[k : k + 1, :] = rows[1, at + 9 * HALF - IN_HALF : at + 9 * HALF - IN_HALF + 1]
-        for a in range(3):
-            start = at + IN_HALF + a * TAP_HALF
-            wout_ref[k, 3 * a + 2] = rows[0, start : start + CH]
-            wout_ref[k, 3 * a + 1, :HALF] = rows[0, start + CH : start + TAP_HALF]
-            wout_ref[k, 3 * a + 1, HALF:] = rows[1, start : start + HALF]
-            wout_ref[k, 3 * a] = rows[1, start + HALF : start + TAP_HALF]
-        start = at + FLOW_ROWS - HALF
-        block = rows[0, start : start + HALF] + rows[1, start : start + HALF]
-        mix_ref[k, :HALF] = block[:, :CH]
-        mix_ref[k, HALF:] = block[:, 256 : 256 + CH]
-        bout_ref[k : k + 1, :] = block[:1, 128 : 128 + CH]
-
-
-def unpack(core, mine, other):
-    return call(
-        unpack_kernel,
-        [
-            sds((2, 9 * HALF, HID), F32),
-            sds((2, 9, CH, HID), F32),
-            sds((2, CH, CH), F32),
-            sds((2, HID), F32),
-            sds((2, CH), F32),
-        ],
-        [core, mine, other],
-        scratch=[pltpu.VMEM((2, 2 * FLOW_ROWS, HID), F32)],
+        last = 4 * ((k + 1) * groups - 1)
+        parts = [
+            mine_ref[last + lane][GROUP - HALF :].astype(F32)
+            + other_ref[last + lane][GROUP - HALF :].astype(F32)
+            for lane in range(4)
+        ]
+        mix_ref[k, :HALF] = parts[0][:, :CH]
+        mix_ref[k, HALF:] = parts[2][:, :CH]
+        bout_ref[k : k + 1, :] = parts[1][:1, :CH]
+        row = 9 * HALF - IN_HALF
+        share, row = 4 * (k * groups + row // GROUP), row % GROUP
+        for lane in range(4):
+            mine = mine_ref[share + lane].astype(F32)[row : row + 1]
+            other = other_ref[share + lane].astype(F32)[row : row + 1]
+            bin_ref[k : k + 1, lane * 128 : (lane + 1) * 128] = jnp.where(
+                core_ref[0] == 1, mine, other
+            )
+    wait_half(1 - core_ref[0], rows, win_ref, wout_ref, sems)
+
+
+KERNEL_GRADS = [((2, 9 * HALF, HID), F32), ((2, 9, CH, HID), F32)]
+
+
+def unpack_own(core, mine):
+    return call(
+        unpack_own_kernel,
+        [sds(*x) for x in KERNEL_GRADS],
+        [core, mine],
+        scratch=[pltpu.VMEM((2 * FLOW_ROWS, HID), F32), pltpu.SemaphoreType.DMA((14,))],
         smem=(0,),
-        name="unpack",
+        hbm_outs=(0, 1),
+        name="unpack_own",
+    )
+
+
+def unpack_other(core, mine, other, win, wout):
+    return call(
+        unpack_other_kernel,
+        [sds(*x) for x in KERNEL_GRADS]
+        + [sds((2, CH, CH), F32), sds((2, HID), F32), sds((2, CH), F32)],
+        [core, mine, other, win, wout],
+        scratch=[pltpu.VMEM((2 * FLOW_ROWS, HID), F32), pltpu.SemaphoreType.DMA((14,))],
+        smem=(0,),
+        hbm=(3, 4),
+        hbm_outs=(0, 1),
+        alias={3: 0, 4: 1},
+        name="unpack_other",
     )
 
 
@@ -664,12 +732,15 @@
         (keep_in1, keep_out1, got_in1, got_out1, small1),
     )
     shares = lax.all_to_all(packed, CHIPS, 0, 0, tiled=True)
-    input_grad = weave(after(gx0, packed))
     cells = float(CELLS * lat_count * lax.axis_size(ENS))
-    spread = totals(after(shares, input_grad), cells)
+    spread = totals(shares, cells)
     mine = lax.all_to_all(spread, CHIPS, 0, 0, tiled=True)
     other = lax.ppermute(mine, "c", swap)
-    in_grad, out_grad, mix_grad, in_bias_grad, out_bias_grad = unpack(core, mine, other)
+    win, wout = unpack_own(core, mine)
+    input_grad = weave(after(gx0, mine))
+    in_grad, out_grad, mix_grad, in_bias_grad, out_bias_grad = unpack_other(
+        core, mine, other, win, wout
+    )
     return (
         rebuilt,
         input_grad,

time: 134 us -> 132 us (0.985)
  blocking collectives: 24.6 us -> 54.6 us
  waiting for transfers between devices: 29.2 us -> 6.12 us
  starting transfers between devices: 31.2 us -> 22.6 us
    all_to_all x0 -> x1, blocking collectives: none -> 30 us  [local(): shares = lax.all_to_all(packed, CHIPS, 0, 0, tiled=True)]
    all_to_all x1 -> x0, waiting for transfers between devices: 20.2 us -> none  [local(): shares = lax.all_to_all(packed, CHIPS, 0, 0, tiled=True)]
    all_to_all x1 -> x0, starting transfers between devices: 8.58 us -> none  [local(): shares = lax.all_to_all(packed, CHIPS, 0, 0, tiled=True)]
    ppermute x1, waiting for transfers between devices: 2.85 us -> 0.01 us  [local(): other = lax.ppermute(mine, 'c', swap)]
    pallas_call x18 -> x19, Pallas kernels: 46.6 us -> 46.6 us  [call(): pl.pallas_call(body, out_shape=outs, in_specs=[pl.BlockSpec(memory_space=...]
  transfers between devices with their start and end apart: 13 -> 12, of which waited for: 5 -> 3; matrix products, arithmetic and copies ran while one was open for 1% -> 1% of each run, Pallas kernels for 21% -> 22%
where the time goes in v2:
time: 132 us
  blocking collectives  54.6 us (41%)
  Pallas kernels  46.6 us (35%)
  starting transfers between devices  22.6 us (17%)
  waiting for transfers between devices  6.12 us (5%)
    pallas_call x19, Pallas kernels, call(): pl.pallas_call(body, out_shape=outs, in_specs=[pl.BlockSpec(memory_space=...  46.6 us
    all_to_all x1, blocking collectives, local(): shares = lax.all_to_all(packed, CHIPS, 0, 0, tiled=True)  30 us
    all_to_all x1, blocking collectives, local(): mine = lax.all_to_all(spread, CHIPS, 0, 0, tiled=True)  24.6 us
    all_to_all x1, starting transfers between devices, local(): recv = lax.all_to_all(block, LAT, 0, 0, tiled=True)  6.91 us
    all_to_all x1, waiting for transfers between devices, local(): recv = lax.all_to_all(block, LAT, 0, 0, tiled=True)  5.11 us
    ppermute x1, starting transfers between devices, local(): other = lax.ppermute(mine, 'c', swap)  4.04 us
    ppermute x1, starting transfers between devices, local(): bottom0 = lax.ppermute(grad0, LAT, back)  3.09 us
    ppermute x1, starting transfers between devices, local(): got_in0 = lax.ppermute(give_in0, 'c', swap)  3.01 us
  transfers between devices with their start and end apart: 12, of which 3 were waited for; matrix products, arithmetic and copies ran while one was open for 1% of the time, Pallas kernels for 22%

profile of v2, /device:TPU:1, one launch (start us, length us, event | category | flops | bytes accessed | tf_op | source)
XLA Modules:
  0.0 132.1 jit_solution(5758394363287489938)
XLA Ops:
  0.6 2.2 %payload.1 = bf16[16,24,960]{2,1,0:T(8,128)(2,1)} custom-call(f32[16,24,192]{2,1,0:T(8,128)} %bitcast.11, f32[16,24,192]{2,1,0:T(8,128)} %bitcast.12), custom_call_target="tpu_custom_call" | custom-call | bytes 1327104 | tf_op jit(solution)/shard_map/payload/pallas_call | solution.py:69
  2.9 6.9 %all-to-all-start = ((bf16[16,24,960]{2,1,0:T(8,128)(2,1)}), bf16[16,24,960]{2,1,0:T(8,128)(2,1)S(1)}, u32[]{:S(2)}, u32[]{:S(2)}) async-start(bf16[16,24,960]{2,1,0:T(8,128)(2,1)} %payload.1), calls=%async_computation | async-start | bytes 1572864 | tf_op jit(solution)/shard_map/all_to_all | solution.py:693
  9.8 0.7 reduce
  10.5 7.0 %prep.1 = (f32[96,96]{1,0:T(8,128)}, f32[96,96]{1,0:T(8,128)}, bf16[512,448]{1,0:T(8,128)(2,1)}, bf16[512,864]{1,0:T(8,128)(2,1)}, bf16[288,1536]{1,0:T(8,128)(2...) custom-call(f32[2,96,96]{2,1,0:T(8,128)} %refs_5_.3, ...), custom_call_target="tpu_custom_call" | custom-call | bytes 8227584 | tf_op jit(solution)/shard_map/prep/pallas_call | solution.py:69
  17.6 5.1 %all-to-all-done.recv_ref = bf16[16,24,960]{2,1,0:T(8,128)(2,1)S(1)} async-done(((bf16[16,24,960]{2,1,0:T(8,128)(2,1)}), bf16[16,24,960]{2,1,0:T(8,128)(2,1)S(1)}, u32[]{:S(2)}, u32[]{:S(2)}) %all-to-all-start) | async-done | bytes 737312 | tf_op jit(solution)/shard_map/all_to_all | solution.py:693
  22.8 0.7 turn.1
  23.5 5.2 %forward.2 = (f32[96,1536]{1,0:T(8,128)S(1)}, bf16[2048,768]{1,0:T(8,128)(2,1)S(1)}, f32[2048,768]{1,0:T(8,128)S(1)}, bf16[192,384]{1,0:T(8,128)(2,1)S(1)}, bf16...) custom-call(f32[2]{0:T(128)S(1)} %add_convert_fusion.flags_ref, ...), custom_call_target="tpu_custom_call" | custom-call | flops 4000000000 | bytes 13179912 | tf_op jit(solution)/shard_map/forward/pallas_call | solution.py:69
  28.7 0.9 collective-permute-start.1
  29.7 0.9 collective-permute-start
  30.5 1.7 %collective-permute-start.2 = (bf16[384,384]{1,0:T(8,128)(2,1)S(1)}, bf16[384,384]{1,0:T(8,128)(2,1)S(1)}, u32[]{:S(2)}, u32[]{:S(2)}) collective-permute-start(bf16[384,384]{1,0:T(8,128)(2,1)S(1)} %get-tuple-element.80.grad_ref.mid_ref), channel_id=1, source_target_pairs={{0,8},{8,16},{16,24},{24,32},{32,40},{40,48},{48,56},{56,64},{64,7... | collective-permute-start | bytes 884744 | tf_op jit(solution)/shard_map/ppermute | solution.py:704
  32.4 1.7 %out_weight.2 = (f32[3,144,512]{2,1,0:T(8,128)S(1)}, f32[3,144,512]{2,1,0:T(8,128)S(1)}, f32[8,96]{1,0:T(8,128)S(1)}) custom-call(s32[1]{0:T(128)} %bitcast.2.core_ref, bf16[384,384]{1,0:T(8,128)(2,1)S(1)} %get-tuple-element.80.grad_ref.mid_ref, bf16[2048,768]{1,0:T(8,128)(2,1)S(1)} %get-tuple-element.81.rows_ref), custom_call_target="tpu_custom_call" | custom-call | flops 2000000000 | bytes 5213188 | tf_op jit(solution)/shard_map/out_weight/pallas_call | solution.py:69
  34.2 5.1 %forward.3 = (f32[96,1536]{1,0:T(8,128)S(1)}, bf16[2048,768]{1,0:T(8,128)(2,1)S(1)}, f32[2048,768]{1,0:T(8,128)S(1)}, f32[48,1536]{1,0:T(8,128)S(1)}) custom-call(f32[2]{0:T(128)S(1)} %add_convert_fusion.flags_ref, bf16[192,384]{1,0:T(8,128)(2,1)S(1)} %collective-permute-done.refs_0_.above_ref, bf16[192,384]{1,0:T(8,128)(2,1)S(1)} %get-tuple-element.84.refs_1_.mid_ref, ...), custom_call_target="tpu_custom_call" | custom-call | flops 4000000000 | bytes 12737544 | tf_op jit(solution)/shard_map/forward/pallas_call | solution.py:69
  39.3 0.8 collective-permute-done.3.below_ref
  40.2 5.0 %backward.2 = (bf16[2048,768]{1,0:T(8,128)(2,1)S(1)}, f32[192,384]{1,0:T(8,128)S(1)}) custom-call(f32[2]{0:T(128)S(1)} %add_convert_fusion.flags_ref, bf16[384,384]{1,0:T(8,128)(2,1)S(1)} %collective-permute-done.2.above_ref, bf16[384,384]{1,0:T(8,128)(2,1)S(1)} %get-tuple-element.80.grad_ref.mid_ref, bf16[384,384]{1,0:T(8,128)(2,1)S(1)} %collective-permute-done.3.below_ref, ...), custom_call_target="tpu_custom_call" | custom-call | flops 6000000000 | bytes 11943944 | tf_op jit(solution)/shard_map/backward/pallas_call | solution.py:69
  45.2 1.3 close.2
  46.5 3.1 %collective-permute-start.5 = (bf16[384,384]{1,0:T(8,128)(2,1)S(1)}, bf16[384,384]{1,0:T(8,128)(2,1)S(1)}, u32[]{:S(2)}, u32[]{:S(2)}) collective-permute-start(bf16[384,384]{1,0:T(8,128)(2,1)S(1)} %get-tuple-element.101.grad_ref.mid_ref), channel_id=1, source_target_pairs={{8,0},{16,8},{24,16},{32,24},{40,32},{48,40},{56,48},{64,56},{72,6... | collective-permute-start | bytes 884744 | tf_op jit(solution)/shard_map/ppermute | solution.py:717
  49.6 1.4 %collective-permute-start.9 = (f32[3,144,512]{2,1,0:T(8,128)S(1)}, f32[3,144,512]{2,1,0:T(8,128)S(1)}, u32[]{:S(2)}, u32[]{:S(2)}) collective-permute-start(f32[3,144,512]{2,1,0:T(8,128)S(1)} %get-tuple-element.127), channel_id=1, source_target_pairs={{0,8},{8,0},{1,9},{9,1},{2,10},{10,2},{3,11},{11,3},{4,12},{12,4},... | collective-permute-start | bytes 2654216 | tf_op jit(solution)/shard_map/ppermute | solution.py:711
  51.0 1.5 %in_weight.2 = (f32[224,512]{1,0:T(8,128)S(1)}, f32[224,512]{1,0:T(8,128)S(1)}) custom-call(s32[1]{0:T(128)} %bitcast.2.core_ref, f32[2]{0:T(128)S(1)} %add_convert_fusion.flags_ref, bf16[192,384]{1,0:T(8,128)(2,1)S(1)} %get-tuple-element.72.refs_0_.above_ref, bf16[192,384]{1,0:T(8,128)(2,1)S(1)} %get-tuple-element.73.refs_1_.mid_ref, ...), custom_call_target="tpu_custom_call" | custom-call | flops 1000000000 | bytes 4505612 | tf_op jit(solution)/shard_map/in_weight/pallas_call | solution.py:69
  52.5 1.7 %out_weight.3 = (f32[3,144,512]{2,1,0:T(8,128)S(1)}, f32[3,144,512]{2,1,0:T(8,128)S(1)}, f32[8,96]{1,0:T(8,128)S(1)}) custom-call(s32[1]{0:T(128)} %bitcast.2.core_ref, bf16[384,384]{1,0:T(8,128)(2,1)S(1)} %get-tuple-element.101.grad_ref.mid_ref, bf16[2048,768]{1,0:T(8,128)(2,1)S(1)} %get-tuple-element.106.rows_ref), custom_call_target="tpu_custom_call" | custom-call | flops 2000000000 | bytes 5213188 | tf_op jit(solution)/shard_map/out_weight/pallas_call | solution.py:69
  54.4 1.4 %weave.2 = f32[1,96,2,768]{3,2,1,0:T(2,128)} custom-call(f32[96,1536]{1,0:T(8,128)S(1)} %get-tuple-element.108.x_ref.refs_4_), custom_call_target="tpu_custom_call" | custom-call | bytes 1179648 | tf_op jit(solution)/shard_map/weave/pallas_call | solution.py:69
  55.8 0.5 collective-permute-start.7
  56.3 4.9 %backward.3 = (bf16[2048,768]{1,0:T(8,128)(2,1)S(1)}, f32[192,384]{1,0:T(8,128)S(1)}) custom-call(f32[2]{0:T(128)S(1)} %add_convert_fusion.flags_ref, bf16[384,384]{1,0:T(8,128)(2,1)S(1)} %collective-permute-done.4.above_ref, bf16[384,384]{1,0:T(8,128)(2,1)S(1)} %get-tuple-element.101.grad_ref.mid_ref, ...), custom_call_target="tpu_custom_call" | custom-call | flops 6000000000 | bytes 11943944 | tf_op jit(solution)/shard_map/backward/pallas_call | solution.py:69
  61.2 1.5 %in_weight.3 = (f32[224,512]{1,0:T(8,128)S(1)}, f32[224,512]{1,0:T(8,128)S(1)}) custom-call(s32[1]{0:T(128)} %bitcast.2.core_ref, f32[2]{0:T(128)S(1)} %add_convert_fusion.flags_ref, bf16[192,384]{1,0:T(8,128)(2,1)S(1)} %collective-permute-done.refs_0_.above_ref, bf16[192,384]{1,0:T(8,128)(2,1)S(1)} %get-tuple-element.84.refs_1_.mid_ref, ...), custom_call_target="tpu_custom_call" | custom-call | flops 1000000000 | bytes 4505612 | tf_op jit(solution)/shard_map/in_weight/pallas_call | solution.py:69
  62.7 3.0 %collective-permute-start.6 = (f32[224,512]{1,0:T(8,128)S(1)}, f32[224,512]{1,0:T(8,128)S(1)}, u32[]{:S(2)}, u32[]{:S(2)}) collective-permute-start(f32[224,512]{1,0:T(8,128)S(1)} %get-tuple-element.123), channel_id=1, source_target_pairs={{0,8},{8,0},{1,9},{9,1},{2,10},{10,2},{3,11},{11,3},{4,12},{12,4},... | collective-permute-start | bytes 1376264 | tf_op jit(solution)/shard_map/ppermute | solution.py:725
  65.7 1.2 close.3
  67.4 30.0 %all_to_all.15.shares_ref = bf16[64,88,128]{2,1,0:T(8,128)(2,1)S(1)} all-to-all(bf16[64,88,128]{2,1,0:T(8,128)(2,1)S(1)} %merge.1), channel_id=1, replica_groups=mesh['y'=4,'xl'=2,'c'=2,'z'=4,'xh'=2] {'y','xl','z','xh'}, dimensions={0} | all-to-all | bytes 2883584 | tf_op jit(solution)/shard_map/all_to_all | solution.py:734
  97.4 0.3 totals.1
  97.7 24.6 %all_to_all.16.mine_ref = bf16[64,88,128]{2,1,0:T(8,128)(2,1)S(1)} all-to-all(bf16[64,88,128]{2,1,0:T(8,128)(2,1)S(1)} %totals.1), channel_id=1, replica_groups=mesh['y'=4,'xl'=2,'c'=2,'z'=4,'xh'=2] {'y','xl','z','xh'}, dimensions={0} | all-to-all | bytes 2883584 | tf_op jit(solution)/shard_map/all_to_all | solution.py:737
  122.3 4.0 %collective-permute-start.10 = (bf16[64,88,128]{2,1,0:T(8,128)(2,1)S(1)}, bf16[64,88,128]{2,1,0:T(8,128)(2,1)S(1)}, u32[]{:S(2)}, u32[]{:S(2)}) collective-permute-start(bf16[64,88,128]{2,1,0:T(8,128)(2,1)S(1)} %all_to_all.16.mine_ref), channel_id=1, source_target_pairs={{0,8},{8,0},{1,9},{9,1},{2,10},{10,2},{3,11},{11,3},{4,12},{12,4},... | collective-permute-start | bytes 4325384 | tf_op jit(solution)/shard_map/ppermute | solution.py:738
  126.4 1.4 %weave.3 = f32[1,96,2,768]{3,2,1,0:T(2,128)} custom-call(f32[96,1536]{1,0:T(8,128)S(1)} %get-tuple-element.129.x_ref), custom_call_target="tpu_custom_call" | custom-call | bytes 1179648 | tf_op jit(solution)/shard_map/weave/pallas_call | solution.py:69
  127.8 1.7 %unpack_own.1 = (f32[2,432,512]{2,1,0:T(8,128)}, f32[2,9,96,512]{3,2,1,0:T(8,128)}) custom-call(s32[1]{0:T(128)} %bitcast.2.core_ref, bf16[64,88,128]{2,1,0:T(8,128)(2,1)S(1)} %all_to_all.16.mine_ref), custom_call_target="tpu_custom_call" | custom-call | bytes 6750212 | tf_op jit(solution)/shard_map/unpack_own/pallas_call | solution.py:69
  129.5 2.4 %unpack_other.1 = (f32[2,432,512]{2,1,0:T(8,128)}, f32[2,9,96,512]{3,2,1,0:T(8,128)}, f32[2,96,96]{2,1,0:T(8,128)}, f32[2,512]{1,0:T(2,128)}, f32[2,96]{1,0:T(2,128)}) custom-call(s32[1]{0:T(128)} %bitcast.2.core_ref, bf16[64,88,128]{2,1,0:T(8,128)(2,1)S(1)} %all_to_all.16.mine_ref, ...), custom_call_target="tpu_custom_call", output_to_operand_aliasing={{0}: (3, {}), {1}: (4, {})} | custom-call | bytes 13579012 | tf_op jit(solution)/shard_map/unpack_other/pallas_call | solution.py:69
  (49 shorter events, 0.8 us)
Async XLA Ops:
  0.6 9.1 %copy-start.15 = (f32[1,192,1,384]{3,2,1,0:T(1,128)S(1)}, f32[1,192,1,384]{3,2,1,0:T(1,128)}, u32[]{:S(2)}) copy-start(f32[1,192,1,384]{3,2,1,0:T(1,128)} %param.10) | copy-start | bytes 884740
  2.9 19.9 %all-to-all-start = ((bf16[16,24,960]{2,1,0:T(8,128)(2,1)}), bf16[16,24,960]{2,1,0:T(8,128)(2,1)S(1)}, u32[]{:S(2)}, u32[]{:S(2)}) async-start(bf16[16,24,960]{2,1,0:T(8,128)(2,1)} %payload.1), calls=%async_computation | async-start | bytes 1572864 | tf_op jit(solution)/shard_map/all_to_all | solution.py:693
  17.6 5.9 %copy-start.4 = (bf16[288,1536]{1,0:T(8,128)(2,1)S(1)}, bf16[288,1536]{1,0:T(8,128)(2,1)}, u32[]{:S(2)}) copy-start(bf16[288,1536]{1,0:T(8,128)(2,1)} %get-tuple-element.76.refs_4_) | copy-start | bytes 2654212
  17.6 5.9 %copy-start.6 = (bf16[512,448]{1,0:T(8,128)(2,1)S(1)}, bf16[512,448]{1,0:T(8,128)(2,1)}, u32[]{:S(2)}) copy-start(bf16[512,448]{1,0:T(8,128)(2,1)} %get-tuple-element.75.refs_3_) | copy-start | bytes 1376260
  17.6 5.9 %copy-start.13 = (f32[96,96]{1,0:T(8,128)S(1)}, f32[96,96]{1,0:T(8,128)}, u32[]{:S(2)}) copy-start(f32[96,96]{1,0:T(8,128)} %get-tuple-element.78.refs_6_) | copy-start | bytes 110596
  17.6 5.9 %copy-start.14 = (f32[96,8]{1,0:T(8,128)S(1)}, f32[96,8]{1,0:T(8,128)}, u32[]{:S(2)}) copy-start(f32[96,8]{1,0:T(8,128)} %get-tuple-element.77.refs_5_) | copy-start | bytes 9220
  28.7 5.4 %collective-permute-start.1 = (bf16[192,384]{1,0:T(8,128)(2,1)S(1)}, bf16[192,384]{1,0:T(8,128)(2,1)S(1)}, u32[]{:S(2)}, u32[]{:S(2)}) collective-permute-start(bf16[192,384]{1,0:T(8,128)(2,1)S(1)} %get-tuple-element.84.refs_1_.mid_ref), channel_id=1, source_target_pairs={{8,0},{16,8},{24,16},{32,24},{40,32},{48,40},{56,48},{64,56},{72,6... | collective-permute-start | bytes 442376 | tf_op jit(solution)/shard_map/ppermute | solution.py:703
  29.7 4.5 %collective-permute-start = (bf16[192,384]{1,0:T(8,128)(2,1)S(1)}, bf16[192,384]{1,0:T(8,128)(2,1)S(1)}, u32[]{:S(2)}, u32[]{:S(2)}) collective-permute-start(bf16[192,384]{1,0:T(8,128)(2,1)S(1)} %get-tuple-element.84.refs_1_.mid_ref), channel_id=1, source_target_pairs={{0,8},{8,16},{16,24},{24,32},{32,40},{40,48},{48,56},{56,64},{64,7... | collective-permute-start | bytes 442376 | tf_op jit(solution)/shard_map/ppermute | solution.py:702
  30.5 9.6 %collective-permute-start.3 = (bf16[384,384]{1,0:T(8,128)(2,1)S(1)}, bf16[384,384]{1,0:T(8,128)(2,1)S(1)}, u32[]{:S(2)}, u32[]{:S(2)}) collective-permute-start(bf16[384,384]{1,0:T(8,128)(2,1)S(1)} %get-tuple-element.80.grad_ref.mid_ref), channel_id=1, source_target_pairs={{8,0},{16,8},{24,16},{32,24},{40,32},{48,40},{56,48},{64,56},{72,6... | collective-permute-start | bytes 884744 | tf_op jit(solution)/shard_map/ppermute | solution.py:705
  30.5 9.6 %collective-permute-start.2 = (bf16[384,384]{1,0:T(8,128)(2,1)S(1)}, bf16[384,384]{1,0:T(8,128)(2,1)S(1)}, u32[]{:S(2)}, u32[]{:S(2)}) collective-permute-start(bf16[384,384]{1,0:T(8,128)(2,1)S(1)} %get-tuple-element.80.grad_ref.mid_ref), channel_id=1, source_target_pairs={{0,8},{8,16},{16,24},{24,32},{32,40},{40,48},{48,56},{56,64},{64,7... | collective-permute-start | bytes 884744 | tf_op jit(solution)/shard_map/ppermute | solution.py:704
  32.3 1.8 %copy-start.3 = (bf16[288,1536]{1,0:T(8,128)(2,1)S(1)}, bf16[288,1536]{1,0:T(8,128)(2,1)}, u32[]{:S(2)}) copy-start(bf16[288,1536]{1,0:T(8,128)(2,1)} %get-tuple-element.86.refs_4_) | copy-start | bytes 2654212
  32.3 1.8 %copy-start.5 = (bf16[512,448]{1,0:T(8,128)(2,1)S(1)}, bf16[512,448]{1,0:T(8,128)(2,1)}, u32[]{:S(2)}) copy-start(bf16[512,448]{1,0:T(8,128)(2,1)} %get-tuple-element.85.refs_3_) | copy-start | bytes 1376260
  32.3 1.8 %copy-start.11 = (f32[96,96]{1,0:T(8,128)S(1)}, f32[96,96]{1,0:T(8,128)}, u32[]{:S(2)}) copy-start(f32[96,96]{1,0:T(8,128)} %get-tuple-element.88.refs_6_) | copy-start | bytes 110596
  32.4 1.8 %copy-start.12 = (f32[96,8]{1,0:T(8,128)S(1)}, f32[96,8]{1,0:T(8,128)}, u32[]{:S(2)}) copy-start(f32[96,8]{1,0:T(8,128)} %get-tuple-element.87.refs_5_) | copy-start | bytes 9220
  34.2 6.0 %copy-start.2 = (bf16[512,864]{1,0:T(8,128)(2,1)S(1)}, bf16[512,864]{1,0:T(8,128)(2,1)}, u32[]{:S(2)}) copy-start(bf16[512,864]{1,0:T(8,128)(2,1)} %get-tuple-element.92.w2t_ref) | copy-start | bytes 2654212
  34.2 5.9 %copy-start.8 = (bf16[144,1536]{1,0:T(8,128)(2,1)S(1)}, bf16[144,1536]{1,0:T(8,128)(2,1)}, u32[]{:S(2)}) copy-start(bf16[144,1536]{1,0:T(8,128)(2,1)} %get-tuple-element.94.w1k_ref) | copy-start | bytes 1327108
  40.1 5.0 %copy-start = (f32[2,96,96]{2,1,0:T(8,128)S(1)}, f32[2,96,96]{2,1,0:T(8,128)}, u32[]{:S(2)}) copy-start(f32[2,96,96]{2,1,0:T(8,128)} %refs_5_.3) | copy-start | bytes 221188
  40.2 5.0 %copy-start.10 = (f32[96,96]{1,0:T(8,128)S(1)}, f32[96,96]{1,0:T(8,128)}, u32[]{:S(2)}) copy-start(f32[96,96]{1,0:T(8,128)} %get-tuple-element.98.refs_3_) | copy-start | bytes 110596
  46.5 9.8 %collective-permute-start.5 = (bf16[384,384]{1,0:T(8,128)(2,1)S(1)}, bf16[384,384]{1,0:T(8,128)(2,1)S(1)}, u32[]{:S(2)}, u32[]{:S(2)}) collective-permute-start(bf16[384,384]{1,0:T(8,128)(2,1)S(1)} %get-tuple-element.101.grad_ref.mid_ref), channel_id=1, source_target_pairs={{8,0},{16,8},{24,16},{32,24},{40,32},{48,40},{56,48},{64,56},{72,6... | collective-permute-start | bytes 884744 | tf_op jit(solution)/shard_map/ppermute | solution.py:717
  49.6 6.7 %collective-permute-start.4 = (bf16[384,384]{1,0:T(8,128)(2,1)S(1)}, bf16[384,384]{1,0:T(8,128)(2,1)S(1)}, u32[]{:S(2)}, u32[]{:S(2)}) collective-permute-start(bf16[384,384]{1,0:T(8,128)(2,1)S(1)} %get-tuple-element.101.grad_ref.mid_ref), channel_id=1, source_target_pairs={{0,8},{8,16},{16,24},{24,32},{32,40},{40,48},{48,56},{56,64},{64,7... | collective-permute-start | bytes 884744 | tf_op jit(solution)/shard_map/ppermute | solution.py:716
  49.6 17.4 %collective-permute-start.9 = (f32[3,144,512]{2,1,0:T(8,128)S(1)}, f32[3,144,512]{2,1,0:T(8,128)S(1)}, u32[]{:S(2)}, u32[]{:S(2)}) collective-permute-start(f32[3,144,512]{2,1,0:T(8,128)S(1)} %get-tuple-element.127), channel_id=1, source_target_pairs={{0,8},{8,0},{1,9},{9,1},{2,10},{10,2},{3,11},{11,3},{4,12},{12,4},... | collective-permute-start | bytes 2654216 | tf_op jit(solution)/shard_map/ppermute | solution.py:711
  52.5 3.8 %copy-start.1 = (bf16[512,864]{1,0:T(8,128)(2,1)S(1)}, bf16[512,864]{1,0:T(8,128)(2,1)}, u32[]{:S(2)}) copy-start(bf16[512,864]{1,0:T(8,128)(2,1)} %get-tuple-element.110.w2t_ref) | copy-start | bytes 2654212
  52.5 3.8 %copy-start.7 = (bf16[144,1536]{1,0:T(8,128)(2,1)S(1)}, bf16[144,1536]{1,0:T(8,128)(2,1)}, u32[]{:S(2)}) copy-start(bf16[144,1536]{1,0:T(8,128)(2,1)} %get-tuple-element.112.w1k_ref) | copy-start | bytes 1327108
  54.3 12.7 %collective-permute-start.8 = (f32[224,512]{1,0:T(8,128)S(1)}, f32[224,512]{1,0:T(8,128)S(1)}, u32[]{:S(2)}, u32[]{:S(2)}) collective-permute-start(f32[224,512]{1,0:T(8,128)S(1)} %get-tuple-element.126), channel_id=1, source_target_pairs={{0,8},{8,0},{1,9},{9,1},{2,10},{10,2},{3,11},{11,3},{4,12},{12,4},... | collective-permute-start | bytes 1376264 | tf_op jit(solution)/shard_map/ppermute | solution.py:719
  55.8 11.4 %collective-permute-start.7 = (f32[3,144,512]{2,1,0:T(8,128)S(1)}, f32[3,144,512]{2,1,0:T(8,128)S(1)}, u32[]{:S(2)}, u32[]{:S(2)}) collective-permute-start(f32[3,144,512]{2,1,0:T(8,128)S(1)} %get-tuple-element.124), channel_id=1, source_target_pairs={{0,8},{8,0},{1,9},{9,1},{2,10},{10,2},{3,11},{11,3},{4,12},{12,4},... | collective-permute-start | bytes 2654216 | tf_op jit(solution)/shard_map/ppermute | solution.py:723
  61.2 4.6 %copy-start.9 = (f32[96,96]{1,0:T(8,128)S(1)}, f32[96,96]{1,0:T(8,128)}, u32[]{:S(2)}) copy-start(f32[96,96]{1,0:T(8,128)} %get-tuple-element.120.refs_3_) | copy-start | bytes 110596
  62.7 4.5 %collective-permute-start.6 = (f32[224,512]{1,0:T(8,128)S(1)}, f32[224,512]{1,0:T(8,128)S(1)}, u32[]{:S(2)}, u32[]{:S(2)}) collective-permute-start(f32[224,512]{1,0:T(8,128)S(1)} %get-tuple-element.123), channel_id=1, source_target_pairs={{0,8},{8,0},{1,9},{9,1},{2,10},{10,2},{3,11},{11,3},{4,12},{12,4},... | collective-permute-start | bytes 1376264 | tf_op jit(solution)/shard_map/ppermute | solution.py:725
  122.3 7.2 %collective-permute-start.10 = (bf16[64,88,128]{2,1,0:T(8,128)(2,1)S(1)}, bf16[64,88,128]{2,1,0:T(8,128)(2,1)S(1)}, u32[]{:S(2)}, u32[]{:S(2)}) collective-permute-start(bf16[64,88,128]{2,1,0:T(8,128)(2,1)S(1)} %all_to_all.16.mine_ref), channel_id=1, source_target_pairs={{0,8},{8,0},{1,9},{9,1},{2,10},{10,2},{3,11},{11,3},{4,12},{12,4},... | collective-permute-start | bytes 4325384 | tf_op jit(solution)/shard_map/ppermute | solution.py:738

commit v3 on v2

--- a/solution.py
+++ b/solution.py
@@ -626,8 +626,8 @@
     for k in range(2):
         last = 4 * ((k + 1) * groups - 1)
         parts = [
-            mine_ref[last + lane][GROUP - HALF :].astype(F32)
-            + other_ref[last + lane][GROUP - HALF :].astype(F32)
+            mine_ref[last + lane].astype(F32)[GROUP - HALF :]
+            + other_ref[last + lane].astype(F32)[GROUP - HALF :]
             for lane in range(4)
         ]
         mix_ref[k, :HALF] = parts[0][:, :CH]

time: 132 us -> 132 us (level)
  no operation moved by 1% of the time
where the time goes in v3:
time: 132 us
  blocking collectives  54.6 us (41%)
  Pallas kernels  46.6 us (35%)
  starting transfers between devices  22.6 us (17%)
  waiting for transfers between devices  6.12 us (5%)
    pallas_call x19, Pallas kernels, call(): pl.pallas_call(body, out_shape=outs, in_specs=[pl.BlockSpec(memory_space=...  46.6 us
    all_to_all x1, blocking collectives, local(): shares = lax.all_to_all(packed, CHIPS, 0, 0, tiled=True)  30 us
    all_to_all x1, blocking collectives, local(): mine = lax.all_to_all(spread, CHIPS, 0, 0, tiled=True)  24.6 us
    all_to_all x1, starting transfers between devices, local(): recv = lax.all_to_all(block, LAT, 0, 0, tiled=True)  6.91 us
    all_to_all x1, waiting for transfers between devices, local(): recv = lax.all_to_all(block, LAT, 0, 0, tiled=True)  5.11 us
    ppermute x1, starting transfers between devices, local(): other = lax.ppermute(mine, 'c', swap)  4.04 us
    ppermute x1, starting transfers between devices, local(): bottom0 = lax.ppermute(grad0, LAT, back)  3.09 us
    ppermute x1, starting transfers between devices, local(): got_in0 = lax.ppermute(give_in0, 'c', swap)  3.01 us
  transfers between devices with their start and end apart: 12, of which 3 were waited for; matrix products, arithmetic and copies ran while one was open for 1% of the time, Pallas kernels for 22%

profile of v3, /device:TPU:1, one launch (start us, length us, event | category | flops | bytes accessed | tf_op | source)
XLA Modules:
  0.0 132.1 jit_solution(5758394363287489938)
XLA Ops:
  0.6 2.2 %payload.1 = bf16[16,24,960]{2,1,0:T(8,128)(2,1)} custom-call(f32[16,24,192]{2,1,0:T(8,128)} %bitcast.11, f32[16,24,192]{2,1,0:T(8,128)} %bitcast.12), custom_call_target="tpu_custom_call" | custom-call | bytes 1327104 | tf_op jit(solution)/shard_map/payload/pallas_call | solution.py:69
  2.9 6.9 %all-to-all-start = ((bf16[16,24,960]{2,1,0:T(8,128)(2,1)}), bf16[16,24,960]{2,1,0:T(8,128)(2,1)S(1)}, u32[]{:S(2)}, u32[]{:S(2)}) async-start(bf16[16,24,960]{2,1,0:T(8,128)(2,1)} %payload.1), calls=%async_computation | async-start | bytes 1572864 | tf_op jit(solution)/shard_map/all_to_all | solution.py:693
  9.8 0.7 reduce
  10.5 7.0 %prep.1 = (f32[96,96]{1,0:T(8,128)}, f32[96,96]{1,0:T(8,128)}, bf16[512,448]{1,0:T(8,128)(2,1)}, bf16[512,864]{1,0:T(8,128)(2,1)}, bf16[288,1536]{1,0:T(8,128)(2...) custom-call(f32[2,96,96]{2,1,0:T(8,128)} %refs_5_.3, ...), custom_call_target="tpu_custom_call" | custom-call | bytes 8227584 | tf_op jit(solution)/shard_map/prep/pallas_call | solution.py:69
  17.6 5.1 %all-to-all-done.recv_ref = bf16[16,24,960]{2,1,0:T(8,128)(2,1)S(1)} async-done(((bf16[16,24,960]{2,1,0:T(8,128)(2,1)}), bf16[16,24,960]{2,1,0:T(8,128)(2,1)S(1)}, u32[]{:S(2)}, u32[]{:S(2)}) %all-to-all-start) | async-done | bytes 737312 | tf_op jit(solution)/shard_map/all_to_all | solution.py:693
  22.8 0.7 turn.1
  23.5 5.2 %forward.2 = (f32[96,1536]{1,0:T(8,128)S(1)}, bf16[2048,768]{1,0:T(8,128)(2,1)S(1)}, f32[2048,768]{1,0:T(8,128)S(1)}, bf16[192,384]{1,0:T(8,128)(2,1)S(1)}, bf16...) custom-call(f32[2]{0:T(128)S(1)} %add_convert_fusion.flags_ref, ...), custom_call_target="tpu_custom_call" | custom-call | flops 4000000000 | bytes 13179912 | tf_op jit(solution)/shard_map/forward/pallas_call | solution.py:69
  28.7 0.9 collective-permute-start.1
  29.7 0.9 collective-permute-start
  30.5 1.7 %collective-permute-start.2 = (bf16[384,384]{1,0:T(8,128)(2,1)S(1)}, bf16[384,384]{1,0:T(8,128)(2,1)S(1)}, u32[]{:S(2)}, u32[]{:S(2)}) collective-permute-start(bf16[384,384]{1,0:T(8,128)(2,1)S(1)} %get-tuple-element.80.grad_ref.mid_ref), channel_id=1, source_target_pairs={{0,8},{8,16},{16,24},{24,32},{32,40},{40,48},{48,56},{56,64},{64,7... | collective-permute-start | bytes 884744 | tf_op jit(solution)/shard_map/ppermute | solution.py:704
  32.4 1.7 %out_weight.2 = (f32[3,144,512]{2,1,0:T(8,128)S(1)}, f32[3,144,512]{2,1,0:T(8,128)S(1)}, f32[8,96]{1,0:T(8,128)S(1)}) custom-call(s32[1]{0:T(128)} %bitcast.2.core_ref, bf16[384,384]{1,0:T(8,128)(2,1)S(1)} %get-tuple-element.80.grad_ref.mid_ref, bf16[2048,768]{1,0:T(8,128)(2,1)S(1)} %get-tuple-element.81.rows_ref), custom_call_target="tpu_custom_call" | custom-call | flops 2000000000 | bytes 5213188 | tf_op jit(solution)/shard_map/out_weight/pallas_call | solution.py:69
  34.2 5.1 %forward.3 = (f32[96,1536]{1,0:T(8,128)S(1)}, bf16[2048,768]{1,0:T(8,128)(2,1)S(1)}, f32[2048,768]{1,0:T(8,128)S(1)}, f32[48,1536]{1,0:T(8,128)S(1)}) custom-call(f32[2]{0:T(128)S(1)} %add_convert_fusion.flags_ref, bf16[192,384]{1,0:T(8,128)(2,1)S(1)} %collective-permute-done.refs_0_.above_ref, bf16[192,384]{1,0:T(8,128)(2,1)S(1)} %get-tuple-element.84.refs_1_.mid_ref, ...), custom_call_target="tpu_custom_call" | custom-call | flops 4000000000 | bytes 12737544 | tf_op jit(solution)/shard_map/forward/pallas_call | solution.py:69
  39.3 0.8 collective-permute-done.3.below_ref
  40.2 5.0 %backward.2 = (bf16[2048,768]{1,0:T(8,128)(2,1)S(1)}, f32[192,384]{1,0:T(8,128)S(1)}) custom-call(f32[2]{0:T(128)S(1)} %add_convert_fusion.flags_ref, bf16[384,384]{1,0:T(8,128)(2,1)S(1)} %collective-permute-done.2.above_ref, bf16[384,384]{1,0:T(8,128)(2,1)S(1)} %get-tuple-element.80.grad_ref.mid_ref, bf16[384,384]{1,0:T(8,128)(2,1)S(1)} %collective-permute-done.3.below_ref, ...), custom_call_target="tpu_custom_call" | custom-call | flops 6000000000 | bytes 11943944 | tf_op jit(solution)/shard_map/backward/pallas_call | solution.py:69
  45.2 1.3 close.2
  46.5 3.1 %collective-permute-start.5 = (bf16[384,384]{1,0:T(8,128)(2,1)S(1)}, bf16[384,384]{1,0:T(8,128)(2,1)S(1)}, u32[]{:S(2)}, u32[]{:S(2)}) collective-permute-start(bf16[384,384]{1,0:T(8,128)(2,1)S(1)} %get-tuple-element.101.grad_ref.mid_ref), channel_id=1, source_target_pairs={{8,0},{16,8},{24,16},{32,24},{40,32},{48,40},{56,48},{64,56},{72,6... | collective-permute-start | bytes 884744 | tf_op jit(solution)/shard_map/ppermute | solution.py:717
  49.6 1.4 %collective-permute-start.9 = (f32[3,144,512]{2,1,0:T(8,128)S(1)}, f32[3,144,512]{2,1,0:T(8,128)S(1)}, u32[]{:S(2)}, u32[]{:S(2)}) collective-permute-start(f32[3,144,512]{2,1,0:T(8,128)S(1)} %get-tuple-element.127), channel_id=1, source_target_pairs={{0,8},{8,0},{1,9},{9,1},{2,10},{10,2},{3,11},{11,3},{4,12},{12,4},... | collective-permute-start | bytes 2654216 | tf_op jit(solution)/shard_map/ppermute | solution.py:711
  51.0 1.5 %in_weight.2 = (f32[224,512]{1,0:T(8,128)S(1)}, f32[224,512]{1,0:T(8,128)S(1)}) custom-call(s32[1]{0:T(128)} %bitcast.2.core_ref, f32[2]{0:T(128)S(1)} %add_convert_fusion.flags_ref, bf16[192,384]{1,0:T(8,128)(2,1)S(1)} %get-tuple-element.72.refs_0_.above_ref, bf16[192,384]{1,0:T(8,128)(2,1)S(1)} %get-tuple-element.73.refs_1_.mid_ref, ...), custom_call_target="tpu_custom_call" | custom-call | flops 1000000000 | bytes 4505612 | tf_op jit(solution)/shard_map/in_weight/pallas_call | solution.py:69
  52.5 1.7 %out_weight.3 = (f32[3,144,512]{2,1,0:T(8,128)S(1)}, f32[3,144,512]{2,1,0:T(8,128)S(1)}, f32[8,96]{1,0:T(8,128)S(1)}) custom-call(s32[1]{0:T(128)} %bitcast.2.core_ref, bf16[384,384]{1,0:T(8,128)(2,1)S(1)} %get-tuple-element.101.grad_ref.mid_ref, bf16[2048,768]{1,0:T(8,128)(2,1)S(1)} %get-tuple-element.106.rows_ref), custom_call_target="tpu_custom_call" | custom-call | flops 2000000000 | bytes 5213188 | tf_op jit(solution)/shard_map/out_weight/pallas_call | solution.py:69
  54.4 1.4 %weave.2 = f32[1,96,2,768]{3,2,1,0:T(2,128)} custom-call(f32[96,1536]{1,0:T(8,128)S(1)} %get-tuple-element.108.x_ref.refs_4_), custom_call_target="tpu_custom_call" | custom-call | bytes 1179648 | tf_op jit(solution)/shard_map/weave/pallas_call | solution.py:69
  55.8 0.5 collective-permute-start.7
  56.3 4.9 %backward.3 = (bf16[2048,768]{1,0:T(8,128)(2,1)S(1)}, f32[192,384]{1,0:T(8,128)S(1)}) custom-call(f32[2]{0:T(128)S(1)} %add_convert_fusion.flags_ref, bf16[384,384]{1,0:T(8,128)(2,1)S(1)} %collective-permute-done.4.above_ref, bf16[384,384]{1,0:T(8,128)(2,1)S(1)} %get-tuple-element.101.grad_ref.mid_ref, ...), custom_call_target="tpu_custom_call" | custom-call | flops 6000000000 | bytes 11943944 | tf_op jit(solution)/shard_map/backward/pallas_call | solution.py:69
  61.2 1.5 %in_weight.3 = (f32[224,512]{1,0:T(8,128)S(1)}, f32[224,512]{1,0:T(8,128)S(1)}) custom-call(s32[1]{0:T(128)} %bitcast.2.core_ref, f32[2]{0:T(128)S(1)} %add_convert_fusion.flags_ref, bf16[192,384]{1,0:T(8,128)(2,1)S(1)} %collective-permute-done.refs_0_.above_ref, bf16[192,384]{1,0:T(8,128)(2,1)S(1)} %get-tuple-element.84.refs_1_.mid_ref, ...), custom_call_target="tpu_custom_call" | custom-call | flops 1000000000 | bytes 4505612 | tf_op jit(solution)/shard_map/in_weight/pallas_call | solution.py:69
  62.7 3.0 %collective-permute-start.6 = (f32[224,512]{1,0:T(8,128)S(1)}, f32[224,512]{1,0:T(8,128)S(1)}, u32[]{:S(2)}, u32[]{:S(2)}) collective-permute-start(f32[224,512]{1,0:T(8,128)S(1)} %get-tuple-element.123), channel_id=1, source_target_pairs={{0,8},{8,0},{1,9},{9,1},{2,10},{10,2},{3,11},{11,3},{4,12},{12,4},... | collective-permute-start | bytes 1376264 | tf_op jit(solution)/shard_map/ppermute | solution.py:725
  65.7 1.2 close.3
  67.4 30.0 %all_to_all.15.shares_ref = bf16[64,88,128]{2,1,0:T(8,128)(2,1)S(1)} all-to-all(bf16[64,88,128]{2,1,0:T(8,128)(2,1)S(1)} %merge.1), channel_id=1, replica_groups=mesh['y'=4,'xl'=2,'c'=2,'z'=4,'xh'=2] {'y','xl','z','xh'}, dimensions={0} | all-to-all | bytes 2883584 | tf_op jit(solution)/shard_map/all_to_all | solution.py:734
  97.4 0.3 totals.1
  97.7 24.6 %all_to_all.16.mine_ref = bf16[64,88,128]{2,1,0:T(8,128)(2,1)S(1)} all-to-all(bf16[64,88,128]{2,1,0:T(8,128)(2,1)S(1)} %totals.1), channel_id=1, replica_groups=mesh['y'=4,'xl'=2,'c'=2,'z'=4,'xh'=2] {'y','xl','z','xh'}, dimensions={0} | all-to-all | bytes 2883584 | tf_op jit(solution)/shard_map/all_to_all | solution.py:737
  122.3 4.0 %collective-permute-start.10 = (bf16[64,88,128]{2,1,0:T(8,128)(2,1)S(1)}, bf16[64,88,128]{2,1,0:T(8,128)(2,1)S(1)}, u32[]{:S(2)}, u32[]{:S(2)}) collective-permute-start(bf16[64,88,128]{2,1,0:T(8,128)(2,1)S(1)} %all_to_all.16.mine_ref), channel_id=1, source_target_pairs={{0,8},{8,0},{1,9},{9,1},{2,10},{10,2},{3,11},{11,3},{4,12},{12,4},... | collective-permute-start | bytes 4325384 | tf_op jit(solution)/shard_map/ppermute | solution.py:738
  126.4 1.4 %weave.3 = f32[1,96,2,768]{3,2,1,0:T(2,128)} custom-call(f32[96,1536]{1,0:T(8,128)S(1)} %get-tuple-element.129.x_ref), custom_call_target="tpu_custom_call" | custom-call | bytes 1179648 | tf_op jit(solution)/shard_map/weave/pallas_call | solution.py:69
  127.8 1.7 %unpack_own.1 = (f32[2,432,512]{2,1,0:T(8,128)}, f32[2,9,96,512]{3,2,1,0:T(8,128)}) custom-call(s32[1]{0:T(128)} %bitcast.2.core_ref, bf16[64,88,128]{2,1,0:T(8,128)(2,1)S(1)} %all_to_all.16.mine_ref), custom_call_target="tpu_custom_call" | custom-call | bytes 6750212 | tf_op jit(solution)/shard_map/unpack_own/pallas_call | solution.py:69
  129.5 2.4 %unpack_other.1 = (f32[2,432,512]{2,1,0:T(8,128)}, f32[2,9,96,512]{3,2,1,0:T(8,128)}, f32[2,96,96]{2,1,0:T(8,128)}, f32[2,512]{1,0:T(2,128)}, f32[2,96]{1,0:T(2,128)}) custom-call(s32[1]{0:T(128)} %bitcast.2.core_ref, bf16[64,88,128]{2,1,0:T(8,128)(2,1)S(1)} %all_to_all.16.mine_ref, ...), custom_call_target="tpu_custom_call", output_to_operand_aliasing={{0}: (3, {}), {1}: (4, {})} | custom-call | bytes 13579012 | tf_op jit(solution)/shard_map/unpack_other/pallas_call | solution.py:69
  (49 shorter events, 0.8 us)
Async XLA Ops:
  0.6 9.1 %copy-start.15 = (f32[1,192,1,384]{3,2,1,0:T(1,128)S(1)}, f32[1,192,1,384]{3,2,1,0:T(1,128)}, u32[]{:S(2)}) copy-start(f32[1,192,1,384]{3,2,1,0:T(1,128)} %param.10) | copy-start | bytes 884740
  2.9 19.9 %all-to-all-start = ((bf16[16,24,960]{2,1,0:T(8,128)(2,1)}), bf16[16,24,960]{2,1,0:T(8,128)(2,1)S(1)}, u32[]{:S(2)}, u32[]{:S(2)}) async-start(bf16[16,24,960]{2,1,0:T(8,128)(2,1)} %payload.1), calls=%async_computation | async-start | bytes 1572864 | tf_op jit(solution)/shard_map/all_to_all | solution.py:693
  17.6 5.9 %copy-start.4 = (bf16[288,1536]{1,0:T(8,128)(2,1)S(1)}, bf16[288,1536]{1,0:T(8,128)(2,1)}, u32[]{:S(2)}) copy-start(bf16[288,1536]{1,0:T(8,128)(2,1)} %get-tuple-element.76.refs_4_) | copy-start | bytes 2654212
  17.6 5.9 %copy-start.6 = (bf16[512,448]{1,0:T(8,128)(2,1)S(1)}, bf16[512,448]{1,0:T(8,128)(2,1)}, u32[]{:S(2)}) copy-start(bf16[512,448]{1,0:T(8,128)(2,1)} %get-tuple-element.75.refs_3_) | copy-start | bytes 1376260
  17.6 5.9 %copy-start.13 = (f32[96,96]{1,0:T(8,128)S(1)}, f32[96,96]{1,0:T(8,128)}, u32[]{:S(2)}) copy-start(f32[96,96]{1,0:T(8,128)} %get-tuple-element.78.refs_6_) | copy-start | bytes 110596
  17.6 5.9 %copy-start.14 = (f32[96,8]{1,0:T(8,128)S(1)}, f32[96,8]{1,0:T(8,128)}, u32[]{:S(2)}) copy-start(f32[96,8]{1,0:T(8,128)} %get-tuple-element.77.refs_5_) | copy-start | bytes 9220
  28.7 5.4 %collective-permute-start.1 = (bf16[192,384]{1,0:T(8,128)(2,1)S(1)}, bf16[192,384]{1,0:T(8,128)(2,1)S(1)}, u32[]{:S(2)}, u32[]{:S(2)}) collective-permute-start(bf16[192,384]{1,0:T(8,128)(2,1)S(1)} %get-tuple-element.84.refs_1_.mid_ref), channel_id=1, source_target_pairs={{8,0},{16,8},{24,16},{32,24},{40,32},{48,40},{56,48},{64,56},{72,6... | collective-permute-start | bytes 442376 | tf_op jit(solution)/shard_map/ppermute | solution.py:703
  29.7 4.5 %collective-permute-start = (bf16[192,384]{1,0:T(8,128)(2,1)S(1)}, bf16[192,384]{1,0:T(8,128)(2,1)S(1)}, u32[]{:S(2)}, u32[]{:S(2)}) collective-permute-start(bf16[192,384]{1,0:T(8,128)(2,1)S(1)} %get-tuple-element.84.refs_1_.mid_ref), channel_id=1, source_target_pairs={{0,8},{8,16},{16,24},{24,32},{32,40},{40,48},{48,56},{56,64},{64,7... | collective-permute-start | bytes 442376 | tf_op jit(solution)/shard_map/ppermute | solution.py:702
  30.5 9.6 %collective-permute-start.3 = (bf16[384,384]{1,0:T(8,128)(2,1)S(1)}, bf16[384,384]{1,0:T(8,128)(2,1)S(1)}, u32[]{:S(2)}, u32[]{:S(2)}) collective-permute-start(bf16[384,384]{1,0:T(8,128)(2,1)S(1)} %get-tuple-element.80.grad_ref.mid_ref), channel_id=1, source_target_pairs={{8,0},{16,8},{24,16},{32,24},{40,32},{48,40},{56,48},{64,56},{72,6... | collective-permute-start | bytes 884744 | tf_op jit(solution)/shard_map/ppermute | solution.py:705
  30.5 9.6 %collective-permute-start.2 = (bf16[384,384]{1,0:T(8,128)(2,1)S(1)}, bf16[384,384]{1,0:T(8,128)(2,1)S(1)}, u32[]{:S(2)}, u32[]{:S(2)}) collective-permute-start(bf16[384,384]{1,0:T(8,128)(2,1)S(1)} %get-tuple-element.80.grad_ref.mid_ref), channel_id=1, source_target_pairs={{0,8},{8,16},{16,24},{24,32},{32,40},{40,48},{48,56},{56,64},{64,7... | collective-permute-start | bytes 884744 | tf_op jit(solution)/shard_map/ppermute | solution.py:704
  32.3 1.8 %copy-start.3 = (bf16[288,1536]{1,0:T(8,128)(2,1)S(1)}, bf16[288,1536]{1,0:T(8,128)(2,1)}, u32[]{:S(2)}) copy-start(bf16[288,1536]{1,0:T(8,128)(2,1)} %get-tuple-element.86.refs_4_) | copy-start | bytes 2654212
  32.3 1.8 %copy-start.5 = (bf16[512,448]{1,0:T(8,128)(2,1)S(1)}, bf16[512,448]{1,0:T(8,128)(2,1)}, u32[]{:S(2)}) copy-start(bf16[512,448]{1,0:T(8,128)(2,1)} %get-tuple-element.85.refs_3_) | copy-start | bytes 1376260
  32.3 1.8 %copy-start.11 = (f32[96,96]{1,0:T(8,128)S(1)}, f32[96,96]{1,0:T(8,128)}, u32[]{:S(2)}) copy-start(f32[96,96]{1,0:T(8,128)} %get-tuple-element.88.refs_6_) | copy-start | bytes 110596
  32.4 1.8 %copy-start.12 = (f32[96,8]{1,0:T(8,128)S(1)}, f32[96,8]{1,0:T(8,128)}, u32[]{:S(2)}) copy-start(f32[96,8]{1,0:T(8,128)} %get-tuple-element.87.refs_5_) | copy-start | bytes 9220
  34.2 6.0 %copy-start.2 = (bf16[512,864]{1,0:T(8,128)(2,1)S(1)}, bf16[512,864]{1,0:T(8,128)(2,1)}, u32[]{:S(2)}) copy-start(bf16[512,864]{1,0:T(8,128)(2,1)} %get-tuple-element.92.w2t_ref) | copy-start | bytes 2654212
  34.2 5.9 %copy-start.8 = (bf16[144,1536]{1,0:T(8,128)(2,1)S(1)}, bf16[144,1536]{1,0:T(8,128)(2,1)}, u32[]{:S(2)}) copy-start(bf16[144,1536]{1,0:T(8,128)(2,1)} %get-tuple-element.94.w1k_ref) | copy-start | bytes 1327108
  40.1 5.0 %copy-start = (f32[2,96,96]{2,1,0:T(8,128)S(1)}, f32[2,96,96]{2,1,0:T(8,128)}, u32[]{:S(2)}) copy-start(f32[2,96,96]{2,1,0:T(8,128)} %refs_5_.3) | copy-start | bytes 221188
  40.2 5.0 %copy-start.10 = (f32[96,96]{1,0:T(8,128)S(1)}, f32[96,96]{1,0:T(8,128)}, u32[]{:S(2)}) copy-start(f32[96,96]{1,0:T(8,128)} %get-tuple-element.98.refs_3_) | copy-start | bytes 110596
  46.5 9.8 %collective-permute-start.5 = (bf16[384,384]{1,0:T(8,128)(2,1)S(1)}, bf16[384,384]{1,0:T(8,128)(2,1)S(1)}, u32[]{:S(2)}, u32[]{:S(2)}) collective-permute-start(bf16[384,384]{1,0:T(8,128)(2,1)S(1)} %get-tuple-element.101.grad_ref.mid_ref), channel_id=1, source_target_pairs={{8,0},{16,8},{24,16},{32,24},{40,32},{48,40},{56,48},{64,56},{72,6... | collective-permute-start | bytes 884744 | tf_op jit(solution)/shard_map/ppermute | solution.py:717
  49.6 6.7 %collective-permute-start.4 = (bf16[384,384]{1,0:T(8,128)(2,1)S(1)}, bf16[384,384]{1,0:T(8,128)(2,1)S(1)}, u32[]{:S(2)}, u32[]{:S(2)}) collective-permute-start(bf16[384,384]{1,0:T(8,128)(2,1)S(1)} %get-tuple-element.101.grad_ref.mid_ref), channel_id=1, source_target_pairs={{0,8},{8,16},{16,24},{24,32},{32,40},{40,48},{48,56},{56,64},{64,7... | collective-permute-start | bytes 884744 | tf_op jit(solution)/shard_map/ppermute | solution.py:716
  49.6 17.4 %collective-permute-start.9 = (f32[3,144,512]{2,1,0:T(8,128)S(1)}, f32[3,144,512]{2,1,0:T(8,128)S(1)}, u32[]{:S(2)}, u32[]{:S(2)}) collective-permute-start(f32[3,144,512]{2,1,0:T(8,128)S(1)} %get-tuple-element.127), channel_id=1, source_target_pairs={{0,8},{8,0},{1,9},{9,1},{2,10},{10,2},{3,11},{11,3},{4,12},{12,4},... | collective-permute-start | bytes 2654216 | tf_op jit(solution)/shard_map/ppermute | solution.py:711
  52.5 3.8 %copy-start.1 = (bf16[512,864]{1,0:T(8,128)(2,1)S(1)}, bf16[512,864]{1,0:T(8,128)(2,1)}, u32[]{:S(2)}) copy-start(bf16[512,864]{1,0:T(8,128)(2,1)} %get-tuple-element.110.w2t_ref) | copy-start | bytes 2654212
  52.5 3.8 %copy-start.7 = (bf16[144,1536]{1,0:T(8,128)(2,1)S(1)}, bf16[144,1536]{1,0:T(8,128)(2,1)}, u32[]{:S(2)}) copy-start(bf16[144,1536]{1,0:T(8,128)(2,1)} %get-tuple-element.112.w1k_ref) | copy-start | bytes 1327108
  54.3 12.7 %collective-permute-start.8 = (f32[224,512]{1,0:T(8,128)S(1)}, f32[224,512]{1,0:T(8,128)S(1)}, u32[]{:S(2)}, u32[]{:S(2)}) collective-permute-start(f32[224,512]{1,0:T(8,128)S(1)} %get-tuple-element.126), channel_id=1, source_target_pairs={{0,8},{8,0},{1,9},{9,1},{2,10},{10,2},{3,11},{11,3},{4,12},{12,4},... | collective-permute-start | bytes 1376264 | tf_op jit(solution)/shard_map/ppermute | solution.py:719
  55.8 11.4 %collective-permute-start.7 = (f32[3,144,512]{2,1,0:T(8,128)S(1)}, f32[3,144,512]{2,1,0:T(8,128)S(1)}, u32[]{:S(2)}, u32[]{:S(2)}) collective-permute-start(f32[3,144,512]{2,1,0:T(8,128)S(1)} %get-tuple-element.124), channel_id=1, source_target_pairs={{0,8},{8,0},{1,9},{9,1},{2,10},{10,2},{3,11},{11,3},{4,12},{12,4},... | collective-permute-start | bytes 2654216 | tf_op jit(solution)/shard_map/ppermute | solution.py:723
  61.2 4.6 %copy-start.9 = (f32[96,96]{1,0:T(8,128)S(1)}, f32[96,96]{1,0:T(8,128)}, u32[]{:S(2)}) copy-start(f32[96,96]{1,0:T(8,128)} %get-tuple-element.120.refs_3_) | copy-start | bytes 110596
  62.7 4.5 %collective-permute-start.6 = (f32[224,512]{1,0:T(8,128)S(1)}, f32[224,512]{1,0:T(8,128)S(1)}, u32[]{:S(2)}, u32[]{:S(2)}) collective-permute-start(f32[224,512]{1,0:T(8,128)S(1)} %get-tuple-element.123), channel_id=1, source_target_pairs={{0,8},{8,0},{1,9},{9,1},{2,10},{10,2},{3,11},{11,3},{4,12},{12,4},... | collective-permute-start | bytes 1376264 | tf_op jit(solution)/shard_map/ppermute | solution.py:725
  122.3 7.2 %collective-permute-start.10 = (bf16[64,88,128]{2,1,0:T(8,128)(2,1)S(1)}, bf16[64,88,128]{2,1,0:T(8,128)(2,1)S(1)}, u32[]{:S(2)}, u32[]{:S(2)}) collective-permute-start(bf16[64,88,128]{2,1,0:T(8,128)(2,1)S(1)} %all_to_all.16.mine_ref), channel_id=1, source_target_pairs={{0,8},{8,0},{1,9},{9,1},{2,10},{10,2},{3,11},{11,3},{4,12},{12,4},... | collective-permute-start | bytes 4325384 | tf_op jit(solution)/shard_map/ppermute | solution.py:738

commit v4 on v3

--- a/solution.py
+++ b/solution.py
@@ -45,6 +45,16 @@
     mid = rest.astype(BF)
     low = (rest - mid.astype(F32)).astype(BF)
     return hi, mid, low
+
+
+def stack_left(m):
+    hi, mid, low = split3(m)
+    return jnp.concatenate([hi, hi, mid, hi, low, mid], axis=1)
+
+
+def mm_six(left, x):
+    hi, mid, low = split3(x)
+    return mm(left, jnp.concatenate([hi, mid, hi, low, hi, mid], axis=0))
 
 
 def from_left(x):
@@ -141,8 +151,8 @@
     inverses = [mm_high(w, b) for w, b in zip(whole, blocks)]
     for k in range(flows):
         inv_ref, lut_ref, w1t_ref, w2t_ref, w2k_ref, w1k_ref, b2c_ref = refs[7 * k : 7 * k + 7]
-        inv_ref[...] = mm_high(inverses[2 * k + 1], inverses[2 * k])
-        lut_ref[...] = mm_high(units[2 * k] + eye, units[2 * k + 1] + eye).T
+        inv_ref[...] = stack_left(mm_high(inverses[2 * k + 1], inverses[2 * k]))
+        lut_ref[...] = stack_left(mm_high(units[2 * k] + eye, units[2 * k + 1] + eye).T)
         for tap in range(9):
             stage1[tap * HALF : (tap + 1) * HALF, :] = 0.5 * w1_ref[k, tap].astype(F32)
             stage2[tap * CH : (tap + 1) * CH, :] = 0.5 * w2_ref[k, 8 - tap].astype(F32)
@@ -166,8 +176,8 @@
     outs = call(
         prep_kernel,
         [
-            sds((CH, CH), F32),
-            sds((CH, CH), F32),
+            sds((CH, 6 * CH), BF),
+            sds((CH, 6 * CH), BF),
             sds((HID, IN_ROWS), BF),
             sds((HID, 9 * CH), BF),
             sds((3 * CH, 3 * HID), BF),
@@ -310,7 +320,7 @@
     inverse = 1.0 + jnp.exp(-(raw + 2.0))
     scale = 1.0 / inverse
     moved_in = yb_ref[...] * inverse - shift
-    x = mm_high(inv_ref[...], jnp.concatenate([ya_ref[...], moved_in], axis=0))
+    x = mm_six(inv_ref[...], jnp.concatenate([ya_ref[...], moved_in], axis=0))
     x_ref[...] = x
     if with_grad:
         moved_grad = yb_ref[...]
@@ -459,7 +469,7 @@
             ga_ref[:HALF, lane : lane + COLS] + in_ref[k * HALF : (k + 1) * HALF]
         )
     whole[HALF:] = moved_ref[...]
-    gx = mm_high(lut_ref[...], whole[...])
+    gx = mm_six(lut_ref[...], whole[...])
     gx_ref[...] = gx
     if next_step:
         scale = scale_ref[...]
@@ -469,7 +479,10 @@
         put_out_grad((moved_grad * x_ref[HALF:] - 1.0) * (1.0 - scale), moved, grad_ref)
     ghi, gmid, _ = split3(whole[...])
     xhi, xmid, _ = split3(x_ref[...])
-    outer = mm_nt(ghi, xhi) + (mm_nt(ghi, xmid) + mm_nt(gmid, xhi))
+    four = mm_nt(
+        jnp.concatenate([ghi, gmid], axis=0), jnp.concatenate([xhi, xmid], axis=0)
+    )
+    outer = four[:CH, :CH] + (four[:CH, CH:] + four[CH:, :CH])
     row = lax.broadcasted_iota(jnp.int32, (CH, CH), 0)
     col = lax.broadcasted_iota(jnp.int32, (CH, CH), 1)
     eye = (row == col).astype(F32)

time: 132 us -> 132 us (level)
  transfers between devices with their start and end apart: 12 -> 12, of which waited for: 3 -> 3; matrix products, arithmetic and copies ran while one was open for 1% -> 1% of each run, Pallas kernels for 22% -> 23%
where the time goes in v4:
time: 132 us
  blocking collectives  54.6 us (41%)
  Pallas kernels  47.1 us (36%)
  starting transfers between devices  22.5 us (17%)
  waiting for transfers between devices  5.56 us (4%)
    pallas_call x19, Pallas kernels, call(): pl.pallas_call(body, out_shape=outs, in_specs=[pl.BlockSpec(memory_space=...  47.1 us
    all_to_all x1, blocking collectives, local(): shares = lax.all_to_all(packed, CHIPS, 0, 0, tiled=True)  30 us
    all_to_all x1, blocking collectives, local(): mine = lax.all_to_all(spread, CHIPS, 0, 0, tiled=True)  24.6 us
    all_to_all x1, starting transfers between devices, local(): recv = lax.all_to_all(block, LAT, 0, 0, tiled=True)  6.91 us
    all_to_all x1, waiting for transfers between devices, local(): recv = lax.all_to_all(block, LAT, 0, 0, tiled=True)  4.41 us
    ppermute x1, starting transfers between devices, local(): other = lax.ppermute(mine, 'c', swap)  4.04 us
    ppermute x1, starting transfers between devices, local(): bottom0 = lax.ppermute(grad0, LAT, back)  3.02 us
    ppermute x1, starting transfers between devices, local(): got_in0 = lax.ppermute(give_in0, 'c', swap)  3 us
  transfers between devices with their start and end apart: 12, of which 3 were waited for; matrix products, arithmetic and copies ran while one was open for 1% of the time, Pallas kernels for 23%

profile of v4, /device:TPU:1, one launch (start us, length us, event | category | flops | bytes accessed | tf_op | source)
XLA Modules:
  0.0 131.9 jit_solution(13136750361971332122)
XLA Ops:
  0.6 2.2 %payload.1 = bf16[16,24,960]{2,1,0:T(8,128)(2,1)} custom-call(f32[16,24,192]{2,1,0:T(8,128)} %bitcast.11, f32[16,24,192]{2,1,0:T(8,128)} %bitcast.12), custom_call_target="tpu_custom_call" | custom-call | bytes 1327104 | tf_op jit(solution)/shard_map/payload/pallas_call | solution.py:79
  2.9 6.9 %all-to-all-start = ((bf16[16,24,960]{2,1,0:T(8,128)(2,1)}), bf16[16,24,960]{2,1,0:T(8,128)(2,1)S(1)}, u32[]{:S(2)}, u32[]{:S(2)}) async-start(bf16[16,24,960]{2,1,0:T(8,128)(2,1)} %payload.1), calls=%async_computation | async-start | bytes 1572864 | tf_op jit(solution)/shard_map/all_to_all | solution.py:706
  9.8 0.7 reduce
  10.5 7.7 %prep.1 = (bf16[96,576]{1,0:T(8,128)(2,1)}, bf16[96,576]{1,0:T(8,128)(2,1)}, bf16[512,448]{1,0:T(8,128)(2,1)}, bf16[512,864]{1,0:T(8,128)(2,1)}, bf16[288,1536]{...) custom-call(f32[2,96,96]{2,1,0:T(8,128)} %refs_5_.3, ...), custom_call_target="tpu_custom_call" | custom-call | bytes 8522496 | tf_op jit(solution)/shard_map/prep/pallas_call | solution.py:79
  18.4 4.4 %all-to-all-done.recv_ref = bf16[16,24,960]{2,1,0:T(8,128)(2,1)S(1)} async-done(((bf16[16,24,960]{2,1,0:T(8,128)(2,1)}), bf16[16,24,960]{2,1,0:T(8,128)(2,1)S(1)}, u32[]{:S(2)}, u32[]{:S(2)}) %all-to-all-start) | async-done | bytes 737312 | tf_op jit(solution)/shard_map/all_to_all | solution.py:706
  22.8 0.7 turn.1
  23.5 5.1 %forward.2 = (f32[96,1536]{1,0:T(8,128)S(1)}, bf16[2048,768]{1,0:T(8,128)(2,1)S(1)}, f32[2048,768]{1,0:T(8,128)S(1)}, bf16[192,384]{1,0:T(8,128)(2,1)S(1)}, bf16...) custom-call(f32[2]{0:T(128)S(1)} %add_convert_fusion.flags_ref, ...), custom_call_target="tpu_custom_call" | custom-call | flops 4000000000 | bytes 13253640 | tf_op jit(solution)/shard_map/forward/pallas_call | solution.py:79
  28.6 0.9 collective-permute-start.1
  29.6 0.9 collective-permute-start
  30.5 1.7 %collective-permute-start.2 = (bf16[384,384]{1,0:T(8,128)(2,1)S(1)}, bf16[384,384]{1,0:T(8,128)(2,1)S(1)}, u32[]{:S(2)}, u32[]{:S(2)}) collective-permute-start(bf16[384,384]{1,0:T(8,128)(2,1)S(1)} %get-tuple-element.80.grad_ref.mid_ref), channel_id=1, source_target_pairs={{0,8},{8,16},{16,24},{24,32},{32,40},{40,48},{48,56},{56,64},{64,7... | collective-permute-start | bytes 884744 | tf_op jit(solution)/shard_map/ppermute | solution.py:717
  32.3 1.7 %out_weight.2 = (f32[3,144,512]{2,1,0:T(8,128)S(1)}, f32[3,144,512]{2,1,0:T(8,128)S(1)}, f32[8,96]{1,0:T(8,128)S(1)}) custom-call(s32[1]{0:T(128)} %bitcast.2.core_ref, bf16[384,384]{1,0:T(8,128)(2,1)S(1)} %get-tuple-element.80.grad_ref.mid_ref, bf16[2048,768]{1,0:T(8,128)(2,1)S(1)} %get-tuple-element.81.rows_ref), custom_call_target="tpu_custom_call" | custom-call | flops 2000000000 | bytes 5213188 | tf_op jit(solution)/shard_map/out_weight/pallas_call | solution.py:79
  34.1 5.0 %forward.3 = (f32[96,1536]{1,0:T(8,128)S(1)}, bf16[2048,768]{1,0:T(8,128)(2,1)S(1)}, f32[2048,768]{1,0:T(8,128)S(1)}, f32[48,1536]{1,0:T(8,128)S(1)}) custom-call(f32[2]{0:T(128)S(1)} %add_convert_fusion.flags_ref, bf16[192,384]{1,0:T(8,128)(2,1)S(1)} %collective-permute-done.refs_0_.above_ref, bf16[192,384]{1,0:T(8,128)(2,1)S(1)} %get-tuple-element.84.refs_1_.mid_ref, ...), custom_call_target="tpu_custom_call" | custom-call | flops 4000000000 | bytes 12811272 | tf_op jit(solution)/shard_map/forward/pallas_call | solution.py:79
  39.2 0.9 collective-permute-done.3.below_ref
  40.1 5.0 %backward.2 = (bf16[2048,768]{1,0:T(8,128)(2,1)S(1)}, f32[192,384]{1,0:T(8,128)S(1)}) custom-call(f32[2]{0:T(128)S(1)} %add_convert_fusion.flags_ref, bf16[384,384]{1,0:T(8,128)(2,1)S(1)} %collective-permute-done.2.above_ref, bf16[384,384]{1,0:T(8,128)(2,1)S(1)} %get-tuple-element.80.grad_ref.mid_ref, bf16[384,384]{1,0:T(8,128)(2,1)S(1)} %collective-permute-done.3.below_ref, ...), custom_call_target="tpu_custom_call" | custom-call | flops 6000000000 | bytes 11943944 | tf_op jit(solution)/shard_map/backward/pallas_call | solution.py:79
  45.1 1.2 close.2
  46.4 3.0 %collective-permute-start.5 = (bf16[384,384]{1,0:T(8,128)(2,1)S(1)}, bf16[384,384]{1,0:T(8,128)(2,1)S(1)}, u32[]{:S(2)}, u32[]{:S(2)}) collective-permute-start(bf16[384,384]{1,0:T(8,128)(2,1)S(1)} %get-tuple-element.101.grad_ref.mid_ref), channel_id=1, source_target_pairs={{8,0},{16,8},{24,16},{32,24},{40,32},{48,40},{56,48},{64,56},{72,6... | collective-permute-start | bytes 884744 | tf_op jit(solution)/shard_map/ppermute | solution.py:730
  49.4 1.4 %collective-permute-start.9 = (f32[3,144,512]{2,1,0:T(8,128)S(1)}, f32[3,144,512]{2,1,0:T(8,128)S(1)}, u32[]{:S(2)}, u32[]{:S(2)}) collective-permute-start(f32[3,144,512]{2,1,0:T(8,128)S(1)} %get-tuple-element.127), channel_id=1, source_target_pairs={{0,8},{8,0},{1,9},{9,1},{2,10},{10,2},{3,11},{11,3},{4,12},{12,4},... | collective-permute-start | bytes 2654216 | tf_op jit(solution)/shard_map/ppermute | solution.py:724
  50.8 1.5 %in_weight.2 = (f32[224,512]{1,0:T(8,128)S(1)}, f32[224,512]{1,0:T(8,128)S(1)}) custom-call(s32[1]{0:T(128)} %bitcast.2.core_ref, f32[2]{0:T(128)S(1)} %add_convert_fusion.flags_ref, bf16[192,384]{1,0:T(8,128)(2,1)S(1)} %get-tuple-element.72.refs_0_.above_ref, bf16[192,384]{1,0:T(8,128)(2,1)S(1)} %get-tuple-element.73.refs_1_.mid_ref, ...), custom_call_target="tpu_custom_call" | custom-call | flops 1000000000 | bytes 4505612 | tf_op jit(solution)/shard_map/in_weight/pallas_call | solution.py:79
  52.4 1.7 %out_weight.3 = (f32[3,144,512]{2,1,0:T(8,128)S(1)}, f32[3,144,512]{2,1,0:T(8,128)S(1)}, f32[8,96]{1,0:T(8,128)S(1)}) custom-call(s32[1]{0:T(128)} %bitcast.2.core_ref, bf16[384,384]{1,0:T(8,128)(2,1)S(1)} %get-tuple-element.101.grad_ref.mid_ref, bf16[2048,768]{1,0:T(8,128)(2,1)S(1)} %get-tuple-element.106.rows_ref), custom_call_target="tpu_custom_call" | custom-call | flops 2000000000 | bytes 5213188 | tf_op jit(solution)/shard_map/out_weight/pallas_call | solution.py:79
  54.2 1.4 %weave.2 = f32[1,96,2,768]{3,2,1,0:T(2,128)} custom-call(f32[96,1536]{1,0:T(8,128)S(1)} %get-tuple-element.108.x_ref.refs_4_), custom_call_target="tpu_custom_call" | custom-call | bytes 1179648 | tf_op jit(solution)/shard_map/weave/pallas_call | solution.py:79
  55.6 0.5 collective-permute-start.7
  56.1 4.9 %backward.3 = (bf16[2048,768]{1,0:T(8,128)(2,1)S(1)}, f32[192,384]{1,0:T(8,128)S(1)}) custom-call(f32[2]{0:T(128)S(1)} %add_convert_fusion.flags_ref, bf16[384,384]{1,0:T(8,128)(2,1)S(1)} %collective-permute-done.4.above_ref, bf16[384,384]{1,0:T(8,128)(2,1)S(1)} %get-tuple-element.101.grad_ref.mid_ref, ...), custom_call_target="tpu_custom_call" | custom-call | flops 6000000000 | bytes 11943944 | tf_op jit(solution)/shard_map/backward/pallas_call | solution.py:79
  61.0 1.5 %in_weight.3 = (f32[224,512]{1,0:T(8,128)S(1)}, f32[224,512]{1,0:T(8,128)S(1)}) custom-call(s32[1]{0:T(128)} %bitcast.2.core_ref, f32[2]{0:T(128)S(1)} %add_convert_fusion.flags_ref, bf16[192,384]{1,0:T(8,128)(2,1)S(1)} %collective-permute-done.refs_0_.above_ref, bf16[192,384]{1,0:T(8,128)(2,1)S(1)} %get-tuple-element.84.refs_1_.mid_ref, ...), custom_call_target="tpu_custom_call" | custom-call | flops 1000000000 | bytes 4505612 | tf_op jit(solution)/shard_map/in_weight/pallas_call | solution.py:79
  62.6 3.0 %collective-permute-start.6 = (f32[224,512]{1,0:T(8,128)S(1)}, f32[224,512]{1,0:T(8,128)S(1)}, u32[]{:S(2)}, u32[]{:S(2)}) collective-permute-start(f32[224,512]{1,0:T(8,128)S(1)} %get-tuple-element.123), channel_id=1, source_target_pairs={{0,8},{8,0},{1,9},{9,1},{2,10},{10,2},{3,11},{11,3},{4,12},{12,4},... | collective-permute-start | bytes 1376264 | tf_op jit(solution)/shard_map/ppermute | solution.py:738
  65.6 1.2 close.3
  67.3 30.0 %all_to_all.15.shares_ref = bf16[64,88,128]{2,1,0:T(8,128)(2,1)S(1)} all-to-all(bf16[64,88,128]{2,1,0:T(8,128)(2,1)S(1)} %merge.1), channel_id=1, replica_groups=mesh['y'=4,'xl'=2,'c'=2,'z'=4,'xh'=2] {'y','xl','z','xh'}, dimensions={0} | all-to-all | bytes 2883584 | tf_op jit(solution)/shard_map/all_to_all | solution.py:747
  97.3 0.3 totals.1
  97.6 24.6 %all_to_all.16.mine_ref = bf16[64,88,128]{2,1,0:T(8,128)(2,1)S(1)} all-to-all(bf16[64,88,128]{2,1,0:T(8,128)(2,1)S(1)} %totals.1), channel_id=1, replica_groups=mesh['y'=4,'xl'=2,'c'=2,'z'=4,'xh'=2] {'y','xl','z','xh'}, dimensions={0} | all-to-all | bytes 2883584 | tf_op jit(solution)/shard_map/all_to_all | solution.py:750
  122.2 4.0 %collective-permute-start.10 = (bf16[64,88,128]{2,1,0:T(8,128)(2,1)S(1)}, bf16[64,88,128]{2,1,0:T(8,128)(2,1)S(1)}, u32[]{:S(2)}, u32[]{:S(2)}) collective-permute-start(bf16[64,88,128]{2,1,0:T(8,128)(2,1)S(1)} %all_to_all.16.mine_ref), channel_id=1, source_target_pairs={{0,8},{8,0},{1,9},{9,1},{2,10},{10,2},{3,11},{11,3},{4,12},{12,4},... | collective-permute-start | bytes 4325384 | tf_op jit(solution)/shard_map/ppermute | solution.py:751
  126.2 1.4 %weave.3 = f32[1,96,2,768]{3,2,1,0:T(2,128)} custom-call(f32[96,1536]{1,0:T(8,128)S(1)} %get-tuple-element.129.x_ref), custom_call_target="tpu_custom_call" | custom-call | bytes 1179648 | tf_op jit(solution)/shard_map/weave/pallas_call | solution.py:79
  127.6 1.7 %unpack_own.1 = (f32[2,432,512]{2,1,0:T(8,128)}, f32[2,9,96,512]{3,2,1,0:T(8,128)}) custom-call(s32[1]{0:T(128)} %bitcast.2.core_ref, bf16[64,88,128]{2,1,0:T(8,128)(2,1)S(1)} %all_to_all.16.mine_ref), custom_call_target="tpu_custom_call" | custom-call | bytes 6750212 | tf_op jit(solution)/shard_map/unpack_own/pallas_call | solution.py:79
  129.3 2.4 %unpack_other.1 = (f32[2,432,512]{2,1,0:T(8,128)}, f32[2,9,96,512]{3,2,1,0:T(8,128)}, f32[2,96,96]{2,1,0:T(8,128)}, f32[2,512]{1,0:T(2,128)}, f32[2,96]{1,0:T(2,128)}) custom-call(s32[1]{0:T(128)} %bitcast.2.core_ref, bf16[64,88,128]{2,1,0:T(8,128)(2,1)S(1)} %all_to_all.16.mine_ref, ...), custom_call_target="tpu_custom_call", output_to_operand_aliasing={{0}: (3, {}), {1}: (4, {})} | custom-call | bytes 13579012 | tf_op jit(solution)/shard_map/unpack_other/pallas_call | solution.py:79
  (49 shorter events, 0.9 us)
Async XLA Ops:
  0.6 9.1 %copy-start.15 = (f32[1,192,1,384]{3,2,1,0:T(1,128)S(1)}, f32[1,192,1,384]{3,2,1,0:T(1,128)}, u32[]{:S(2)}) copy-start(f32[1,192,1,384]{3,2,1,0:T(1,128)} %param.10) | copy-start | bytes 884740
  2.9 19.9 %all-to-all-start = ((bf16[16,24,960]{2,1,0:T(8,128)(2,1)}), bf16[16,24,960]{2,1,0:T(8,128)(2,1)S(1)}, u32[]{:S(2)}, u32[]{:S(2)}) async-start(bf16[16,24,960]{2,1,0:T(8,128)(2,1)} %payload.1), calls=%async_computation | async-start | bytes 1572864 | tf_op jit(solution)/shard_map/all_to_all | solution.py:706
  18.3 5.2 %copy-start.4 = (bf16[288,1536]{1,0:T(8,128)(2,1)S(1)}, bf16[288,1536]{1,0:T(8,128)(2,1)}, u32[]{:S(2)}) copy-start(bf16[288,1536]{1,0:T(8,128)(2,1)} %get-tuple-element.76.refs_4_) | copy-start | bytes 2654212
  18.3 5.2 %copy-start.6 = (bf16[512,448]{1,0:T(8,128)(2,1)S(1)}, bf16[512,448]{1,0:T(8,128)(2,1)}, u32[]{:S(2)}) copy-start(bf16[512,448]{1,0:T(8,128)(2,1)} %get-tuple-element.75.refs_3_) | copy-start | bytes 1376260
  18.3 5.2 %copy-start.12 = (bf16[96,576]{1,0:T(8,128)(2,1)S(1)}, bf16[96,576]{1,0:T(8,128)(2,1)}, u32[]{:S(2)}) copy-start(bf16[96,576]{1,0:T(8,128)(2,1)} %get-tuple-element.78.refs_6_) | copy-start | bytes 331780
  18.3 5.2 %copy-start.14 = (f32[96,8]{1,0:T(8,128)S(1)}, f32[96,8]{1,0:T(8,128)}, u32[]{:S(2)}) copy-start(f32[96,8]{1,0:T(8,128)} %get-tuple-element.77.refs_5_) | copy-start | bytes 9220
  28.6 5.4 %collective-permute-start.1 = (bf16[192,384]{1,0:T(8,128)(2,1)S(1)}, bf16[192,384]{1,0:T(8,128)(2,1)S(1)}, u32[]{:S(2)}, u32[]{:S(2)}) collective-permute-start(bf16[192,384]{1,0:T(8,128)(2,1)S(1)} %get-tuple-element.84.refs_1_.mid_ref), channel_id=1, source_target_pairs={{8,0},{16,8},{24,16},{32,24},{40,32},{48,40},{56,48},{64,56},{72,6... | collective-permute-start | bytes 442376 | tf_op jit(solution)/shard_map/ppermute | solution.py:716
  29.6 4.5 %collective-permute-start = (bf16[192,384]{1,0:T(8,128)(2,1)S(1)}, bf16[192,384]{1,0:T(8,128)(2,1)S(1)}, u32[]{:S(2)}, u32[]{:S(2)}) collective-permute-start(bf16[192,384]{1,0:T(8,128)(2,1)S(1)} %get-tuple-element.84.refs_1_.mid_ref), channel_id=1, source_target_pairs={{0,8},{8,16},{16,24},{24,32},{32,40},{40,48},{48,56},{56,64},{64,7... | collective-permute-start | bytes 442376 | tf_op jit(solution)/shard_map/ppermute | solution.py:715
  30.5 9.6 %collective-permute-start.3 = (bf16[384,384]{1,0:T(8,128)(2,1)S(1)}, bf16[384,384]{1,0:T(8,128)(2,1)S(1)}, u32[]{:S(2)}, u32[]{:S(2)}) collective-permute-start(bf16[384,384]{1,0:T(8,128)(2,1)S(1)} %get-tuple-element.80.grad_ref.mid_ref), channel_id=1, source_target_pairs={{8,0},{16,8},{24,16},{32,24},{40,32},{48,40},{56,48},{64,56},{72,6... | collective-permute-start | bytes 884744 | tf_op jit(solution)/shard_map/ppermute | solution.py:718
  30.5 9.6 %collective-permute-start.2 = (bf16[384,384]{1,0:T(8,128)(2,1)S(1)}, bf16[384,384]{1,0:T(8,128)(2,1)S(1)}, u32[]{:S(2)}, u32[]{:S(2)}) collective-permute-start(bf16[384,384]{1,0:T(8,128)(2,1)S(1)} %get-tuple-element.80.grad_ref.mid_ref), channel_id=1, source_target_pairs={{0,8},{8,16},{16,24},{24,32},{32,40},{40,48},{48,56},{56,64},{64,7... | collective-permute-start | bytes 884744 | tf_op jit(solution)/shard_map/ppermute | solution.py:717
  32.2 1.8 %copy-start.3 = (bf16[288,1536]{1,0:T(8,128)(2,1)S(1)}, bf16[288,1536]{1,0:T(8,128)(2,1)}, u32[]{:S(2)}) copy-start(bf16[288,1536]{1,0:T(8,128)(2,1)} %get-tuple-element.86.refs_4_) | copy-start | bytes 2654212
  32.3 1.8 %copy-start.5 = (bf16[512,448]{1,0:T(8,128)(2,1)S(1)}, bf16[512,448]{1,0:T(8,128)(2,1)}, u32[]{:S(2)}) copy-start(bf16[512,448]{1,0:T(8,128)(2,1)} %get-tuple-element.85.refs_3_) | copy-start | bytes 1376260
  32.3 1.8 %copy-start.11 = (bf16[96,576]{1,0:T(8,128)(2,1)S(1)}, bf16[96,576]{1,0:T(8,128)(2,1)}, u32[]{:S(2)}) copy-start(bf16[96,576]{1,0:T(8,128)(2,1)} %get-tuple-element.88.refs_6_) | copy-start | bytes 331780
  32.3 1.8 %copy-start.13 = (f32[96,8]{1,0:T(8,128)S(1)}, f32[96,8]{1,0:T(8,128)}, u32[]{:S(2)}) copy-start(f32[96,8]{1,0:T(8,128)} %get-tuple-element.87.refs_5_) | copy-start | bytes 9220
  34.1 6.0 %copy-start.2 = (bf16[512,864]{1,0:T(8,128)(2,1)S(1)}, bf16[512,864]{1,0:T(8,128)(2,1)}, u32[]{:S(2)}) copy-start(bf16[512,864]{1,0:T(8,128)(2,1)} %get-tuple-element.92.w2t_ref) | copy-start | bytes 2654212
  34.1 5.9 %copy-start.8 = (bf16[144,1536]{1,0:T(8,128)(2,1)S(1)}, bf16[144,1536]{1,0:T(8,128)(2,1)}, u32[]{:S(2)}) copy-start(bf16[144,1536]{1,0:T(8,128)(2,1)} %get-tuple-element.94.w1k_ref) | copy-start | bytes 1327108
  40.1 5.0 %copy-start = (f32[2,96,96]{2,1,0:T(8,128)S(1)}, f32[2,96,96]{2,1,0:T(8,128)}, u32[]{:S(2)}) copy-start(f32[2,96,96]{2,1,0:T(8,128)} %refs_5_.3) | copy-start | bytes 221188
  40.1 5.0 %copy-start.10 = (bf16[96,576]{1,0:T(8,128)(2,1)S(1)}, bf16[96,576]{1,0:T(8,128)(2,1)}, u32[]{:S(2)}) copy-start(bf16[96,576]{1,0:T(8,128)(2,1)} %get-tuple-element.98.refs_3_) | copy-start | bytes 331780
  46.4 9.8 %collective-permute-start.5 = (bf16[384,384]{1,0:T(8,128)(2,1)S(1)}, bf16[384,384]{1,0:T(8,128)(2,1)S(1)}, u32[]{:S(2)}, u32[]{:S(2)}) collective-permute-start(bf16[384,384]{1,0:T(8,128)(2,1)S(1)} %get-tuple-element.101.grad_ref.mid_ref), channel_id=1, source_target_pairs={{8,0},{16,8},{24,16},{32,24},{40,32},{48,40},{56,48},{64,56},{72,6... | collective-permute-start | bytes 884744 | tf_op jit(solution)/shard_map/ppermute | solution.py:730
  49.4 6.8 %collective-permute-start.4 = (bf16[384,384]{1,0:T(8,128)(2,1)S(1)}, bf16[384,384]{1,0:T(8,128)(2,1)S(1)}, u32[]{:S(2)}, u32[]{:S(2)}) collective-permute-start(bf16[384,384]{1,0:T(8,128)(2,1)S(1)} %get-tuple-element.101.grad_ref.mid_ref), channel_id=1, source_target_pairs={{0,8},{8,16},{16,24},{24,32},{32,40},{40,48},{48,56},{56,64},{64,7... | collective-permute-start | bytes 884744 | tf_op jit(solution)/shard_map/ppermute | solution.py:729
  49.4 17.4 %collective-permute-start.9 = (f32[3,144,512]{2,1,0:T(8,128)S(1)}, f32[3,144,512]{2,1,0:T(8,128)S(1)}, u32[]{:S(2)}, u32[]{:S(2)}) collective-permute-start(f32[3,144,512]{2,1,0:T(8,128)S(1)} %get-tuple-element.127), channel_id=1, source_target_pairs={{0,8},{8,0},{1,9},{9,1},{2,10},{10,2},{3,11},{11,3},{4,12},{12,4},... | collective-permute-start | bytes 2654216 | tf_op jit(solution)/shard_map/ppermute | solution.py:724
  52.3 3.8 %copy-start.1 = (bf16[512,864]{1,0:T(8,128)(2,1)S(1)}, bf16[512,864]{1,0:T(8,128)(2,1)}, u32[]{:S(2)}) copy-start(bf16[512,864]{1,0:T(8,128)(2,1)} %get-tuple-element.110.w2t_ref) | copy-start | bytes 2654212
  52.4 3.8 %copy-start.7 = (bf16[144,1536]{1,0:T(8,128)(2,1)S(1)}, bf16[144,1536]{1,0:T(8,128)(2,1)}, u32[]{:S(2)}) copy-start(bf16[144,1536]{1,0:T(8,128)(2,1)} %get-tuple-element.112.w1k_ref) | copy-start | bytes 1327108
  54.1 12.6 %collective-permute-start.8 = (f32[224,512]{1,0:T(8,128)S(1)}, f32[224,512]{1,0:T(8,128)S(1)}, u32[]{:S(2)}, u32[]{:S(2)}) collective-permute-start(f32[224,512]{1,0:T(8,128)S(1)} %get-tuple-element.126), channel_id=1, source_target_pairs={{0,8},{8,0},{1,9},{9,1},{2,10},{10,2},{3,11},{11,3},{4,12},{12,4},... | collective-permute-start | bytes 1376264 | tf_op jit(solution)/shard_map/ppermute | solution.py:732
  55.6 11.4 %collective-permute-start.7 = (f32[3,144,512]{2,1,0:T(8,128)S(1)}, f32[3,144,512]{2,1,0:T(8,128)S(1)}, u32[]{:S(2)}, u32[]{:S(2)}) collective-permute-start(f32[3,144,512]{2,1,0:T(8,128)S(1)} %get-tuple-element.124), channel_id=1, source_target_pairs={{0,8},{8,0},{1,9},{9,1},{2,10},{10,2},{3,11},{11,3},{4,12},{12,4},... | collective-permute-start | bytes 2654216 | tf_op jit(solution)/shard_map/ppermute | solution.py:736
  61.0 4.6 %copy-start.9 = (bf16[96,576]{1,0:T(8,128)(2,1)S(1)}, bf16[96,576]{1,0:T(8,128)(2,1)}, u32[]{:S(2)}) copy-start(bf16[96,576]{1,0:T(8,128)(2,1)} %get-tuple-element.120.refs_3_) | copy-start | bytes 331780
  62.6 4.4 %collective-permute-start.6 = (f32[224,512]{1,0:T(8,128)S(1)}, f32[224,512]{1,0:T(8,128)S(1)}, u32[]{:S(2)}, u32[]{:S(2)}) collective-permute-start(f32[224,512]{1,0:T(8,128)S(1)} %get-tuple-element.123), channel_id=1, source_target_pairs={{0,8},{8,0},{1,9},{9,1},{2,10},{10,2},{3,11},{11,3},{4,12},{12,4},... | collective-permute-start | bytes 1376264 | tf_op jit(solution)/shard_map/ppermute | solution.py:738
  122.2 7.2 %collective-permute-start.10 = (bf16[64,88,128]{2,1,0:T(8,128)(2,1)S(1)}, bf16[64,88,128]{2,1,0:T(8,128)(2,1)S(1)}, u32[]{:S(2)}, u32[]{:S(2)}) collective-permute-start(bf16[64,88,128]{2,1,0:T(8,128)(2,1)S(1)} %all_to_all.16.mine_ref), channel_id=1, source_target_pairs={{0,8},{8,0},{1,9},{9,1},{2,10},{10,2},{3,11},{11,3},{4,12},{12,4},... | collective-permute-start | bytes 4325384 | tf_op jit(solution)/shard_map/ppermute | solution.py:751

commit v5 on v3

--- a/solution.py
+++ b/solution.py
@@ -612,8 +612,9 @@
                     copy.wait()
 
 
-def unpack_own_kernel(core_ref, mine_ref, win_ref, wout_ref, rows, sems):
+def unpack_own_kernel(core_ref, mine_ref, x_ref, win_ref, wout_ref, woven_ref, rows, sems):
     put_half(core_ref[0], mine_ref, rows, win_ref, wout_ref, sems)
+    weave_kernel(x_ref, woven_ref)
     wait_half(core_ref[0], rows, win_ref, wout_ref, sems)
 
 
@@ -647,11 +648,11 @@
 KERNEL_GRADS = [((2, 9 * HALF, HID), F32), ((2, 9, CH, HID), F32)]
 
 
-def unpack_own(core, mine):
+def unpack_own(core, mine, x):
     return call(
         unpack_own_kernel,
-        [sds(*x) for x in KERNEL_GRADS],
-        [core, mine],
+        [sds(*x) for x in KERNEL_GRADS] + [sds((1, CH, 2, ROW), F32)],
+        [core, mine, x],
         scratch=[pltpu.VMEM((2 * FLOW_ROWS, HID), F32), pltpu.SemaphoreType.DMA((14,))],
         smem=(0,),
         hbm_outs=(0, 1),
@@ -736,8 +737,7 @@
     spread = totals(shares, cells)
     mine = lax.all_to_all(spread, CHIPS, 0, 0, tiled=True)
     other = lax.ppermute(mine, "c", swap)
-    win, wout = unpack_own(core, mine)
-    input_grad = weave(after(gx0, mine))
+    win, wout, input_grad = unpack_own(core, mine, gx0)
     in_grad, out_grad, mix_grad, in_bias_grad, out_bias_grad = unpack_other(
         core, mine, other, win, wout
     )

time: 132 us -> 132 us (level)
    pallas_call x19 -> x18, Pallas kernels: 46.6 us -> 46.5 us  [call(): pl.pallas_call(body, out_shape=outs, in_specs=[pl.BlockSpec(memory_space=...]
where the time goes in v5:
time: 132 us
  blocking collectives  54.6 us (41%)
  Pallas kernels  46.5 us (35%)
  starting transfers between devices  22.6 us (17%)
  waiting for transfers between devices  6.12 us (5%)
    pallas_call x18, Pallas kernels, call(): pl.pallas_call(body, out_shape=outs, in_specs=[pl.BlockSpec(memory_space=...  46.5 us
    all_to_all x1, blocking collectives, local(): shares = lax.all_to_all(packed, CHIPS, 0, 0, tiled=True)  30 us
    all_to_all x1, blocking collectives, local(): mine = lax.all_to_all(spread, CHIPS, 0, 0, tiled=True)  24.6 us
    all_to_all x1, starting transfers between devices, local(): recv = lax.all_to_all(block, LAT, 0, 0, tiled=True)  6.91 us
    all_to_all x1, waiting for transfers between devices, local(): recv = lax.all_to_all(block, LAT, 0, 0, tiled=True)  5.11 us
    ppermute x1, starting transfers between devices, local(): other = lax.ppermute(mine, 'c', swap)  4.04 us
    ppermute x1, starting transfers between devices, local(): bottom0 = lax.ppermute(grad0, LAT, back)  3.09 us
    ppermute x1, starting transfers between devices, local(): got_in0 = lax.ppermute(give_in0, 'c', swap)  3.01 us
  transfers between devices with their start and end apart: 12, of which 3 were waited for; matrix products, arithmetic and copies ran while one was open for 1% of the time, Pallas kernels for 22%

profile of v5, /device:TPU:1, one launch (start us, length us, event | category | flops | bytes accessed | tf_op | source)
XLA Modules:
  0.0 132.0 jit_solution(17211545486800678418)
XLA Ops:
  0.6 2.2 %payload.1 = bf16[16,24,960]{2,1,0:T(8,128)(2,1)} custom-call(f32[16,24,192]{2,1,0:T(8,128)} %bitcast.11, f32[16,24,192]{2,1,0:T(8,128)} %bitcast.12), custom_call_target="tpu_custom_call" | custom-call | bytes 1327104 | tf_op jit(solution)/shard_map/payload/pallas_call | solution.py:69
  2.9 6.9 %all-to-all-start = ((bf16[16,24,960]{2,1,0:T(8,128)(2,1)}), bf16[16,24,960]{2,1,0:T(8,128)(2,1)S(1)}, u32[]{:S(2)}, u32[]{:S(2)}) async-start(bf16[16,24,960]{2,1,0:T(8,128)(2,1)} %payload.1), calls=%async_computation | async-start | bytes 1572864 | tf_op jit(solution)/shard_map/all_to_all | solution.py:694
  9.8 0.7 reduce
  10.5 7.0 %prep.1 = (f32[96,96]{1,0:T(8,128)}, f32[96,96]{1,0:T(8,128)}, bf16[512,448]{1,0:T(8,128)(2,1)}, bf16[512,864]{1,0:T(8,128)(2,1)}, bf16[288,1536]{1,0:T(8,128)(2...) custom-call(f32[2,96,96]{2,1,0:T(8,128)} %refs_5_.3, ...), custom_call_target="tpu_custom_call" | custom-call | bytes 8227584 | tf_op jit(solution)/shard_map/prep/pallas_call | solution.py:69
  17.6 5.1 %all-to-all-done.recv_ref = bf16[16,24,960]{2,1,0:T(8,128)(2,1)S(1)} async-done(((bf16[16,24,960]{2,1,0:T(8,128)(2,1)}), bf16[16,24,960]{2,1,0:T(8,128)(2,1)S(1)}, u32[]{:S(2)}, u32[]{:S(2)}) %all-to-all-start) | async-done | bytes 737312 | tf_op jit(solution)/shard_map/all_to_all | solution.py:694
  22.8 0.7 turn.1
  23.5 5.2 %forward.2 = (f32[96,1536]{1,0:T(8,128)S(1)}, bf16[2048,768]{1,0:T(8,128)(2,1)S(1)}, f32[2048,768]{1,0:T(8,128)S(1)}, bf16[192,384]{1,0:T(8,128)(2,1)S(1)}, bf16...) custom-call(f32[2]{0:T(128)S(1)} %add_convert_fusion.flags_ref, ...), custom_call_target="tpu_custom_call" | custom-call | flops 4000000000 | bytes 13179912 | tf_op jit(solution)/shard_map/forward/pallas_call | solution.py:69
  28.7 0.9 collective-permute-start.1
  29.7 0.9 collective-permute-start
  30.5 1.7 %collective-permute-start.2 = (bf16[384,384]{1,0:T(8,128)(2,1)S(1)}, bf16[384,384]{1,0:T(8,128)(2,1)S(1)}, u32[]{:S(2)}, u32[]{:S(2)}) collective-permute-start(bf16[384,384]{1,0:T(8,128)(2,1)S(1)} %get-tuple-element.80.grad_ref.mid_ref), channel_id=1, source_target_pairs={{0,8},{8,16},{16,24},{24,32},{32,40},{40,48},{48,56},{56,64},{64,7... | collective-permute-start | bytes 884744 | tf_op jit(solution)/shard_map/ppermute | solution.py:705
  32.4 1.7 %out_weight.2 = (f32[3,144,512]{2,1,0:T(8,128)S(1)}, f32[3,144,512]{2,1,0:T(8,128)S(1)}, f32[8,96]{1,0:T(8,128)S(1)}) custom-call(s32[1]{0:T(128)} %bitcast.2.core_ref, bf16[384,384]{1,0:T(8,128)(2,1)S(1)} %get-tuple-element.80.grad_ref.mid_ref, bf16[2048,768]{1,0:T(8,128)(2,1)S(1)} %get-tuple-element.81.rows_ref), custom_call_target="tpu_custom_call" | custom-call | flops 2000000000 | bytes 5213188 | tf_op jit(solution)/shard_map/out_weight/pallas_call | solution.py:69
  34.2 5.1 %forward.3 = (f32[96,1536]{1,0:T(8,128)S(1)}, bf16[2048,768]{1,0:T(8,128)(2,1)S(1)}, f32[2048,768]{1,0:T(8,128)S(1)}, f32[48,1536]{1,0:T(8,128)S(1)}) custom-call(f32[2]{0:T(128)S(1)} %add_convert_fusion.flags_ref, bf16[192,384]{1,0:T(8,128)(2,1)S(1)} %collective-permute-done.refs_0_.above_ref, bf16[192,384]{1,0:T(8,128)(2,1)S(1)} %get-tuple-element.84.refs_1_.mid_ref, ...), custom_call_target="tpu_custom_call" | custom-call | flops 4000000000 | bytes 12737544 | tf_op jit(solution)/shard_map/forward/pallas_call | solution.py:69
  39.3 0.8 collective-permute-done.3.below_ref
  40.2 5.0 %backward.2 = (bf16[2048,768]{1,0:T(8,128)(2,1)S(1)}, f32[192,384]{1,0:T(8,128)S(1)}) custom-call(f32[2]{0:T(128)S(1)} %add_convert_fusion.flags_ref, bf16[384,384]{1,0:T(8,128)(2,1)S(1)} %collective-permute-done.2.above_ref, bf16[384,384]{1,0:T(8,128)(2,1)S(1)} %get-tuple-element.80.grad_ref.mid_ref, bf16[384,384]{1,0:T(8,128)(2,1)S(1)} %collective-permute-done.3.below_ref, ...), custom_call_target="tpu_custom_call" | custom-call | flops 6000000000 | bytes 11943944 | tf_op jit(solution)/shard_map/backward/pallas_call | solution.py:69
  45.2 1.3 close.2
  46.5 3.1 %collective-permute-start.5 = (bf16[384,384]{1,0:T(8,128)(2,1)S(1)}, bf16[384,384]{1,0:T(8,128)(2,1)S(1)}, u32[]{:S(2)}, u32[]{:S(2)}) collective-permute-start(bf16[384,384]{1,0:T(8,128)(2,1)S(1)} %get-tuple-element.101.grad_ref.mid_ref), channel_id=1, source_target_pairs={{8,0},{16,8},{24,16},{32,24},{40,32},{48,40},{56,48},{64,56},{72,6... | collective-permute-start | bytes 884744 | tf_op jit(solution)/shard_map/ppermute | solution.py:718
  49.6 1.4 %collective-permute-start.9 = (f32[3,144,512]{2,1,0:T(8,128)S(1)}, f32[3,144,512]{2,1,0:T(8,128)S(1)}, u32[]{:S(2)}, u32[]{:S(2)}) collective-permute-start(f32[3,144,512]{2,1,0:T(8,128)S(1)} %get-tuple-element.126), channel_id=1, source_target_pairs={{0,8},{8,0},{1,9},{9,1},{2,10},{10,2},{3,11},{11,3},{4,12},{12,4},... | collective-permute-start | bytes 2654216 | tf_op jit(solution)/shard_map/ppermute | solution.py:712
  51.0 1.5 %in_weight.2 = (f32[224,512]{1,0:T(8,128)S(1)}, f32[224,512]{1,0:T(8,128)S(1)}) custom-call(s32[1]{0:T(128)} %bitcast.2.core_ref, f32[2]{0:T(128)S(1)} %add_convert_fusion.flags_ref, bf16[192,384]{1,0:T(8,128)(2,1)S(1)} %get-tuple-element.72.refs_0_.above_ref, bf16[192,384]{1,0:T(8,128)(2,1)S(1)} %get-tuple-element.73.refs_1_.mid_ref, ...), custom_call_target="tpu_custom_call" | custom-call | flops 1000000000 | bytes 4505612 | tf_op jit(solution)/shard_map/in_weight/pallas_call | solution.py:69
  52.5 1.7 %out_weight.3 = (f32[3,144,512]{2,1,0:T(8,128)S(1)}, f32[3,144,512]{2,1,0:T(8,128)S(1)}, f32[8,96]{1,0:T(8,128)S(1)}) custom-call(s32[1]{0:T(128)} %bitcast.2.core_ref, bf16[384,384]{1,0:T(8,128)(2,1)S(1)} %get-tuple-element.101.grad_ref.mid_ref, bf16[2048,768]{1,0:T(8,128)(2,1)S(1)} %get-tuple-element.106.rows_ref), custom_call_target="tpu_custom_call" | custom-call | flops 2000000000 | bytes 5213188 | tf_op jit(solution)/shard_map/out_weight/pallas_call | solution.py:69
  54.4 1.4 %weave.1 = f32[1,96,2,768]{3,2,1,0:T(2,128)} custom-call(f32[96,1536]{1,0:T(8,128)S(1)} %get-tuple-element.108.x_ref.refs_4_), custom_call_target="tpu_custom_call" | custom-call | bytes 1179648 | tf_op jit(solution)/shard_map/weave/pallas_call | solution.py:69
  55.8 0.5 collective-permute-start.7
  56.3 4.9 %backward.3 = (bf16[2048,768]{1,0:T(8,128)(2,1)S(1)}, f32[192,384]{1,0:T(8,128)S(1)}) custom-call(f32[2]{0:T(128)S(1)} %add_convert_fusion.flags_ref, bf16[384,384]{1,0:T(8,128)(2,1)S(1)} %collective-permute-done.4.above_ref, bf16[384,384]{1,0:T(8,128)(2,1)S(1)} %get-tuple-element.101.grad_ref.mid_ref, ...), custom_call_target="tpu_custom_call" | custom-call | flops 6000000000 | bytes 11943944 | tf_op jit(solution)/shard_map/backward/pallas_call | solution.py:69
  61.2 1.5 %in_weight.3 = (f32[224,512]{1,0:T(8,128)S(1)}, f32[224,512]{1,0:T(8,128)S(1)}) custom-call(s32[1]{0:T(128)} %bitcast.2.core_ref, f32[2]{0:T(128)S(1)} %add_convert_fusion.flags_ref, bf16[192,384]{1,0:T(8,128)(2,1)S(1)} %collective-permute-done.refs_0_.above_ref, bf16[192,384]{1,0:T(8,128)(2,1)S(1)} %get-tuple-element.84.refs_1_.mid_ref, ...), custom_call_target="tpu_custom_call" | custom-call | flops 1000000000 | bytes 4505612 | tf_op jit(solution)/shard_map/in_weight/pallas_call | solution.py:69
  62.7 3.0 %collective-permute-start.6 = (f32[224,512]{1,0:T(8,128)S(1)}, f32[224,512]{1,0:T(8,128)S(1)}, u32[]{:S(2)}, u32[]{:S(2)}) collective-permute-start(f32[224,512]{1,0:T(8,128)S(1)} %get-tuple-element.117), channel_id=1, source_target_pairs={{0,8},{8,0},{1,9},{9,1},{2,10},{10,2},{3,11},{11,3},{4,12},{12,4},... | collective-permute-start | bytes 1376264 | tf_op jit(solution)/shard_map/ppermute | solution.py:726
  65.7 1.2 close.3
  67.2 0.3 merge.1
  67.4 30.0 %all_to_all.15.shares_ref = bf16[64,88,128]{2,1,0:T(8,128)(2,1)S(1)} all-to-all(bf16[64,88,128]{2,1,0:T(8,128)(2,1)S(1)} %merge.1), channel_id=1, replica_groups=mesh['y'=4,'xl'=2,'c'=2,'z'=4,'xh'=2] {'y','xl','z','xh'}, dimensions={0} | all-to-all | bytes 2883584 | tf_op jit(solution)/shard_map/all_to_all | solution.py:735
  97.4 0.3 totals.1
  97.7 24.6 %all_to_all.16.mine_ref = bf16[64,88,128]{2,1,0:T(8,128)(2,1)S(1)} all-to-all(bf16[64,88,128]{2,1,0:T(8,128)(2,1)S(1)} %totals.1), channel_id=1, replica_groups=mesh['y'=4,'xl'=2,'c'=2,'z'=4,'xh'=2] {'y','xl','z','xh'}, dimensions={0} | all-to-all | bytes 2883584 | tf_op jit(solution)/shard_map/all_to_all | solution.py:738
  122.3 4.0 %collective-permute-start.10 = (bf16[64,88,128]{2,1,0:T(8,128)(2,1)S(1)}, bf16[64,88,128]{2,1,0:T(8,128)(2,1)S(1)}, u32[]{:S(2)}, u32[]{:S(2)}) collective-permute-start(bf16[64,88,128]{2,1,0:T(8,128)(2,1)S(1)} %all_to_all.16.mine_ref), channel_id=1, source_target_pairs={{0,8},{8,0},{1,9},{9,1},{2,10},{10,2},{3,11},{11,3},{4,12},{12,4},... | collective-permute-start | bytes 4325384 | tf_op jit(solution)/shard_map/ppermute | solution.py:739
  126.4 3.0 %unpack_own.1 = (f32[2,432,512]{2,1,0:T(8,128)}, f32[2,9,96,512]{3,2,1,0:T(8,128)}, f32[1,96,2,768]{3,2,1,0:T(2,128)}) custom-call(s32[1]{0:T(128)} %bitcast.2.core_ref, bf16[64,88,128]{2,1,0:T(8,128)(2,1)S(1)} %all_to_all.16.mine_ref, f32[96,1536]{1,0:T(8,128)S(1)} %get-tuple-element.128.x_ref), custom_call_target="tpu_custom_call" | custom-call | bytes 7929860 | tf_op jit(solution)/shard_map/unpack_own/pallas_call | solution.py:69
  129.4 2.4 %unpack_other.1 = (f32[2,432,512]{2,1,0:T(8,128)}, f32[2,9,96,512]{3,2,1,0:T(8,128)}, f32[2,96,96]{2,1,0:T(8,128)}, f32[2,512]{1,0:T(2,128)}, f32[2,96]{1,0:T(2,128)}) custom-call(s32[1]{0:T(128)} %bitcast.2.core_ref, bf16[64,88,128]{2,1,0:T(8,128)(2,1)S(1)} %all_to_all.16.mine_ref, ...), custom_call_target="tpu_custom_call", output_to_operand_aliasing={{0}: (3, {}), {1}: (4, {})} | custom-call | bytes 13579012 | tf_op jit(solution)/shard_map/unpack_other/pallas_call | solution.py:69
  (48 shorter events, 0.5 us)
Async XLA Ops:
  0.6 9.1 %copy-start.15 = (f32[1,192,1,384]{3,2,1,0:T(1,128)S(1)}, f32[1,192,1,384]{3,2,1,0:T(1,128)}, u32[]{:S(2)}) copy-start(f32[1,192,1,384]{3,2,1,0:T(1,128)} %param.10) | copy-start | bytes 884740
  2.9 19.9 %all-to-all-start = ((bf16[16,24,960]{2,1,0:T(8,128)(2,1)}), bf16[16,24,960]{2,1,0:T(8,128)(2,1)S(1)}, u32[]{:S(2)}, u32[]{:S(2)}) async-start(bf16[16,24,960]{2,1,0:T(8,128)(2,1)} %payload.1), calls=%async_computation | async-start | bytes 1572864 | tf_op jit(solution)/shard_map/all_to_all | solution.py:694
  17.6 5.9 %copy-start.4 = (bf16[288,1536]{1,0:T(8,128)(2,1)S(1)}, bf16[288,1536]{1,0:T(8,128)(2,1)}, u32[]{:S(2)}) copy-start(bf16[288,1536]{1,0:T(8,128)(2,1)} %get-tuple-element.76.refs_4_) | copy-start | bytes 2654212
  17.6 5.9 %copy-start.6 = (bf16[512,448]{1,0:T(8,128)(2,1)S(1)}, bf16[512,448]{1,0:T(8,128)(2,1)}, u32[]{:S(2)}) copy-start(bf16[512,448]{1,0:T(8,128)(2,1)} %get-tuple-element.75.refs_3_) | copy-start | bytes 1376260
  17.6 5.9 %copy-start.13 = (f32[96,96]{1,0:T(8,128)S(1)}, f32[96,96]{1,0:T(8,128)}, u32[]{:S(2)}) copy-start(f32[96,96]{1,0:T(8,128)} %get-tuple-element.78.refs_6_) | copy-start | bytes 110596
  17.6 5.9 %copy-start.14 = (f32[96,8]{1,0:T(8,128)S(1)}, f32[96,8]{1,0:T(8,128)}, u32[]{:S(2)}) copy-start(f32[96,8]{1,0:T(8,128)} %get-tuple-element.77.refs_5_) | copy-start | bytes 9220
  28.7 5.4 %collective-permute-start.1 = (bf16[192,384]{1,0:T(8,128)(2,1)S(1)}, bf16[192,384]{1,0:T(8,128)(2,1)S(1)}, u32[]{:S(2)}, u32[]{:S(2)}) collective-permute-start(bf16[192,384]{1,0:T(8,128)(2,1)S(1)} %get-tuple-element.84.refs_1_.mid_ref), channel_id=1, source_target_pairs={{8,0},{16,8},{24,16},{32,24},{40,32},{48,40},{56,48},{64,56},{72,6... | collective-permute-start | bytes 442376 | tf_op jit(solution)/shard_map/ppermute | solution.py:704
  29.7 4.5 %collective-permute-start = (bf16[192,384]{1,0:T(8,128)(2,1)S(1)}, bf16[192,384]{1,0:T(8,128)(2,1)S(1)}, u32[]{:S(2)}, u32[]{:S(2)}) collective-permute-start(bf16[192,384]{1,0:T(8,128)(2,1)S(1)} %get-tuple-element.84.refs_1_.mid_ref), channel_id=1, source_target_pairs={{0,8},{8,16},{16,24},{24,32},{32,40},{40,48},{48,56},{56,64},{64,7... | collective-permute-start | bytes 442376 | tf_op jit(solution)/shard_map/ppermute | solution.py:703
  30.5 9.6 %collective-permute-start.3 = (bf16[384,384]{1,0:T(8,128)(2,1)S(1)}, bf16[384,384]{1,0:T(8,128)(2,1)S(1)}, u32[]{:S(2)}, u32[]{:S(2)}) collective-permute-start(bf16[384,384]{1,0:T(8,128)(2,1)S(1)} %get-tuple-element.80.grad_ref.mid_ref), channel_id=1, source_target_pairs={{8,0},{16,8},{24,16},{32,24},{40,32},{48,40},{56,48},{64,56},{72,6... | collective-permute-start | bytes 884744 | tf_op jit(solution)/shard_map/ppermute | solution.py:706
  30.5 9.6 %collective-permute-start.2 = (bf16[384,384]{1,0:T(8,128)(2,1)S(1)}, bf16[384,384]{1,0:T(8,128)(2,1)S(1)}, u32[]{:S(2)}, u32[]{:S(2)}) collective-permute-start(bf16[384,384]{1,0:T(8,128)(2,1)S(1)} %get-tuple-element.80.grad_ref.mid_ref), channel_id=1, source_target_pairs={{0,8},{8,16},{16,24},{24,32},{32,40},{40,48},{48,56},{56,64},{64,7... | collective-permute-start | bytes 884744 | tf_op jit(solution)/shard_map/ppermute | solution.py:705
  32.3 1.8 %copy-start.3 = (bf16[288,1536]{1,0:T(8,128)(2,1)S(1)}, bf16[288,1536]{1,0:T(8,128)(2,1)}, u32[]{:S(2)}) copy-start(bf16[288,1536]{1,0:T(8,128)(2,1)} %get-tuple-element.86.refs_4_) | copy-start | bytes 2654212
  32.3 1.8 %copy-start.5 = (bf16[512,448]{1,0:T(8,128)(2,1)S(1)}, bf16[512,448]{1,0:T(8,128)(2,1)}, u32[]{:S(2)}) copy-start(bf16[512,448]{1,0:T(8,128)(2,1)} %get-tuple-element.85.refs_3_) | copy-start | bytes 1376260
  32.3 1.8 %copy-start.11 = (f32[96,96]{1,0:T(8,128)S(1)}, f32[96,96]{1,0:T(8,128)}, u32[]{:S(2)}) copy-start(f32[96,96]{1,0:T(8,128)} %get-tuple-element.88.refs_6_) | copy-start | bytes 110596
  32.4 1.8 %copy-start.12 = (f32[96,8]{1,0:T(8,128)S(1)}, f32[96,8]{1,0:T(8,128)}, u32[]{:S(2)}) copy-start(f32[96,8]{1,0:T(8,128)} %get-tuple-element.87.refs_5_) | copy-start | bytes 9220
  34.2 6.0 %copy-start.2 = (bf16[512,864]{1,0:T(8,128)(2,1)S(1)}, bf16[512,864]{1,0:T(8,128)(2,1)}, u32[]{:S(2)}) copy-start(bf16[512,864]{1,0:T(8,128)(2,1)} %get-tuple-element.92.w2t_ref) | copy-start | bytes 2654212
  34.2 5.9 %copy-start.8 = (bf16[144,1536]{1,0:T(8,128)(2,1)S(1)}, bf16[144,1536]{1,0:T(8,128)(2,1)}, u32[]{:S(2)}) copy-start(bf16[144,1536]{1,0:T(8,128)(2,1)} %get-tuple-element.94.w1k_ref) | copy-start | bytes 1327108
  40.1 5.0 %copy-start = (f32[2,96,96]{2,1,0:T(8,128)S(1)}, f32[2,96,96]{2,1,0:T(8,128)}, u32[]{:S(2)}) copy-start(f32[2,96,96]{2,1,0:T(8,128)} %refs_5_.3) | copy-start | bytes 221188
  40.2 5.0 %copy-start.10 = (f32[96,96]{1,0:T(8,128)S(1)}, f32[96,96]{1,0:T(8,128)}, u32[]{:S(2)}) copy-start(f32[96,96]{1,0:T(8,128)} %get-tuple-element.98.refs_3_) | copy-start | bytes 110596
  46.5 9.8 %collective-permute-start.5 = (bf16[384,384]{1,0:T(8,128)(2,1)S(1)}, bf16[384,384]{1,0:T(8,128)(2,1)S(1)}, u32[]{:S(2)}, u32[]{:S(2)}) collective-permute-start(bf16[384,384]{1,0:T(8,128)(2,1)S(1)} %get-tuple-element.101.grad_ref.mid_ref), channel_id=1, source_target_pairs={{8,0},{16,8},{24,16},{32,24},{40,32},{48,40},{56,48},{64,56},{72,6... | collective-permute-start | bytes 884744 | tf_op jit(solution)/shard_map/ppermute | solution.py:718
  49.6 6.7 %collective-permute-start.4 = (bf16[384,384]{1,0:T(8,128)(2,1)S(1)}, bf16[384,384]{1,0:T(8,128)(2,1)S(1)}, u32[]{:S(2)}, u32[]{:S(2)}) collective-permute-start(bf16[384,384]{1,0:T(8,128)(2,1)S(1)} %get-tuple-element.101.grad_ref.mid_ref), channel_id=1, source_target_pairs={{0,8},{8,16},{16,24},{24,32},{32,40},{40,48},{48,56},{56,64},{64,7... | collective-permute-start | bytes 884744 | tf_op jit(solution)/shard_map/ppermute | solution.py:717
  49.6 17.4 %collective-permute-start.9 = (f32[3,144,512]{2,1,0:T(8,128)S(1)}, f32[3,144,512]{2,1,0:T(8,128)S(1)}, u32[]{:S(2)}, u32[]{:S(2)}) collective-permute-start(f32[3,144,512]{2,1,0:T(8,128)S(1)} %get-tuple-element.126), channel_id=1, source_target_pairs={{0,8},{8,0},{1,9},{9,1},{2,10},{10,2},{3,11},{11,3},{4,12},{12,4},... | collective-permute-start | bytes 2654216 | tf_op jit(solution)/shard_map/ppermute | solution.py:712
  52.5 3.8 %copy-start.1 = (bf16[512,864]{1,0:T(8,128)(2,1)S(1)}, bf16[512,864]{1,0:T(8,128)(2,1)}, u32[]{:S(2)}) copy-start(bf16[512,864]{1,0:T(8,128)(2,1)} %get-tuple-element.110.w2t_ref) | copy-start | bytes 2654212
  52.5 3.8 %copy-start.7 = (bf16[144,1536]{1,0:T(8,128)(2,1)S(1)}, bf16[144,1536]{1,0:T(8,128)(2,1)}, u32[]{:S(2)}) copy-start(bf16[144,1536]{1,0:T(8,128)(2,1)} %get-tuple-element.112.w1k_ref) | copy-start | bytes 1327108
  54.3 12.7 %collective-permute-start.8 = (f32[224,512]{1,0:T(8,128)S(1)}, f32[224,512]{1,0:T(8,128)S(1)}, u32[]{:S(2)}, u32[]{:S(2)}) collective-permute-start(f32[224,512]{1,0:T(8,128)S(1)} %get-tuple-element.125), channel_id=1, source_target_pairs={{0,8},{8,0},{1,9},{9,1},{2,10},{10,2},{3,11},{11,3},{4,12},{12,4},... | collective-permute-start | bytes 1376264 | tf_op jit(solution)/shard_map/ppermute | solution.py:720
  55.8 11.4 %collective-permute-start.7 = (f32[3,144,512]{2,1,0:T(8,128)S(1)}, f32[3,144,512]{2,1,0:T(8,128)S(1)}, u32[]{:S(2)}, u32[]{:S(2)}) collective-permute-start(f32[3,144,512]{2,1,0:T(8,128)S(1)} %get-tuple-element.118), channel_id=1, source_target_pairs={{0,8},{8,0},{1,9},{9,1},{2,10},{10,2},{3,11},{11,3},{4,12},{12,4},... | collective-permute-start | bytes 2654216 | tf_op jit(solution)/shard_map/ppermute | solution.py:724
  61.2 4.6 %copy-start.9 = (f32[96,96]{1,0:T(8,128)S(1)}, f32[96,96]{1,0:T(8,128)}, u32[]{:S(2)}) copy-start(f32[96,96]{1,0:T(8,128)} %get-tuple-element.122.refs_3_) | copy-start | bytes 110596
  62.7 4.5 %collective-permute-start.6 = (f32[224,512]{1,0:T(8,128)S(1)}, f32[224,512]{1,0:T(8,128)S(1)}, u32[]{:S(2)}, u32[]{:S(2)}) collective-permute-start(f32[224,512]{1,0:T(8,128)S(1)} %get-tuple-element.117), channel_id=1, source_target_pairs={{0,8},{8,0},{1,9},{9,1},{2,10},{10,2},{3,11},{11,3},{4,12},{12,4},... | collective-permute-start | bytes 1376264 | tf_op jit(solution)/shard_map/ppermute | solution.py:726
  122.3 7.1 %collective-permute-start.10 = (bf16[64,88,128]{2,1,0:T(8,128)(2,1)S(1)}, bf16[64,88,128]{2,1,0:T(8,128)(2,1)S(1)}, u32[]{:S(2)}, u32[]{:S(2)}) collective-permute-start(bf16[64,88,128]{2,1,0:T(8,128)(2,1)S(1)} %all_to_all.16.mine_ref), channel_id=1, source_target_pairs={{0,8},{8,0},{1,9},{9,1},{2,10},{10,2},{3,11},{11,3},{4,12},{12,4},... | collective-permute-start | bytes 4325384 | tf_op jit(solution)/shard_map/ppermute | solution.py:739
